TPU v7x, 32 devices: a whole 2x2x4 slice. The times are simulated.
32 devices in a mesh: dp: 8 (over z, x), tensor: 4 (over y, core).
Axes of the slice: x: 2, y: 2, z: 4, core: 2. Of those that a mesh axis runs over, the one named last changes fastest.
Arguments:
- tokens: bfloat16 [16384, 1536], P(('dp', 'tensor')), may hold values from -6 to 6
- cotangent: bfloat16 [16384, 1536], P(('dp', 'tensor')), may hold values from -6 to 6
- lengths: int32 [16], P('dp'), may hold values from 1 to 1024, 12288 in all
- qkv_weight: float32 [1536, 3072], P('dp', 'tensor')
- out_weight: float32 [1536, 1536], P('tensor', 'dp'), may hold values from -6 to 6
- gate_up_weight: float32 [2, 1536, 4096], P(None, 'dp', 'tensor'), may hold values from -1 to 1
- down_weight: float32 [4096, 1536], P('tensor', 'dp')
- norm_gains: float32 [2, 1536], P(None, ('dp', 'tensor')), may hold values from 0 to 4
- qkv_first: float32 [1536, 3072], P('dp', 'tensor')
- out_first: float32 [1536, 1536], P('tensor', 'dp')
- gate_up_first: float32 [2, 1536, 4096], P(None, 'dp', 'tensor')
- down_first: float32 [4096, 1536], P('tensor', 'dp')
- gains_first: float32 [2, 1536], P(None, ('dp', 'tensor'))
- qkv_second: float32 [1536, 3072], P('dp', 'tensor'), as said below
- out_second: float32 [1536, 1536], P('tensor', 'dp'), as said below
- gate_up_second: float32 [2, 1536, 4096], P(None, 'dp', 'tensor'), as said below
- down_second: float32 [4096, 1536], P('tensor', 'dp'), as said below
- gains_second: float32 [2, 1536], P(None, ('dp', 'tensor')), as said below
Outputs:
- layer_out: bfloat16 [16384, 1536], P(('dp', 'tensor'))
- grad_tokens: float32 [16384, 1536], P(('dp', 'tensor'))
- new_qkv: float32 [1536, 3072], P('dp', 'tensor')
- new_out: float32 [1536, 1536], P('tensor', 'dp')
- new_gate_up: float32 [2, 1536, 4096], P(None, 'dp', 'tensor')
- new_down: float32 [4096, 1536], P('tensor', 'dp')
- new_gains: float32 [2, 1536], P(None, ('dp', 'tensor'))
- next_qkv_first: float32 [1536, 3072], P('dp', 'tensor')
- next_out_first: float32 [1536, 1536], P('tensor', 'dp')
- next_gate_up_first: float32 [2, 1536, 4096], P(None, 'dp', 'tensor')
- next_down_first: float32 [4096, 1536], P('tensor', 'dp')
- next_gains_first: float32 [2, 1536], P(None, ('dp', 'tensor'))
- next_qkv_second: float32 [1536, 3072], P('dp', 'tensor')
- next_out_second: float32 [1536, 1536], P('tensor', 'dp')
- next_gate_up_second: float32 [2, 1536, 4096], P(None, 'dp', 'tensor')
- next_down_second: float32 [4096, 1536], P('tensor', 'dp')
- next_gains_second: float32 [2, 1536], P(None, ('dp', 'tensor'))
- weight_norms: float32 [7], replicated
- update_norms: float32 [5], replicated
- gain_update_norms: float32 [2], replicated
Inputs may be any that keep to these rules, and one draw needn't show every extreme that they name: Sequence lengths sum to 12288. `qkv_second`: Positive. `out_second`: Positive. `gate_up_second`: Positive. `down_second`: Positive. `gains_second`: Positive.
All inputs are finite; a program needn't handle non-finite values. No bound on the sum of `lengths` on one device may be relied on, other than what follows from the above.
Results may differ from a plain program's by a relative error of at most 0.023.
Values may be sent and summed in bfloat16 or wider, within the bound.
A program may use at most 256 MiB of HBM per device.

v0:
```python
import jax
import jax.numpy as jnp
from jax import lax
from jax.sharding import PartitionSpec as P

HEAD = 96
SEQ_LEN = 1024
SEQS_DEV = 2
STEP = 10
GROUP = 2


NORM_EPSILON = 1e-05
ROPE_THETA = 100000.0
BETA_ONE = 0.9
BETA_TWO = 0.999
ADAM_EPSILON = 1e-06
WEIGHT_DECAY = 0.01
LEARN_RATE = 0.3
NEGATIVE = -1e30
BLOCK_ROWS = 512


def rms_norm(values, gain_row):
    return (
        values
        * lax.rsqrt(jnp.mean(values * values, axis=-1, keepdims=True) + NORM_EPSILON)
        * gain_row
    )


def rotary_tables(length):
    half_width = HEAD // 2
    frequency = ROPE_THETA ** (-(jnp.arange(half_width, dtype=jnp.float32) * (2.0 / HEAD)))
    angles = jnp.arange(length, dtype=jnp.float32)[:, None] * frequency[None, :]
    return (jnp.cos(angles), jnp.sin(angles))


def rotate(values, cosine, sine_part):
    half_width = values.shape[-1] // 2
    first_half = values[..., :half_width]
    second_half = values[..., half_width:]
    return jnp.concatenate(
        [
            first_half * cosine - second_half * sine_part,
            second_half * cosine + first_half * sine_part,
        ],
        axis=-1,
    )


def contract_rows(left, right):
    return lax.dot_general(
        left, right, (((0,), (0,)), ((), ())), preferred_element_type=jnp.float32
    )


def contract_cols(left, right):
    return lax.dot_general(
        left, right, (((1,), (1,)), ((), ())), preferred_element_type=jnp.float32
    )


def block_scores(query_block, key_rows, row_start, length):
    row_count = query_block.shape[0]
    key_count = key_rows.shape[0]
    scores = jnp.einsum(
        "rkgd,lkd->kgrl", query_block, key_rows, preferred_element_type=jnp.float32
    ) * HEAD ** (-0.5)
    row_ids = row_start + lax.broadcasted_iota(jnp.int32, (row_count, key_count), 0)
    col_ids = lax.broadcasted_iota(jnp.int32, (row_count, key_count), 1)
    allowed = (col_ids <= row_ids) & (col_ids < length)
    return jnp.where(allowed, scores, NEGATIVE)


def attend_sequence(member):
    queries, key_rows, value_rows, length = member
    row_count = min(BLOCK_ROWS, queries.shape[0])
    results = []
    log_parts = []
    for row_start in range(0, queries.shape[0], row_count):
        scores = block_scores(
            queries[row_start : row_start + row_count], key_rows, row_start, length
        )
        highest = jnp.max(scores, axis=-1, keepdims=True)
        exponent = jnp.exp(scores - highest)
        totals = jnp.sum(exponent, axis=-1, keepdims=True)
        weights = (exponent / totals).astype(jnp.bfloat16)
        results.append(
            jnp.einsum("kgrl,lkd->rkgd", weights, value_rows, preferred_element_type=jnp.float32)
        )
        log_parts.append(highest + jnp.log(totals))
    return (jnp.concatenate(results, axis=0), jnp.concatenate(log_parts, axis=2))


def attend_back(member):
    queries, key_rows, value_rows, out_grad, log_totals, length = member
    row_count = min(BLOCK_ROWS, queries.shape[0])
    score_scale = HEAD ** (-0.5)
    query_parts = []
    key_grad = jnp.zeros(key_rows.shape, jnp.float32)
    value_grad = jnp.zeros(value_rows.shape, jnp.float32)
    for row_start in range(0, queries.shape[0], row_count):
        query_block = queries[row_start : row_start + row_count]
        grad_block = out_grad[row_start : row_start + row_count]
        scores = block_scores(query_block, key_rows, row_start, length)
        weights = jnp.exp(scores - log_totals[:, :, row_start : row_start + row_count, :])
        weight_grad = jnp.einsum(
            "rkgd,lkd->kgrl", grad_block, value_rows, preferred_element_type=jnp.float32
        )
        inner_sum = jnp.sum(weights * weight_grad, axis=-1, keepdims=True)
        score_grad = (weights * (weight_grad - inner_sum)).astype(jnp.bfloat16)
        query_parts.append(
            jnp.einsum("kgrl,lkd->rkgd", score_grad, key_rows, preferred_element_type=jnp.float32)
            * score_scale
        )
        key_grad = (
            key_grad
            + jnp.einsum(
                "kgrl,rkgd->lkd", score_grad, query_block, preferred_element_type=jnp.float32
            )
            * score_scale
        )
        value_grad = value_grad + jnp.einsum(
            "kgrl,rkgd->lkd",
            weights.astype(jnp.bfloat16),
            grad_block,
            preferred_element_type=jnp.float32,
        )
    return (jnp.concatenate(query_parts, axis=0), key_grad, value_grad)


def shards(
    tokens,
    cotangent,
    lengths,
    qkv_weight,
    out_weight,
    gate_up_weight,
    down_weight,
    norm_gains,
    qkv_first,
    out_first,
    gate_up_first,
    down_first,
    gains_first,
    qkv_second,
    out_second,
    gate_up_second,
    down_second,
    gains_second,
):
    shard_rows = tokens.shape[0]
    group_rows = SEQS_DEV * SEQ_LEN
    qkv_work, out_work, gate_up_work, down_work = (
        lax.all_gather(qkv_weight.astype(jnp.bfloat16), "dp", axis=0, tiled=True),
        lax.all_gather(out_weight.astype(jnp.bfloat16), "dp", axis=1, tiled=True),
        lax.all_gather(gate_up_weight.astype(jnp.bfloat16), "dp", axis=1, tiled=True),
        lax.all_gather(down_weight.astype(jnp.bfloat16), "dp", axis=1, tiled=True),
    )
    gain_work = lax.all_gather(
        norm_gains.astype(jnp.bfloat16), ("dp", "tensor"), axis=1, tiled=True
    ).astype(jnp.float32)
    attention_gain = gain_work[0]
    feedforward_gain = gain_work[1]
    inputs = tokens.astype(jnp.float32)
    normed = lax.all_gather(
        rms_norm(inputs, attention_gain).astype(jnp.bfloat16), "tensor", axis=0, tiled=True
    )
    kv_local = qkv_work.shape[1] // ((GROUP + 2) * HEAD)
    projected = jnp.dot(normed, qkv_work, preferred_element_type=jnp.float32).reshape(
        SEQS_DEV, SEQ_LEN, kv_local, GROUP + 2, HEAD
    )
    cosine, sine_part = rotary_tables(SEQ_LEN)
    cosine_five = cosine[None, :, None, None, :]
    sine_five = sine_part[None, :, None, None, :]
    cosine_four = cosine[None, :, None, :]
    sine_four = sine_part[None, :, None, :]
    queries = rotate(projected[:, :, :, :GROUP], cosine_five, sine_five).astype(jnp.bfloat16)
    key_rows = rotate(projected[:, :, :, GROUP], cosine_four, sine_four).astype(jnp.bfloat16)
    value_rows = projected[:, :, :, GROUP + 1].astype(jnp.bfloat16)
    attended, log_totals = lax.map(attend_sequence, (queries, key_rows, value_rows, lengths))
    attention_rows = attended.astype(jnp.bfloat16).reshape(group_rows, kv_local * GROUP * HEAD)
    residual = inputs + lax.psum_scatter(
        jnp.dot(
            lax.slice_in_dim(attention_rows, 0, shard_rows * lax.axis_size("tensor"), axis=0),
            out_work,
            preferred_element_type=jnp.float32,
        ),
        "tensor",
        scatter_dimension=0,
        tiled=True,
    )
    normed_two = lax.all_gather(
        rms_norm(residual, feedforward_gain).astype(jnp.bfloat16), "tensor", axis=0, tiled=True
    )
    gate_proj = jnp.dot(normed_two, gate_up_work[0], preferred_element_type=jnp.float32)
    up_proj = jnp.dot(normed_two, gate_up_work[1], preferred_element_type=jnp.float32)
    hidden = (jax.nn.silu(gate_proj) * up_proj).astype(jnp.bfloat16)
    layer_out = (
        residual
        + lax.psum_scatter(
            jnp.dot(
                lax.slice_in_dim(hidden, 0, lax.axis_size("tensor") * shard_rows, axis=0),
                down_work,
                preferred_element_type=jnp.float32,
            ).astype(jnp.bfloat16),
            "tensor",
            scatter_dimension=0,
            tiled=True,
        ).astype(jnp.float32)
    ).astype(jnp.bfloat16)
    upstream = lax.all_gather(cotangent, "tensor", axis=0, tiled=True)
    down_grad = contract_rows(hidden, upstream)
    hidden_grad = contract_cols(upstream, down_work)
    sigmoid_gate = jax.nn.sigmoid(gate_proj)
    gate_grad = (
        hidden_grad * up_proj * sigmoid_gate * (1.0 + gate_proj * (1.0 - sigmoid_gate))
    ).astype(jnp.bfloat16)
    up_grad = (hidden_grad * gate_proj * sigmoid_gate).astype(jnp.bfloat16)
    gate_up_grad = jnp.stack(
        [contract_rows(normed_two, gate_grad), contract_rows(normed_two, up_grad)]
    )
    gate_slice = lax.slice_in_dim(gate_grad, 0, shard_rows * lax.axis_size("tensor"), axis=0)
    up_slice = lax.slice_in_dim(up_grad, 0, shard_rows * lax.axis_size("tensor"), axis=0)
    normed_two_grad = lax.psum_scatter(
        contract_cols(gate_slice, gate_up_work[0]) + contract_cols(up_slice, gate_up_work[1]),
        "tensor",
        scatter_dimension=0,
        tiled=True,
    )
    norm_out, norm_pull = jax.vjp(rms_norm, residual, feedforward_gain)
    residual_part, ffn_gain_grad = norm_pull(normed_two_grad)
    residual_grad = cotangent.astype(jnp.float32) + residual_part
    attention_grad = lax.all_gather(
        residual_grad.astype(jnp.bfloat16), "tensor", axis=0, tiled=True
    )
    out_weight_grad = contract_rows(attention_rows, attention_grad)
    attended_grad = (
        contract_cols(attention_grad, out_work)
        .astype(jnp.bfloat16)
        .reshape(SEQS_DEV, SEQ_LEN, kv_local, GROUP, HEAD)
    )
    query_grad, key_grad, value_grad = lax.map(
        attend_back, (queries, key_rows, value_rows, attended_grad, log_totals, lengths)
    )
    query_raw = rotate(query_grad, cosine_five, -sine_five)
    key_raw = rotate(key_grad, cosine_four, -sine_four)
    projected_grad = (
        jnp.concatenate([query_raw, key_raw[:, :, :, None], value_grad[:, :, :, None]], axis=3)
        .astype(jnp.bfloat16)
        .reshape(group_rows, kv_local * (GROUP + 2) * HEAD)
    )
    qkv_weight_grad = contract_rows(normed, projected_grad)
    normed_grad = lax.psum_scatter(
        contract_cols(projected_grad, qkv_work).astype(jnp.bfloat16),
        "tensor",
        scatter_dimension=0,
        tiled=True,
    ).astype(jnp.float32)
    first_out, first_pull = jax.vjp(rms_norm, inputs, attention_gain)
    input_part, attention_gain_grad = first_pull(normed_grad)
    grad_tokens = residual_grad + input_part
    gain_sums = lax.psum_scatter(
        jnp.stack([attention_gain_grad, ffn_gain_grad]),
        ("dp", "tensor"),
        scatter_dimension=1,
        tiled=True,
    )
    qkv_sum, out_sum, gate_up_sum, down_sum = (
        lax.psum_scatter(
            qkv_weight_grad.astype(jnp.bfloat16), "dp", scatter_dimension=0, tiled=True
        ).astype(jnp.float32),
        lax.psum_scatter(
            out_weight_grad.astype(jnp.bfloat16), "dp", scatter_dimension=1, tiled=True
        ).astype(jnp.float32),
        lax.psum_scatter(
            gate_up_grad.astype(jnp.bfloat16), "dp", scatter_dimension=1, tiled=True
        ).astype(jnp.float32),
        lax.psum_scatter(
            down_grad.astype(jnp.bfloat16), "dp", scatter_dimension=1, tiled=True
        ).astype(jnp.float32),
    )
    masters = (
        qkv_weight,
        out_weight,
        gate_up_weight[0],
        gate_up_weight[1],
        down_weight,
        norm_gains[0],
        norm_gains[1],
    )
    firsts = (
        qkv_first,
        out_first,
        gate_up_first[0],
        gate_up_first[1],
        down_first,
        gains_first[0],
        gains_first[1],
    )
    seconds = (
        qkv_second,
        out_second,
        gate_up_second[0],
        gate_up_second[1],
        down_second,
        gains_second[0],
        gains_second[1],
    )
    gradients = (
        qkv_sum,
        out_sum,
        gate_up_sum[0],
        gate_up_sum[1],
        down_sum,
        gain_sums[0],
        gain_sums[1],
    )
    correct_one = 1.0 - BETA_ONE**STEP
    correct_two = 1.0 - BETA_TWO**STEP
    new_firsts = []
    new_seconds = []
    updates = []
    for master, moment, square, gradient in zip(masters, firsts, seconds, gradients):
        moment = BETA_ONE * moment + (1.0 - BETA_ONE) * gradient
        square = BETA_TWO * square + (1.0 - BETA_TWO) * gradient * gradient
        new_firsts.append(moment)
        new_seconds.append(square)
        updates.append(
            moment / correct_one / (jnp.sqrt(square / correct_two) + ADAM_EPSILON)
            + WEIGHT_DECAY * master
        )
    weight_local = jnp.stack([jnp.sum(master * master) for master in masters])
    update_local = jnp.stack([jnp.sum(update * update) for update in updates])
    weight_squares, update_squares = lax.psum((weight_local, update_local), ("dp", "tensor"))
    weight_norms = jnp.sqrt(weight_squares)
    all_update_norms = jnp.sqrt(update_squares)
    new_weights = [
        masters[number]
        - LEARN_RATE * (weight_norms[number] / all_update_norms[number]) * updates[number]
        for number in range(7)
    ]
    return (
        layer_out,
        grad_tokens,
        new_weights[0],
        new_weights[1],
        jnp.stack([new_weights[2], new_weights[3]]),
        new_weights[4],
        jnp.stack([new_weights[5], new_weights[6]]),
        new_firsts[0],
        new_firsts[1],
        jnp.stack([new_firsts[2], new_firsts[3]]),
        new_firsts[4],
        jnp.stack([new_firsts[5], new_firsts[6]]),
        new_seconds[0],
        new_seconds[1],
        jnp.stack([new_seconds[2], new_seconds[3]]),
        new_seconds[4],
        jnp.stack([new_seconds[5], new_seconds[6]]),
        weight_norms,
        all_update_norms[:5],
        all_update_norms[5:],
    )


def solution(mesh):
    in_specs = (
        P(("dp", "tensor"), None),
        P(("dp", "tensor"), None),
        P("dp"),
        P("dp", "tensor"),
        P("tensor", "dp"),
        P(None, "dp", "tensor"),
        P("tensor", "dp"),
        P(None, ("dp", "tensor")),
        P("dp", "tensor"),
        P("tensor", "dp"),
        P(None, "dp", "tensor"),
        P("tensor", "dp"),
        P(None, ("dp", "tensor")),
        P("dp", "tensor"),
        P("tensor", "dp"),
        P(None, "dp", "tensor"),
        P("tensor", "dp"),
        P(None, ("dp", "tensor")),
    )
    out_specs = (
        P(("dp", "tensor"), None),
        P(("dp", "tensor"), None),
        P("dp", "tensor"),
        P("tensor", "dp"),
        P(None, "dp", "tensor"),
        P("tensor", "dp"),
        P(None, ("dp", "tensor")),
        P("dp", "tensor"),
        P("tensor", "dp"),
        P(None, "dp", "tensor"),
        P("tensor", "dp"),
        P(None, ("dp", "tensor")),
        P("dp", "tensor"),
        P("tensor", "dp"),
        P(None, "dp", "tensor"),
        P("tensor", "dp"),
        P(None, ("dp", "tensor")),
        P(),
        P(),
        P(),
    )
    return jax.shard_map(shards, mesh=mesh, in_specs=in_specs, out_specs=out_specs, check_vma=False)
```

profile of v0, /device:TPU:0, one launch (start us, length us, event | category | flops | bytes accessed | tf_op | source)
XLA Modules:
  0.0 1642.8 jit_solution(7120193356054065357)
XLA Ops:
  9.9 43.1 %all-gather = bf16[32,48,2]{1,2,0:T(2,128)(2,1)S(1)} all-gather(bf16[1,48,2]{1,2,0:T(2,128)(2,1)S(1)} %convert_bitcast_fusion.1), channel_id=1, replica_groups=mesh['dp'=8,'tensor'=4] {'dp','tensor'}, dimensions={0}, use_global_device_ids=true | all-gather | bytes 6336 | tf_op jit(solution)/shard_map/all_gather | solution.py:161
  65.5 47.1 %all-gather.10.cloned.1.call-done = bf16[2048,1536]{1,0:T(8,128)(2,1)} async-done(((bf16[512,1536]{1,0:T(8,128)(2,1)}), bf16[2048,1536]{1,0:T(8,128)(2,1)}) %all-gather.10.cloned.1.call-update) | async-done | bytes 6291472 | tf_op jit(solution)/shard_map/all_gather | solution.py:167
  143.4 35.4 %while.26 = (s32[]{:T(128)}, bf16[2,1024,2,2,96]{1,4,3,2,0:T(8,128)(2,1)}, f32[2,2,2,1024,1]{3,2,1,4,0:T(2,128)S(1)}, bf16[2,1024,2,96]{1,3,2,0:T(8,128)(2,1)S(1...) while((s32[]{:T(128)}, ...), condition=%wide.region_6.7_spmd, body=%wide.region_1.6_spmd.sunk | while | flops 1664615936 | bytes 72000216 | solution.py:182
  196.1 96.5 %reduce-scatter.12.cloned.1.call-done = f32[512,1536]{1,0:T(8,128)} async-done(((f32[2048,1536]{1,0:T(8,128)}), f32[512,1536]{1,0:T(8,128)}) %reduce-scatter.12.cloned.1.call-update) | async-done | bytes 3145744 | tf_op jit(solution)/shard_map/reduce_scatter | solution.py:184
  299.8 94.5 %all-gather.18.cloned.1.call-done = bf16[2,1536,1024]{2,1,0:T(8,128)(2,1)} async-done(((bf16[2,192,1024]{2,1,0:T(8,128)(2,1)}), bf16[2,1536,1024]{2,1,0:T(8,128)(2,1)}) %all-gather.18.cloned.1.call-update) | async-done | bytes 6291472 | tf_op jit(solution)/shard_map/all_gather | solution.py:158
  394.3 46.6 %all-gather.16.cloned.1.call-done = bf16[2048,1536]{1,0:T(8,128)(2,1)} async-done(((bf16[512,1536]{1,0:T(8,128)(2,1)}), bf16[2048,1536]{1,0:T(8,128)(2,1)}) %all-gather.16.cloned.1.call-update) | async-done | bytes 6291472 | tf_op jit(solution)/shard_map/all_gather | solution.py:194
  440.9 12.7 fusion.109
  463.1 41.0 %all-gather.20.cloned.1.call-done = bf16[1024,1536]{0,1:T(8,128)(2,1)} async-done(((bf16[1024,192]{0,1:T(8,128)(2,1)}), bf16[1024,1536]{0,1:T(8,128)(2,1)}) %all-gather.20.cloned.1.call-update) | async-done | bytes 3145744 | tf_op jit(solution)/shard_map/all_gather | solution.py:159
  504.1 46.6 %all-gather.22.cloned.1.call-done = bf16[2048,1536]{1,0:T(8,128)(2,1)} async-done(((bf16[512,1536]{1,0:T(8,128)(2,1)}), bf16[2048,1536]{1,0:T(8,128)(2,1)}) %all-gather.22.cloned.1.call-update) | async-done | bytes 6291472 | tf_op jit(solution)/shard_map/all_gather | solution.py:213
  550.7 18.6 %multiply_convert_fusion = (bf16[2048,1024]{1,0:T(8,128)(2,1)}, bf16[2048,1024]{1,0:T(8,128)(2,1)S(1)}, bf16[2048,1024]{1,0:T(8,128)(2,1)}) fusion(f32[2048,1024]{1,0:T(8,128)} %fusion.108, f32[2048,1024]{1,0:T(8,128)} %fusion.109, bf16[2048,1536]{1,0:T(8,128)(2,1)} %all-gather.22.cloned.1.call-done, bf16[1024,1536]{0,1:T(8,128)(2,1)} %all-gather.20.cloned.1.call-done), kind=kOutput, calls=%fused_computation.126 | convolution fusion | flops 6476005376 | bytes 38797312 | tf_op jit(solution)/shard_map/dot_general | solution.py:59
  579.6 12.7 convolution_add_fusion
  592.4 99.2 %reduce-scatter.16.cloned.1.call-done = f32[512,1536]{1,0:T(8,128)} async-done(((f32[2048,1536]{1,0:T(8,128)}), f32[512,1536]{1,0:T(8,128)}) %reduce-scatter.16.cloned.1.call-update) | async-done | bytes 3145744 | tf_op jit(solution)/shard_map/reduce_scatter | solution.py:226
  698.4 46.5 %all-gather.24.cloned.1.call-done = bf16[2048,1536]{1,0:T(8,128)(2,1)} async-done(((bf16[512,1536]{1,0:T(8,128)(2,1)}), bf16[2048,1536]{1,0:T(8,128)(2,1)}) %all-gather.24.cloned.1.call-update) | async-done | bytes 6291472 | tf_op jit(solution)/shard_map/all_gather | solution.py:235
  759.6 225.6 %while.27 = (s32[]{:T(128)}, f32[2,1024,2,2,96]{1,0,4,3,2:T(2,128)}, f32[2,1024,2,96]{1,0,3,2:T(2,128)}, bf16[2,1024,2,96]{1,0,3,2:T(2,128)(2,1)}, bf16[2,1024,2...) while((s32[]{:T(128)}, ...), condition=%wide.region_15.16_spmd, body=%wide.region_12.15_spmd.sunk | while | flops 4093113856 | bytes 249064752 | solution.py:244
  773.5 13.5 dynamic_update_slice.29
  803.8 15.1 fusion.260
  830.2 14.4 dynamic_update_slice.28
  844.6 27.7 %dynamic_update_slice.27 = f32[2,1024,2,2,96]{1,0,4,3,2:T(2,128)} dynamic-update-slice(f32[2,1024,2,2,96]{1,0,4,3,2:T(2,128)} %get-tuple-element.501, f32[1,1024,2,2,96]{1,0,4,3,2:T(1,128)S(1)} %copy.184, s32[]{:T(128)S(6)} %copy.205, s32[]{:T(128)} %constant.54.clone.1..sunk.1, s32[]{:T(128)} %constant.54.clone.1..sunk.1, s32[]{:T(128)} %constant.54.clone.1..sunk.1, s32[]{:T(128)} %constant.54.clone.1..sunk.1) | dynamic-update-slice | bytes 3145732 | tf_op jit(solution)/shard_map/while/body/jit(dynamic_update_index_in_dim)/dynamic_update_slice | solution.py:182
  886.0 13.5 dynamic_update_slice.29
  916.3 15.1 fusion.260
  942.7 14.4 dynamic_update_slice.28
  957.1 27.7 %dynamic_update_slice.27 = f32[2,1024,2,2,96]{1,0,4,3,2:T(2,128)} dynamic-update-slice(f32[2,1024,2,2,96]{1,0,4,3,2:T(2,128)} %get-tuple-element.501, f32[1,1024,2,2,96]{1,0,4,3,2:T(1,128)S(1)} %copy.184, s32[]{:T(128)S(6)} %copy.205, s32[]{:T(128)} %constant.54.clone.1..sunk.1, s32[]{:T(128)} %constant.54.clone.1..sunk.1, s32[]{:T(128)} %constant.54.clone.1..sunk.1, s32[]{:T(128)} %constant.54.clone.1..sunk.1) | dynamic-update-slice | bytes 3145732 | tf_op jit(solution)/shard_map/while/body/jit(dynamic_update_index_in_dim)/dynamic_update_slice | solution.py:182
  1009.1 11.3 convolution_convert_fusion.2
  1020.5 10.8 fusion.100
  1071.6 11.7 convolution_convert_fusion.1
  1085.5 60.1 %reduce-scatter.26.cloned.1.call-done = bf16[1024,192]{0,1:T(8,128)(2,1)} async-done(((bf16[1024,1536]{0,1:T(8,128)(2,1)}), bf16[1024,192]{0,1:T(8,128)(2,1)}) %reduce-scatter.26.cloned.1.call-update) | async-done | bytes 393232 | tf_op jit(solution)/shard_map/reduce_scatter | solution.py:280
  1149.3 117.5 %reduce-scatter.24.cloned.1.call-done = bf16[2,192,1024]{2,1,0:T(8,128)(2,1)} async-done(((bf16[2,1536,1024]{2,1,0:T(8,128)(2,1)}), bf16[2,192,1024]{2,1,0:T(8,128)(2,1)}) %reduce-scatter.24.cloned.1.call-update) | async-done | bytes 786448 | tf_op jit(solution)/shard_map/reduce_scatter | solution.py:277
  1272.5 61.6 %reduce-scatter.22.cloned.1.call-done = bf16[384,192]{0,1:T(8,128)(2,1)} async-done(((bf16[384,1536]{0,1:T(8,128)(2,1)}), bf16[384,192]{0,1:T(8,128)(2,1)}) %reduce-scatter.22.cloned.1.call-update) | async-done | bytes 147472 | tf_op jit(solution)/shard_map/reduce_scatter | solution.py:274
  1336.9 69.1 %reduce-scatter.20.cloned.1.call-done = bf16[192,768]{1,0:T(8,128)(2,1)} async-done(((bf16[1536,768]{1,0:T(8,128)(2,1)}), bf16[192,768]{1,0:T(8,128)(2,1)}) %reduce-scatter.20.cloned.1.call-update) | async-done | bytes 294928 | tf_op jit(solution)/shard_map/reduce_scatter | solution.py:271
  1414.2 92.7 %reduce-scatter.28.cloned.1.call-done = f32[48,2]{1,0:T(8,128)} async-done(((f32[1536,2]{1,0:T(8,128)}), f32[48,2]{1,0:T(8,128)}) %reduce-scatter.28.cloned.1.call-update) | async-done | bytes 400
  1513.2 53.7 %reduce-scatter.14.cloned.1.call-done = bf16[512,1536]{1,0:T(8,128)(2,1)} async-done(((bf16[2048,1536]{1,0:T(8,128)(2,1)}), bf16[512,1536]{1,0:T(8,128)(2,1)}) %reduce-scatter.14.cloned.1.call-update) | async-done | bytes 1572880 | tf_op jit(solution)/shard_map/reduce_scatter | solution.py:202
  1573.1 39.3 %all-reduce = (f32[7]{0:T(128)S(1)}, f32[7]{0:T(128)S(1)}) all-reduce(f32[7]{0:T(128)S(1)} %stack.102, f32[7]{0:T(128)S(1)} %stack.114), channel_id=1, replica_groups=mesh['dp'=8,'tensor'=4] {'dp','tensor'}, use_global_device_ids=true, to_apply=%region_25.26 | all-reduce | flops 14 | bytes 112 | tf_op jit(solution)/shard_map/psum | solution.py:336
  (331 shorter events, 342.8 us)
Async XLA Ops:
  7.2 58.3 %all-gather.12.cloned.1.call-start = ((), (), s32[]{:S(2)}) async-start(), calls=%async_computation.10 | async-start | bytes 2654208 | tf_op jit(solution)/shard_map/all_gather | solution.py:156
  9.2 103.4 %all-gather.10.cloned.1.call-start = ((), (), s32[]{:S(2)}) async-start(), calls=%async_computation.9 | async-start | bytes 7864320 | tf_op jit(solution)/shard_map/all_gather | solution.py:167
  58.4 125.3 %all-gather.14.cloned.1.call-start = ((), (), s32[]{:S(2)}) async-start(), calls=%async_computation.11 | async-start | bytes 1327104 | tf_op jit(solution)/shard_map/all_gather | solution.py:157
  59.1 233.5 %reduce-scatter.12.cloned.1.call-start = ((), (), s32[]{:S(2)}) async-start(), calls=%async_computation.12 | async-start | bytes 15728640 | tf_op jit(solution)/shard_map/reduce_scatter | solution.py:184
  60.7 77.0 %copy-start.23 = (f32[1024,48]{0,1:T(8,128)}, f32[1024,48]{0,1:T(8,128)S(1)}, u32[]{:S(2)}) copy-start(f32[1024,48]{0,1:T(8,128)S(1)} %get-tuple-element.309) | copy-start | bytes 589828
  193.5 99.2 %copy-start.7 = (bf16[512,1536]{1,0:T(8,128)(2,1)S(1)}, bf16[512,1536]{1,0:T(8,128)(2,1)}, u32[]{:S(2)}) copy-start(bf16[512,1536]{1,0:T(8,128)(2,1)} %param.22) | copy-start | bytes 4718596
  193.5 200.8 %all-gather.18.cloned.1.call-start = ((), (), s32[]{:S(2)}) async-start(), calls=%async_computation.14 | async-start | bytes 7077888 | tf_op jit(solution)/shard_map/all_gather | solution.py:158
  196.1 100.6 %copy-start.39 = (f32[1536]{0:T(1024)S(1)}, f32[1536]{0:T(1024)}, u32[]{:S(2)}) copy-start(f32[1536]{0:T(1024)} %get-tuple-element.192) | copy-start | bytes 18436
  196.1 244.8 %all-gather.16.cloned.1.call-start = ((), (), s32[]{:S(2)}) async-start(), calls=%async_computation.13 | async-start | bytes 7864320 | tf_op jit(solution)/shard_map/all_gather | solution.py:194
  295.0 400.9 %copy-start.43 = (f32[512]{0:T(512)}, f32[512]{0:T(512)S(1)}, u32[]{:S(2)}) copy-start(f32[512]{0:T(512)S(1)} %fusion.143) | copy-start | bytes 6148
  298.1 206.0 %all-gather.20.cloned.1.call-start = ((), (), s32[]{:S(2)}) async-start(), calls=%async_computation.15 | async-start | bytes 3538944 | tf_op jit(solution)/shard_map/all_gather | solution.py:159
  299.0 251.7 %all-gather.22.cloned.1.call-start = ((), (), s32[]{:S(2)}) async-start(), calls=%async_computation.17 | async-start | bytes 7864320 | tf_op jit(solution)/shard_map/all_gather | solution.py:213
  299.8 391.8 %reduce-scatter.16.cloned.1.call-start = ((), (), s32[]{:S(2)}) async-start(), calls=%async_computation.18 | async-start | bytes 15728640 | tf_op jit(solution)/shard_map/reduce_scatter | solution.py:226
  592.3 103.6 %copy-start.15 = (bf16[512,1536]{1,0:T(8,128)(2,1)S(1)}, bf16[512,1536]{1,0:T(8,128)(2,1)}, u32[]{:S(2)}) copy-start(bf16[512,1536]{1,0:T(8,128)(2,1)} %param.23) | copy-start | bytes 4718596
  592.3 152.6 %all-gather.24.cloned.1.call-start = ((), (), s32[]{:S(2)}) async-start(), calls=%async_computation.19 | async-start | bytes 7864320 | tf_op jit(solution)/shard_map/all_gather | solution.py:235
  698.3 369.2 %reduce-scatter.18.cloned.1.call-start = ((), (), s32[]{:S(2)}) async-start(), calls=%async_computation.20 | async-start | bytes 7864320 | tf_op jit(solution)/shard_map/reduce_scatter | solution.py:255
  759.6 225.6 %copy-start.24 = (f32[1024,48]{0,1:T(8,128)S(1)}, f32[1024,48]{0,1:T(8,128)}, u32[]{:S(2)}) copy-start(f32[1024,48]{0,1:T(8,128)} %copy-done.23) | copy-start | bytes 589828
  759.6 225.6 %copy-start.32 = (f32[1024,48]{0,1:T(8,128)S(1)}, f32[1024,48]{0,1:T(8,128)}, u32[]{:S(2)}) copy-start(f32[1024,48]{0,1:T(8,128)} %get-tuple-element.307) | copy-start | bytes 589828
  1009.1 136.5 %reduce-scatter.26.cloned.1.call-start = ((), (), s32[]{:S(2)}) async-start(), calls=%async_computation.24 | async-start | bytes 3538944 | tf_op jit(solution)/shard_map/reduce_scatter | solution.py:280
  1020.4 246.3 %reduce-scatter.24.cloned.1.call-start = ((), (), s32[]{:S(2)}) async-start(), calls=%async_computation.23 | async-start | bytes 7077888 | tf_op jit(solution)/shard_map/reduce_scatter | solution.py:277
  1043.3 290.7 %reduce-scatter.22.cloned.1.call-start = ((), (), s32[]{:S(2)}) async-start(), calls=%async_computation.22 | async-start | bytes 1327104 | tf_op jit(solution)/shard_map/reduce_scatter | solution.py:274
  1052.0 353.9 %reduce-scatter.20.cloned.1.call-start = ((), (), s32[]{:S(2)}) async-start(), calls=%async_computation.21 | async-start | bytes 2654208 | tf_op jit(solution)/shard_map/reduce_scatter | solution.py:271
  1061.3 445.6 %reduce-scatter.28.cloned.1.call-start = ((), (), s32[]{:S(2)}) async-start(), calls=%async_computation.25 | async-start | bytes 811008
  1071.5 495.4 %reduce-scatter.14.cloned.1.call-start = ((), (), s32[]{:S(2)}) async-start(), calls=%async_computation.16 | async-start | bytes 7864320 | tf_op jit(solution)/shard_map/reduce_scatter | solution.py:202
  1149.3 119.9 %copy-start.21 = (f32[2,192,1024]{2,1,0:T(8,128)S(1)}, f32[2,192,1024]{2,1,0:T(8,128)}, u32[]{:S(2)}) copy-start(f32[2,192,1024]{2,1,0:T(8,128)} %param.32) | copy-start | bytes 4718596
  1272.4 141.8 %copy-start.53 = (f32[512]{0:T(512)S(1)}, f32[512]{0:T(512)}, u32[]{:S(2)}) copy-start(f32[512]{0:T(512)} %copy-done.52) | copy-start | bytes 6148
  1272.4 235.5 %copy-start.55 = (f32[2,48]{1,0:T(2,128)S(1)}, f32[2,48]{1,0:T(2,128)}, u32[]{:S(2)}) copy-start(f32[2,48]{1,0:T(2,128)} %param.34) | copy-start | bytes 1156
  1272.4 235.5 %copy-start.56 = (f32[2,48]{1,0:T(2,128)S(1)}, f32[2,48]{1,0:T(2,128)}, u32[]{:S(2)}) copy-start(f32[2,48]{1,0:T(2,128)} %param.39) | copy-start | bytes 1156
  1272.4 294.5 %copy-start.5 = (f32[512,1536]{1,0:T(8,128)S(1)}, f32[512,1536]{1,0:T(8,128)}, u32[]{:S(2)}) copy-start(f32[512,1536]{1,0:T(8,128)} %copy-done.3) | copy-start | bytes 9437188
  1272.4 294.5 %copy-start.40 = (f32[1536]{0:T(1024)S(1)}, f32[1536]{0:T(1024)}, u32[]{:S(2)}) copy-start(f32[1536]{0:T(1024)} %get-tuple-element.192) | copy-start | bytes 18436
  1272.4 294.5 %copy-start.44 = (f32[512]{0:T(512)S(1)}, f32[512]{0:T(512)}, u32[]{:S(2)}) copy-start(f32[512]{0:T(512)} %copy-done.43) | copy-start | bytes 6148
  1272.5 294.5 %copy-start.51 = (f32[512]{0:T(512)S(1)}, f32[512]{0:T(512)}, u32[]{:S(2)}) copy-start(f32[512]{0:T(512)} %copy-done.50) | copy-start | bytes 6148
  (55 other events, 492.1 us)
Sparse Core Ops, SparseCore 0:
  10.8 54.6 all-gather.11
  67.6 44.9 all-gather.9
  115.3 41.0 all-gather.13
  193.6 99.0 reduce-scatter.11
  295.3 99.0 all-gather.17
  396.3 44.5 all-gather.15
  443.7 60.4 all-gather.19
  505.7 44.9 all-gather.21
  592.4 99.0 reduce-scatter.15
  698.5 46.3 all-gather.23
  1009.2 58.3 reduce-scatter.17
  1071.4 74.1 reduce-scatter.25
  1149.6 117.0 reduce-scatter.23
  1270.9 63.1 reduce-scatter.21
  1337.8 68.1 reduce-scatter.19
  1412.3 94.5 reduce-scatter.27
  1509.5 57.4 reduce-scatter.13
where the time goes:
time: 1660 us; the launch traced here: 1640 us
  waiting for transfers between devices  985 us (59%)
  matrix products  246 us (15%)
  local copies, waits for them, and re-layouts  178 us (11%)
  other arithmetic  125 us (8%)
  blocking collectives  82.4 us (5%)
  between operations  24.1 us (1%)
    reduce_scatter x1, waiting for transfers between devices, shards(): lax.psum_scatter(gate_up_grad.astype(jnp.bfloat16), 'dp', scatter_dimensi...  117 us
    reduce_scatter x1, waiting for transfers between devices, shards(): lax.psum_scatter(contract_cols(gate_slice, gate_up_work[0]) + contract_co...  99.2 us
    reduce_scatter x1, waiting for transfers between devices, shards(): lax.psum_scatter(jnp.dot(lax.slice_in_dim(attention_rows, 0, shard_rows *...  96.5 us
    all_gather x1, waiting for transfers between devices, shards(): lax.all_gather(gate_up_weight.astype(jnp.bfloat16), 'dp', axis=1, tiled=T...  94.5 us
    unnamed x18, waiting for transfers between devices  93.7 us
    reduce_scatter x1, waiting for transfers between devices, shards(): lax.psum_scatter(qkv_weight_grad.astype(jnp.bfloat16), 'dp', scatter_dime...  69.1 us
    reduce_scatter x1, waiting for transfers between devices, shards(): lax.psum_scatter(out_weight_grad.astype(jnp.bfloat16), 'dp', scatter_dime...  61.6 us
    dynamic_update_slice x8, local copies, waits for them, and re-layouts, shards(): lax.map(attend_back, (queries, key_rows, value_rows, attended_grad, log_t...  60.4 us
  transfers between devices with their start and end apart: 17, of which 16 were waited for; matrix products, arithmetic and copies ran while one was open for 12% of the time, Pallas kernels for 0%

commit v1 on v0

v1 whole, which is shorter than its diff:
```python
import functools

import jax
import jax.numpy as jnp
import numpy as np
from jax import lax
from jax.experimental import pallas as pl
from jax.experimental.pallas import tpu as pltpu
from jax.sharding import PartitionSpec as P

HEAD = 96
PAD = 128
SEQ_LEN = 1024
SEQS_DEV = 2
STEP = 10
GROUP = 2

NORM_EPSILON = 1e-05
ROPE_THETA = 100000.0
BETA_ONE = 0.9
BETA_TWO = 0.999
ADAM_EPSILON = 1e-06
WEIGHT_DECAY = 0.01
LEARN_RATE = 0.3
NEGATIVE = -1e30
LOG2E = 1.4426950408889634
SCALE = HEAD ** (-0.5)
Q_ROWS = 256
G_COLS = 4 * HEAD
G_PAD = 4 * PAD
VMEM_LIMIT = 56 << 20

F32 = jnp.float32
BF16 = jnp.bfloat16
VM = pl.BlockSpec(memory_space=pltpu.VMEM)
SM = pl.BlockSpec(memory_space=pltpu.SMEM)


def dot_nn(a, b):
    return lax.dot_general(a, b, (((1,), (0,)), ((), ())), preferred_element_type=F32)


def dot_nt(a, b):
    return lax.dot_general(a, b, (((1,), (1,)), ((), ())), preferred_element_type=F32)


def dot_tn(a, b):
    return lax.dot_general(a, b, (((0,), (0,)), ((), ())), preferred_element_type=F32)


def params():
    return pltpu.CompilerParams(vmem_limit_bytes=VMEM_LIMIT)


def cost(flops, moved):
    return pl.CostEstimate(flops=int(flops), bytes_accessed=int(moved), transcendentals=0)


def spread_matrix():
    source = lax.broadcasted_iota(jnp.int32, (G_COLS, G_PAD), 0)
    target = lax.broadcasted_iota(jnp.int32, (G_COLS, G_PAD), 1)
    return ((target // PAD) * HEAD + target % PAD == source) & (target % PAD < HEAD)


def assemble_kernel(n_z, blk, info, spread, *refs):
    n_blocks = 2 * n_z
    blocks, out, rows = refs[:n_blocks], refs[n_blocks], refs[n_blocks + 1]
    z, x = info[0], info[1]
    for j in range(2):
        for k in range(n_z):
            source = (lax.rem(z + n_z - k, n_z)) * 2 + (x ^ j)
            rows[pl.ds(pl.multiple_of(source * blk, 16), blk), :] = blocks[j * n_z + k][...]
    groups = out.shape[1] // G_PAD
    for g in range(groups):
        out[:, g * G_PAD : (g + 1) * G_PAD] = dot_nn(
            rows[:, g * G_COLS : (g + 1) * G_COLS], spread[...]
        ).astype(BF16)


def assemble(blocks, info, spread, n_z):
    blk, cols = blocks[0].shape
    depth = blk * len(blocks)
    wide = cols // G_COLS * G_PAD
    return pl.pallas_call(
        functools.partial(assemble_kernel, n_z, blk),
        out_shape=jax.ShapeDtypeStruct((depth, wide), BF16),
        in_specs=[SM, VM] + [VM] * len(blocks),
        out_specs=VM,
        scratch_shapes=[pltpu.VMEM((depth, cols), BF16)],
        compiler_params=params(),
        cost_estimate=cost(2 * depth * cols * G_PAD, 4 * depth * cols),
        name="assemble_weights",
    )(info, spread, *blocks)


def swap_halves(values):
    lane = lax.broadcasted_iota(jnp.int32, values.shape, 1)
    return jnp.where(
        lane < HEAD // 2,
        pltpu.roll(values, PAD - HEAD // 2, 1),
        pltpu.roll(values, HEAD // 2, 1),
    )


def store_relative(refs, rows_each, start, local, value):
    index = start // rows_each
    offset = start % rows_each
    for r, ref in enumerate(refs):

        @pl.when((local ^ r) == index)
        def _():
            ref[offset : offset + value.shape[0], :] = value


def attn_fwd_kernel(nb, rows_each, kv, info, *refs):
    xs = refs[:nb]
    gain, w_qkv, w_out, cos_t, sin_t = refs[nb : nb + 5]
    normed, qkvp, att, lse = refs[nb + 5 : nb + 9]
    parts = refs[nb + 9 : nb + 9 + nb]
    length, local = info[0], info[1]
    seq_len = nb * rows_each
    chunk = 32
    for r in range(nb):
        base = (local ^ r) * rows_each

        def norm_rows(i, carry):
            v = xs[r][pl.ds(pl.multiple_of(i * chunk, chunk), chunk), :].astype(F32)
            inv = lax.rsqrt(jnp.mean(v * v, axis=-1, keepdims=True) + NORM_EPSILON)
            normed[pl.ds(pl.multiple_of(base + i * chunk, chunk), chunk), :] = (
                v * inv * gain[...]
            ).astype(BF16)
            return carry

        lax.fori_loop(0, rows_each // chunk, norm_rows, 0)

    for i in range(seq_len // Q_ROWS):
        rows = slice(i * Q_ROWS, (i + 1) * Q_ROWS)
        for j in range(kv):
            proj = dot_nn(normed[rows, :], w_qkv[:, j * G_PAD : (j + 1) * G_PAD])
            for h in range(4):
                part = proj[:, h * PAD : (h + 1) * PAD]
                if h < 3:
                    part = part * cos_t[rows, :] + swap_halves(part) * sin_t[rows, :]
                qkvp[rows, (4 * j + h) * PAD : (4 * j + h + 1) * PAD] = part.astype(BF16)

    lse[...] = jnp.zeros_like(lse)

    def one_head(h, carry):
        group = h // GROUP
        q_col = pl.ds(pl.multiple_of((4 * group + h % GROUP) * PAD, PAD), PAD)
        k_col = pl.ds(pl.multiple_of((4 * group + 2) * PAD, PAD), PAD)
        v_col = pl.ds(pl.multiple_of((4 * group + 3) * PAD, PAD), PAD)
        a_col = pl.ds(pl.multiple_of(h * PAD, PAD), PAD)
        for i in range(seq_len // Q_ROWS):
            n = (i + 1) * Q_ROWS
            rows = slice(i * Q_ROWS, n)
            s = dot_nt(qkvp[rows, q_col], qkvp[0:n, k_col])
            row_ids = lax.broadcasted_iota(jnp.int32, (Q_ROWS, 1), 0) + i * Q_ROWS + 1
            limit = jnp.minimum(row_ids, length)
            col_ids = lax.broadcasted_iota(jnp.int32, (Q_ROWS, n), 1)
            s = jnp.where(col_ids < limit, s, NEGATIVE)
            top = jnp.max(s, axis=-1, keepdims=True)
            e = jnp.exp2((s - top) * (SCALE * LOG2E))
            total = jnp.sum(e, axis=-1, keepdims=True)
            p = (e * (1.0 / total)).astype(BF16)
            att[rows, a_col] = dot_nn(p, qkvp[0:n, v_col]).astype(BF16)
            lane = lax.broadcasted_iota(jnp.int32, (Q_ROWS, PAD), 1)
            log_total = top * (SCALE * LOG2E) + jnp.log2(total)
            lse[rows, :] = jnp.where(lane == h, log_total, lse[rows, :])
        return carry

    lax.fori_loop(0, kv * GROUP, one_head, 0)

    for i in range(seq_len // Q_ROWS):
        rows = slice(i * Q_ROWS, (i + 1) * Q_ROWS)
        part = dot_nt(att[rows, :], w_out[...]).astype(BF16)
        store_relative(parts, rows_each, i * Q_ROWS, local, part)


def attn_fwd(xs, info, gain, w_qkv, w_out, cos_t, sin_t):
    nb = len(xs)
    rows_each, width = xs[0].shape
    seq_len = nb * rows_each
    kv = w_qkv.shape[1] // G_PAD
    heads = kv * GROUP
    flops = 2 * seq_len * width * (kv * G_PAD + heads * PAD) + heads * seq_len * seq_len * 4 * 256
    return pl.pallas_call(
        functools.partial(attn_fwd_kernel, nb, rows_each, kv),
        out_shape=[
            jax.ShapeDtypeStruct((seq_len, width), BF16),
            jax.ShapeDtypeStruct((seq_len, kv * G_PAD), BF16),
            jax.ShapeDtypeStruct((seq_len, heads * PAD), BF16),
            jax.ShapeDtypeStruct((seq_len, PAD), F32),
        ]
        + [jax.ShapeDtypeStruct((rows_each, width), BF16)] * nb,
        in_specs=[SM] + [VM] * (nb + 5),
        out_specs=[VM] * (4 + nb),
        compiler_params=params(),
        cost_estimate=cost(flops, 20 << 20),
        name="attention_forward",
    )(info, *xs, gain, w_qkv, w_out, cos_t, sin_t)


def attn_bwd_kernel(nb, rows_each, kv, info, *refs):
    ags = refs[:nb]
    w_qkv, w_out, qkvp, lse, cos_t, sin_t = refs[nb : nb + 6]
    dproj = refs[nb + 6]
    parts = refs[nb + 7 : nb + 7 + nb]
    datt, dk_acc, dv_acc = refs[nb + 7 + nb :]
    length, local = info[0], info[1]
    seq_len = nb * rows_each
    heads = kv * GROUP
    for r in range(nb):
        base = (local ^ r) * rows_each
        for i in range(rows_each // Q_ROWS):
            datt[pl.ds(pl.multiple_of(base + i * Q_ROWS, Q_ROWS), Q_ROWS), :] = dot_nn(
                ags[r][i * Q_ROWS : (i + 1) * Q_ROWS, :], w_out[...]
            ).astype(BF16)

    def unrotate(grad, rows):
        return grad * cos_t[rows, :] - swap_halves(grad) * sin_t[rows, :]

    def one_head(h, carry):
        group = h // GROUP
        member = h % GROUP
        q_col = pl.ds(pl.multiple_of((4 * group + member) * PAD, PAD), PAD)
        k_col = pl.ds(pl.multiple_of((4 * group + 2) * PAD, PAD), PAD)
        v_col = pl.ds(pl.multiple_of((4 * group + 3) * PAD, PAD), PAD)
        a_col = pl.ds(pl.multiple_of(h * PAD, PAD), PAD)

        @pl.when(member == 0)
        def _():
            dk_acc[...] = jnp.zeros_like(dk_acc)
            dv_acc[...] = jnp.zeros_like(dv_acc)

        for i in range(seq_len // Q_ROWS):
            n = (i + 1) * Q_ROWS
            rows = slice(i * Q_ROWS, n)
            q = qkvp[rows, q_col]
            keys = qkvp[0:n, k_col]
            do = datt[rows, a_col]
            lane = lax.broadcasted_iota(jnp.int32, (Q_ROWS, PAD), 1)
            row_lse = jnp.sum(jnp.where(lane == h, lse[rows, :], 0.0), axis=-1, keepdims=True)
            s = dot_nt(q, keys)
            row_ids = lax.broadcasted_iota(jnp.int32, (Q_ROWS, 1), 0) + i * Q_ROWS + 1
            limit = jnp.minimum(row_ids, length)
            col_ids = lax.broadcasted_iota(jnp.int32, (Q_ROWS, n), 1)
            s = jnp.where(col_ids < limit, s, NEGATIVE)
            p = jnp.exp2(s * (SCALE * LOG2E) - row_lse)
            dp = dot_nt(do, qkvp[0:n, v_col])
            inner = jnp.sum(p * dp, axis=-1, keepdims=True)
            ds = (p * (dp - inner)).astype(BF16)
            dv_acc[0:n, :] += dot_tn(p.astype(BF16), do)
            dk_acc[0:n, :] += dot_tn(ds, q)
            dq = dot_nn(ds, keys) * SCALE
            dproj[rows, q_col] = unrotate(dq, rows).astype(BF16)

        @pl.when(member == GROUP - 1)
        def _():
            for i in range(seq_len // Q_ROWS):
                rows = slice(i * Q_ROWS, (i + 1) * Q_ROWS)
                dproj[rows, k_col] = unrotate(dk_acc[rows, :] * SCALE, rows).astype(BF16)
                dproj[rows, v_col] = dv_acc[rows, :].astype(BF16)

        return carry

    lax.fori_loop(0, heads, one_head, 0)

    for i in range(seq_len // Q_ROWS):
        rows = slice(i * Q_ROWS, (i + 1) * Q_ROWS)
        part = dot_nt(dproj[rows, :], w_qkv[...]).astype(BF16)
        store_relative(parts, rows_each, i * Q_ROWS, local, part)


def attn_bwd(ags, info, w_qkv, w_out, qkvp, lse, cos_t, sin_t):
    nb = len(ags)
    rows_each, width = ags[0].shape
    seq_len = nb * rows_each
    kv = w_qkv.shape[1] // G_PAD
    heads = kv * GROUP
    flops = 2 * seq_len * width * (kv * G_PAD + heads * PAD) + heads * seq_len * seq_len * 10 * 256
    return pl.pallas_call(
        functools.partial(attn_bwd_kernel, nb, rows_each, kv),
        out_shape=[jax.ShapeDtypeStruct((seq_len, kv * G_PAD), BF16)]
        + [jax.ShapeDtypeStruct((rows_each, width), BF16)] * nb,
        in_specs=[SM] + [VM] * (nb + 6),
        out_specs=[VM] * (1 + nb),
        scratch_shapes=[
            pltpu.VMEM((seq_len, heads * PAD), BF16),
            pltpu.VMEM((seq_len, PAD), F32),
            pltpu.VMEM((seq_len, PAD), F32),
        ],
        compiler_params=params(),
        cost_estimate=cost(flops, 20 << 20),
        name="attention_backward",
    )(info, *ags, w_qkv, w_out, qkvp, lse, cos_t, sin_t)


def weight_grad_kernel(n_z, blk, n_pairs, row_counts, info, spread, *refs):
    lefts, rights = refs[:n_pairs], refs[n_pairs : 2 * n_pairs]
    same, other = refs[2 * n_pairs :]
    z, x = info[0], info[1]
    width = lefts[0].shape[1]
    for c in range(width // G_COLS):
        cols = slice(c * G_COLS, (c + 1) * G_COLS)
        total = None
        for p in range(n_pairs):
            if row_counts is None:
                right = rights[p][...]
            else:
                start = pl.multiple_of(info[2 + p], 16)
                right = rights[p][pl.ds(start, lefts[p].shape[0]), :]
            term = dot_tn(lefts[p][:, cols], right)
            total = term if total is None else total + term
        compact = dot_nt(total.astype(BF16), spread[...]).astype(BF16)
        for b in range(G_COLS // blk):
            owner = c * (G_COLS // blk) + b
            shift = lax.rem(owner // 2 + n_z - z, n_z)
            value = compact[b * blk : (b + 1) * blk, :]

            @pl.when(x == owner % 2)
            def _():
                same[shift, :, :] = value

            @pl.when(x != owner % 2)
            def _():
                other[shift, :, :] = value


def weight_grad(lefts, rights, info, spread, n_z, blk, right_cols, offsets):
    n_pairs = len(lefts)
    rows, width = lefts[0].shape
    out = jax.ShapeDtypeStruct((n_z, blk, G_COLS), BF16)
    right_specs = [
        pl.BlockSpec((right.shape[0], G_PAD), functools.partial(lambda c, i: (0, c), right_cols))
        for right in rights
    ]
    full = lambda a: pl.BlockSpec(a.shape, lambda i: (0,) * a.ndim)
    return pl.pallas_call(
        functools.partial(weight_grad_kernel, n_z, blk, n_pairs, offsets),
        grid=(1,),
        out_shape=[out, out],
        in_specs=[SM, full(spread)] + [full(left) for left in lefts] + right_specs,
        out_specs=[pl.BlockSpec(out.shape, lambda i: (0, 0, 0))] * 2,
        compiler_params=params(),
        cost_estimate=cost(2 * n_pairs * rows * width * G_PAD, 12 << 20),
        name="attention_weight_gradient",
    )(info, spread, *lefts, *rights)


def ffn_kernel(nb, rows_each, *refs):
    ns, ups = refs[:nb], refs[nb : 2 * nb]
    w = refs[2 * nb]
    hidden, d_gate, d_up = refs[2 * nb + 1 : 2 * nb + 4]
    outs = refs[2 * nb + 4 : 3 * nb + 4]
    grads = refs[3 * nb + 4 : 4 * nb + 4]
    for r in range(nb):

        def rows_step(i, carry):
            rows = pl.ds(pl.multiple_of(i * Q_ROWS, Q_ROWS), Q_ROWS)
            kept = pl.ds(pl.multiple_of(r * rows_each + i * Q_ROWS, Q_ROWS), Q_ROWS)
            n = ns[r][rows, :]
            gate = dot_nn(n, w[0])
            up = dot_nn(n, w[1])
            sig = 1.0 / (1.0 + jnp.exp(-gate))
            silu = gate * sig
            hid = (silu * up).astype(BF16)
            hidden[kept, :] = hid
            dh = dot_nn(ups[r][rows, :], w[2])
            dg = (dh * up * sig * (1.0 + gate * (1.0 - sig))).astype(BF16)
            du = (dh * silu).astype(BF16)
            d_gate[kept, :] = dg
            d_up[kept, :] = du
            grads[r][rows, :] = (dot_nt(dg, w[0]) + dot_nt(du, w[1])).astype(BF16)
            outs[r][rows, :] = dot_nt(hid, w[2]).astype(BF16)
            return carry

        lax.fori_loop(0, rows_each // Q_ROWS, rows_step, 0)


def ffn(ns, ups, w):
    nb = len(ns)
    rows_each, width = ns[0].shape
    units = w.shape[2]
    kept = jax.ShapeDtypeStruct((nb * rows_each, units), BF16)
    part = jax.ShapeDtypeStruct((rows_each, width), BF16)
    return pl.pallas_call(
        functools.partial(ffn_kernel, nb, rows_each),
        out_shape=[kept] * 3 + [part] * (2 * nb),
        in_specs=[VM] * (2 * nb + 1),
        out_specs=[VM] * (3 + 2 * nb),
        compiler_params=params(),
        cost_estimate=cost(12 * nb * rows_each * width * units, 28 << 20),
        name="feed_forward",
    )(*ns, *ups, w)


def ffn_grad_kernel(n_blocks, n_halves, rows_each, *refs):
    ns, ups = refs[:n_blocks], refs[n_blocks : 2 * n_blocks]
    kept = refs[2 * n_blocks : 2 * n_blocks + 3 * n_halves]
    out = refs[-1]
    width = ns[0].shape[1]
    per_half = n_blocks // n_halves
    tile = G_COLS
    for which in range(3):
        lefts = ups if which == 2 else ns

        def col_step(c, carry):
            cols = pl.ds(pl.multiple_of(c * tile, tile), tile)
            total = None
            for b in range(n_blocks):
                half, r = b // per_half, b % per_half
                right = kept[3 * half + (0 if which == 2 else 1 + which)]
                term = dot_tn(
                    lefts[b][:, cols], right[r * rows_each : (r + 1) * rows_each, :]
                )
                total = term if total is None else total + term
            out[which, cols, :] = total.astype(BF16)
            return carry

        lax.fori_loop(0, width // tile, col_step, 0)


def ffn_grad(ns, ups, kept):
    n_blocks = len(ns)
    rows_each, width = ns[0].shape
    units = kept[0].shape[1]
    return pl.pallas_call(
        functools.partial(ffn_grad_kernel, n_blocks, len(kept) // 3, rows_each),
        out_shape=jax.ShapeDtypeStruct((3, width, units), BF16),
        in_specs=[VM] * (2 * n_blocks + len(kept)),
        out_specs=VM,
        compiler_params=params(),
        cost_estimate=cost(6 * n_blocks * rows_each * width * units, 34 << 20),
        name="feed_forward_weight_gradient",
    )(*ns, *ups, *kept)


def permute_xor(value, axis, bit):
    size = lax.axis_size(axis)
    return lax.ppermute(value, axis, [(i, i ^ bit) for i in range(size)])


def shift_z(value, k, n_z):
    return lax.ppermute(
        value, "dp", [(z * 2 + x, ((z + k) % n_z) * 2 + x) for z in range(n_z) for x in range(2)]
    )


def bits_down(size):
    bits = []
    bit = size // 2
    while bit:
        bits.append(bit)
        bit //= 2
    return bits


def gather_relative(block):
    size = lax.axis_size("tensor")
    have = {0: block}
    for bit in bits_down(size):
        for r in list(have):
            have[r ^ bit] = permute_xor(have[r], "tensor", bit)
    return [have[r] for r in range(size)]


def scatter_relative(parts):
    size = lax.axis_size("tensor")
    have = dict(enumerate(parts))
    for bit in reversed(bits_down(size)):
        for r in [r for r in have if r & bit]:
            received = permute_xor(have.pop(r), "tensor", bit)
            summed = have[r ^ bit].astype(F32) + received.astype(F32)
            have[r ^ bit] = summed if bit == size // 2 else summed.astype(BF16)
    return have[0].astype(F32)


def gather_dp(block, n_z):
    same = [block] + [shift_z(block, k, n_z) for k in range(1, n_z)]
    return same + [permute_xor(b, "dp", 1) for b in same]


def scatter_dp(same, other, n_z):
    received = permute_xor(other, "dp", 1)
    held = same.astype(F32) + received.astype(F32)
    total = held[0]
    narrow = held.astype(BF16)
    for k in range(1, n_z):
        total = total + shift_z(narrow[k], k, n_z).astype(F32)
    return total


def sum_everywhere(value):
    for axis in ("tensor", "dp"):
        for bit in reversed(bits_down(lax.axis_size(axis))):
            value = value + permute_xor(value, axis, bit)
    return value


def rms_norm(values, gain_row):
    return (
        values
        * lax.rsqrt(jnp.mean(values * values, axis=-1, keepdims=True) + NORM_EPSILON)
        * gain_row
    )


def rotary_tables():
    half = HEAD // 2
    frequency = ROPE_THETA ** (-(jnp.arange(half, dtype=F32) * (2.0 / HEAD)))
    angles = jnp.arange(SEQ_LEN, dtype=F32)[:, None] * frequency[None, :]
    cosine, sine = jnp.cos(angles), jnp.sin(angles)
    empty = jnp.zeros((SEQ_LEN, PAD - HEAD), F32)
    return (
        jnp.concatenate([cosine, cosine, empty], axis=1),
        jnp.concatenate([-sine, sine, empty], axis=1),
    )


def shards(
    tokens,
    cotangent,
    lengths,
    qkv_weight,
    out_weight,
    gate_up_weight,
    down_weight,
    norm_gains,
    qkv_first,
    out_first,
    gate_up_first,
    down_first,
    gains_first,
    qkv_second,
    out_second,
    gate_up_second,
    down_second,
    gains_second,
):
    rows_each, width = tokens.shape
    n_t = lax.axis_size("tensor")
    n_dp = lax.axis_size("dp")
    n_z = n_dp // 2
    nb = n_t // 2
    t = lax.axis_index("tensor")
    d = lax.axis_index("dp")
    local = lax.rem(t, nb)
    mine = t // nb
    place = jnp.stack([d // 2, lax.rem(d, 2)]).astype(jnp.int32)
    info = [
        jnp.stack([lengths[mine], local]).astype(jnp.int32),
        jnp.stack([lengths[1 - mine], local]).astype(jnp.int32),
    ]
    spread = spread_matrix().astype(BF16)
    blk = qkv_weight.shape[0]
    kv = qkv_weight.shape[1] // G_COLS

    gain_cols = norm_gains.shape[1]
    gain_start = (d * n_t + t) * gain_cols
    gain_rows = lax.dynamic_update_slice(
        jnp.zeros((2, width), F32),
        norm_gains.astype(BF16).astype(F32),
        (0, gain_start),
    )
    gain_work = sum_everywhere(gain_rows)
    attention_gain, feedforward_gain = gain_work[0:1], gain_work[1:2]

    qkv_half = qkv_weight.astype(BF16)
    out_half = out_weight.astype(BF16).T
    w_qkv = assemble(gather_dp(qkv_half, n_z), place, spread, n_z)
    w_out_cols = out_half.shape[1]
    out_fill = -w_out_cols % G_COLS
    out_blocks = gather_dp(out_half, n_z)
    if out_fill:
        out_blocks = [jnp.pad(b, ((0, 0), (0, out_fill))) for b in out_blocks]
    w_out = assemble(out_blocks, place, spread, n_z)[:, : kv * GROUP * PAD]
    ffn_half = jnp.concatenate(
        [gate_up_weight.astype(BF16), down_weight.astype(BF16).T[None]], axis=0
    )
    w_ffn = lax.all_gather(ffn_half, "dp", axis=1, tiled=True)

    inputs = tokens.astype(F32)
    x_blocks = gather_relative(tokens)
    cos_t, sin_t = rotary_tables()
    fwd = [
        attn_fwd(
            x_blocks[s * nb : (s + 1) * nb], info[s], attention_gain, w_qkv, w_out, cos_t, sin_t
        )
        for s in range(2)
    ]
    residual = inputs + scatter_relative(list(fwd[0][4:]) + list(fwd[1][4:]))

    n_blocks = gather_relative(rms_norm(residual, feedforward_gain).astype(BF16))
    c_blocks = gather_relative(cotangent)
    far = ffn(n_blocks[nb:], c_blocks[nb:], w_ffn)
    near = ffn(n_blocks[:nb], c_blocks[:nb], w_ffn)
    normed_two_grad = scatter_relative(list(near[3 + nb :]) + list(far[3 + nb :]))
    out_sum = scatter_relative(list(near[3 : 3 + nb]) + list(far[3 : 3 + nb]))
    layer_out = (residual + out_sum).astype(BF16)
    ffn_grads = ffn_grad(n_blocks, c_blocks, list(near[:3]) + list(far[:3]))
    ffn_sum = lax.psum_scatter(ffn_grads, "dp", scatter_dimension=1, tiled=True).astype(F32)

    _, norm_pull = jax.vjp(rms_norm, residual, feedforward_gain)
    residual_part, ffn_gain_grad = norm_pull(normed_two_grad)
    residual_grad = cotangent.astype(F32) + residual_part
    a_blocks = gather_relative(residual_grad.astype(BF16))
    bwd = [
        attn_bwd(
            a_blocks[s * nb : (s + 1) * nb],
            info[s],
            w_qkv,
            w_out,
            fwd[s][1],
            fwd[s][3],
            cos_t,
            sin_t,
        )
        for s in range(2)
    ]
    starts = [(local ^ r) * rows_each for r in range(nb)] * 2
    out_info = jnp.concatenate([place, jnp.stack(starts).astype(jnp.int32)])
    att = [fwd[0][2]] * nb + [fwd[1][2]] * nb
    att_fill = -att[0].shape[1] % G_PAD
    if att_fill:
        att = [jnp.pad(a, ((0, 0), (0, att_fill))) for a in att]
    out_pair = weight_grad(a_blocks, att, out_info, spread, n_z, blk, 0, True)
    out_grad_sum = scatter_dp(*out_pair, n_z)[:, :w_out_cols].T
    qkv_grad_sum = jnp.concatenate(
        [
            scatter_dp(
                *weight_grad(
                    [fwd[0][0], fwd[1][0]],
                    [bwd[0][0], bwd[1][0]],
                    place,
                    spread,
                    n_z,
                    blk,
                    j,
                    None,
                ),
                n_z,
            )
            for j in range(kv)
        ],
        axis=1,
    )
    normed_grad = scatter_relative(list(bwd[0][1:]) + list(bwd[1][1:]))
    _, first_pull = jax.vjp(rms_norm, inputs, attention_gain)
    input_part, attention_gain_grad = first_pull(normed_grad)
    grad_tokens = residual_grad + input_part
    gain_all = sum_everywhere(jnp.concatenate([attention_gain_grad, ffn_gain_grad], axis=0))
    gain_sums = lax.dynamic_slice(gain_all, (0, gain_start), (2, gain_cols))

    masters = (
        qkv_weight,
        out_weight,
        gate_up_weight[0],
        gate_up_weight[1],
        down_weight,
        norm_gains[0],
        norm_gains[1],
    )
    firsts = (
        qkv_first,
        out_first,
        gate_up_first[0],
        gate_up_first[1],
        down_first,
        gains_first[0],
        gains_first[1],
    )
    seconds = (
        qkv_second,
        out_second,
        gate_up_second[0],
        gate_up_second[1],
        down_second,
        gains_second[0],
        gains_second[1],
    )
    gradients = (
        qkv_grad_sum,
        out_grad_sum,
        ffn_sum[0],
        ffn_sum[1],
        ffn_sum[2].T,
        gain_sums[0],
        gain_sums[1],
    )
    correct_one = 1.0 - BETA_ONE**STEP
    correct_two = 1.0 - BETA_TWO**STEP
    new_firsts = []
    new_seconds = []
    updates = []
    for master, moment, square, gradient in zip(masters, firsts, seconds, gradients):
        moment = BETA_ONE * moment + (1.0 - BETA_ONE) * gradient
        square = BETA_TWO * square + (1.0 - BETA_TWO) * gradient * gradient
        new_firsts.append(moment)
        new_seconds.append(square)
        updates.append(
            moment / correct_one / (jnp.sqrt(square / correct_two) + ADAM_EPSILON)
            + WEIGHT_DECAY * master
        )
    squares = jnp.stack(
        [jnp.sum(master * master) for master in masters]
        + [jnp.sum(update * update) for update in updates]
    )
    norms = jnp.sqrt(sum_everywhere(squares[None])[0])
    weight_norms, all_update_norms = norms[:7], norms[7:]
    new_weights = [
        masters[number]
        - LEARN_RATE * (weight_norms[number] / all_update_norms[number]) * updates[number]
        for number in range(7)
    ]
    return (
        layer_out,
        grad_tokens,
        new_weights[0],
        new_weights[1],
        jnp.stack([new_weights[2], new_weights[3]]),
        new_weights[4],
        jnp.stack([new_weights[5], new_weights[6]]),
        new_firsts[0],
        new_firsts[1],
        jnp.stack([new_firsts[2], new_firsts[3]]),
        new_firsts[4],
        jnp.stack([new_firsts[5], new_firsts[6]]),
        new_seconds[0],
        new_seconds[1],
        jnp.stack([new_seconds[2], new_seconds[3]]),
        new_seconds[4],
        jnp.stack([new_seconds[5], new_seconds[6]]),
        weight_norms,
        all_update_norms[:5],
        all_update_norms[5:],
    )


def solution(mesh):
    rows = P(("dp", "tensor"), None)
    gains = P(None, ("dp", "tensor"))
    weights = (P("dp", "tensor"), P("tensor", "dp"), P(None, "dp", "tensor"), P("tensor", "dp"), gains)
    in_specs = (rows, rows, P("dp")) + weights * 3
    out_specs = (rows, rows) + weights * 3 + (P(), P(), P())
    return jax.shard_map(shards, mesh=mesh, in_specs=in_specs, out_specs=out_specs, check_vma=False)
```

time: 1660 us -> 762 us (0.46)
  waiting for transfers between devices: 985 us -> 325 us
  matrix products: 246 us -> 0 us
  Pallas kernels: 0 us -> 238 us
  local copies, waits for them, and re-layouts: 178 us -> 24.1 us
  starting transfers between devices: 0.7 us -> 91 us
  blocking collectives: 82.4 us -> 0 us
  other arithmetic: 125 us -> 55.5 us
    reduce_scatter x8 -> x1, waiting for transfers between devices: 564 us -> 0.01 us  [shards(): lax.psum_scatter(ffn_grads, 'dp', scatter_dimension=1, tiled=True)]
    all_gather x8 -> x1, waiting for transfers between devices: 327 us -> 0.01 us  [shards(): w_ffn = lax.all_gather(ffn_half, 'dp', axis=1, tiled=True)]
    ppermute x0 -> x65, waiting for transfers between devices: none -> 325 us  [the longest x50 301 us: permute_xor(): return lax.ppermute(value, axis, [(i, i ^ bit) for i in range(size)])]
    dot_general x43 -> x0, matrix products: 246 us -> none  [the longest x5 55.3 us: contract_cols(): lax.dot_general(left, right, (((1,), (1,)), ((), ())), preferred_element_...]
    pallas_call x0 -> x12, Pallas kernels: none -> 238 us  [the longest x2 56.4 us: ffn(): pl.pallas_call(functools.partial(ffn_kernel, nb, rows_each), out_shape=[k...]
    dynamic_update_slice x12 -> x1, local copies, waits for them, and re-layouts: 119 us -> 0.16 us  [shards(): lax.dynamic_update_slice(jnp.zeros((2, width), F32), norm_gains.astype(BF...]
    unnamed x18 -> x2, waiting for transfers between devices: 93.7 us -> 0.03 us
    ppermute x0 -> x65, starting transfers between devices: none -> 91 us  [the longest x50 53.6 us: permute_xor(): return lax.ppermute(value, axis, [(i, i ^ bit) for i in range(size)])]
  transfers between devices with their start and end apart: 17 -> 67, of which waited for: 16 -> 32; matrix products, arithmetic and copies ran while one was open for 12% -> 5% of each run, Pallas kernels for 0% -> 23%
where the time goes in v1:
time: 762 us; the launch traced here: 757 us
  waiting for transfers between devices  325 us (43%)
  Pallas kernels  238 us (31%)
  starting transfers between devices  91 us (12%)
  other arithmetic  55.5 us (7%)
  between operations  24.2 us (3%)
  local copies, waits for them, and re-layouts  24.1 us (3%)
    ppermute x50, waiting for transfers between devices, permute_xor(): return lax.ppermute(value, axis, [(i, i ^ bit) for i in range(size)])  301 us
    pallas_call x2, Pallas kernels, ffn(): pl.pallas_call(functools.partial(ffn_kernel, nb, rows_each), out_shape=[k...  56.4 us
    pallas_call x2, Pallas kernels, attn_fwd(): pl.pallas_call(functools.partial(attn_fwd_kernel, nb, rows_each, kv), out...  54.5 us
    ppermute x50, starting transfers between devices, permute_xor(): return lax.ppermute(value, axis, [(i, i ^ bit) for i in range(size)])  53.6 us
    pallas_call x2, Pallas kernels, attn_bwd(): pl.pallas_call(functools.partial(attn_bwd_kernel, nb, rows_each, kv), out...  53.5 us
    ppermute x15, starting transfers between devices, shift_z(): lax.ppermute(value, 'dp', [(z * 2 + x, (z + k) % n_z * 2 + x) for z in ra...  37.3 us
    pallas_call x1, Pallas kernels, ffn_grad(): pl.pallas_call(functools.partial(ffn_grad_kernel, n_blocks, len(kept) //...  34.3 us
    pallas_call x3, Pallas kernels, weight_grad(): pl.pallas_call(functools.partial(weight_grad_kernel, n_z, blk, n_pairs, o...  29.8 us
  transfers between devices with their start and end apart: 67, of which 32 were waited for; matrix products, arithmetic and copies ran while one was open for 5% of the time, Pallas kernels for 23%

profile of v1, /device:TPU:0, one launch (start us, length us, event | category | flops | bytes accessed | tf_op | source)
XLA Modules:
  0.0 757.1 jit_solution(5794391618887336622)
XLA Ops:
  20.5 27.9 %collective-permute-done.2 = f32[2,1536]{1,0:T(2,128)S(1)} collective-permute-done((f32[2,1536]{1,0:T(2,128)S(1)}, f32[2,1536]{1,0:T(2,128)S(1)}, u32[]{:S(2)}, u32[]{:S(2)}) %collective-permute-start.2) | collective-permute-done | bytes 12320 | tf_op jit(solution)/shard_map/ppermute | solution.py:441
  67.7 11.0 %collective-permute-done.15.refs_3_ = bf16[192,384]{1,0:T(8,128)(2,1)S(1)} collective-permute-done((bf16[192,384]{1,0:T(8,128)(2,1)S(1)}, bf16[192,384]{1,0:T(8,128)(2,1)S(1)}, u32[]{:S(2)}, u32[]{:S(2)}) %collective-permute-start.15) | collective-permute-done | bytes 147488 | tf_op jit(solution)/shard_map/ppermute | solution.py:445
  78.7 4.4 collective-permute-start.8
  91.0 7.7 %collective-permute-done.8.refs_3_ = bf16[192,768]{1,0:T(8,128)(2,1)S(1)} collective-permute-done((bf16[192,768]{1,0:T(8,128)(2,1)S(1)}, bf16[192,768]{1,0:T(8,128)(2,1)S(1)}, u32[]{:S(2)}, u32[]{:S(2)}) %collective-permute-start.8) | collective-permute-done | bytes 294944 | tf_op jit(solution)/shard_map/ppermute | solution.py:445
  108.3 5.2 collective-permute-done.9.refs_4_
  113.4 12.6 %collective-permute-done.10.refs_5_ = bf16[192,768]{1,0:T(8,128)(2,1)S(1)} collective-permute-done((bf16[192,768]{1,0:T(8,128)(2,1)S(1)}, bf16[192,768]{1,0:T(8,128)(2,1)S(1)}, u32[]{:S(2)}, u32[]{:S(2)}) %collective-permute-start.10) | collective-permute-done | bytes 294944 | tf_op jit(solution)/shard_map/ppermute | solution.py:441
  126.1 12.6 %collective-permute-done.11.refs_6_ = bf16[192,768]{1,0:T(8,128)(2,1)S(1)} collective-permute-done((bf16[192,768]{1,0:T(8,128)(2,1)S(1)}, bf16[192,768]{1,0:T(8,128)(2,1)S(1)}, u32[]{:S(2)}, u32[]{:S(2)}) %collective-permute-start.11) | collective-permute-done | bytes 294944 | tf_op jit(solution)/shard_map/ppermute | solution.py:441
  138.7 10.9 %collective-permute-done.12.refs_7_ = bf16[192,768]{1,0:T(8,128)(2,1)S(1)} collective-permute-done((bf16[192,768]{1,0:T(8,128)(2,1)S(1)}, bf16[192,768]{1,0:T(8,128)(2,1)S(1)}, u32[]{:S(2)}, u32[]{:S(2)}) %collective-permute-start.12) | collective-permute-done | bytes 294944 | tf_op jit(solution)/shard_map/ppermute | solution.py:441
  150.4 5.3 assemble_weights.2.refs_3_.refs_2_
  155.7 27.1 %attention_forward.3 = (bf16[1024,1536]{1,0:T(8,128)(2,1)}, bf16[1024,1024]{1,0:T(8,128)(2,1)}, bf16[1024,512]{1,0:T(8,128)(2,1)}, f32[1024,128]{1,0:T(8,128)}, ...) custom-call(s32[2]{0:T(128)} %pad_add_fusion.2.info, bf16[512,1536]{1,0:T(8,128)(2,1)} %collective-permute-done.21.refs_0_, ...), custom_call_target="tpu_custom_call" | custom-call | flops 9126805504 | bytes 20971520 | tf_op jit(solution)/shard_map/attention_forward/pallas_call | solution.py:187
  185.2 27.4 %attention_forward.2 = (bf16[1024,1536]{1,0:T(8,128)(2,1)}, bf16[1024,1024]{1,0:T(8,128)(2,1)}, bf16[1024,512]{1,0:T(8,128)(2,1)}, f32[1024,128]{1,0:T(8,128)}, ...) custom-call(s32[2]{0:T(128)} %pad_add_fusion.info, bf16[512,1536]{1,0:T(8,128)(2,1)} %refs_0_.1, ...), custom_call_target="tpu_custom_call" | custom-call | flops 9126805504 | bytes 20971520 | tf_op jit(solution)/shard_map/attention_forward/pallas_call | solution.py:187
  216.3 34.5 %collective-permute-done.24 = bf16[512,1536]{1,0:T(8,128)(2,1)S(1)} collective-permute-done((bf16[512,1536]{1,0:T(8,128)(2,1)S(1)}, bf16[512,1536]{1,0:T(8,128)(2,1)S(1)}, u32[]{:S(2)}, u32[]{:S(2)}) %collective-permute-start.24) | collective-permute-done | bytes 1572896 | tf_op jit(solution)/shard_map/ppermute | solution.py:441
  254.8 29.7 %collective-permute-done.30.refs_2_.refs_6_ = bf16[512,1536]{1,0:T(8,128)(2,1)S(1)} collective-permute-done((bf16[512,1536]{1,0:T(8,128)(2,1)}, bf16[512,1536]{1,0:T(8,128)(2,1)S(1)}, u32[]{:S(2)}, u32[]{:S(2)}) %collective-permute-start.30) | collective-permute-done | bytes 1572896 | tf_op jit(solution)/shard_map/ppermute | solution.py:441
  285.7 31.6 %collective-permute-done.28.refs_0_.refs_2_ = bf16[512,1536]{1,0:T(8,128)(2,1)S(1)} collective-permute-done((bf16[512,1536]{1,0:T(8,128)(2,1)}, bf16[512,1536]{1,0:T(8,128)(2,1)S(1)}, u32[]{:S(2)}, u32[]{:S(2)}) %collective-permute-start.28) | collective-permute-done | bytes 1572896 | tf_op jit(solution)/shard_map/ppermute | solution.py:441
  323.0 28.1 %feed_forward.3 = (bf16[1024,1024]{1,0:T(8,128)(2,1)}, bf16[1024,1024]{1,0:T(8,128)(2,1)}, bf16[1024,1024]{1,0:T(8,128)(2,1)}, bf16[512,1536]{1,0:T(8,128)(2,1)}...) custom-call(bf16[512,1536]{1,0:T(8,128)(2,1)} %copy-done.64, ...), custom_call_target="tpu_custom_call" | custom-call | flops 19327352832 | bytes 29360128 | tf_op jit(solution)/shard_map/feed_forward/pallas_call | solution.py:387
  351.1 28.3 %feed_forward.2 = (bf16[1024,1024]{1,0:T(8,128)(2,1)}, bf16[1024,1024]{1,0:T(8,128)(2,1)}, bf16[1024,1024]{1,0:T(8,128)(2,1)}, bf16[512,1536]{1,0:T(8,128)(2,1)}...) custom-call(bf16[512,1536]{1,0:T(8,128)(2,1)} %multiply_convert_fusion.refs_0_, ...), custom_call_target="tpu_custom_call" | custom-call | flops 19327352832 | bytes 29360128 | tf_op jit(solution)/shard_map/feed_forward/pallas_call | solution.py:387
  379.4 34.3 %feed_forward_weight_gradient.1 = bf16[3,1536,1024]{2,1,0:T(8,128)(2,1)} custom-call(bf16[512,1536]{1,0:T(8,128)(2,1)} %multiply_convert_fusion.refs_0_, bf16[512,1536]{1,0:T(8,128)(2,1)} %collective-permute-done.25.refs_1_, bf16[512,1536]{1,0:T(8,128)(2,1)} %copy-done.64, bf16[512,1536]{1,0:T(8,128)(2,1)} %collective-permute-done.29.refs_1_.refs_3_, ...), custom_call_target="tpu_custom_call" | custom-call | flops 19327352832 | bytes 35651584 | tf_op jit(solution)/shard_map/feed_forward_weight_gradient/pallas_call | solution.py:428
  422.0 34.7 %collective-permute-done.36 = bf16[512,1536]{1,0:T(8,128)(2,1)S(1)} collective-permute-done((bf16[512,1536]{1,0:T(8,128)(2,1)S(1)}, bf16[512,1536]{1,0:T(8,128)(2,1)S(1)}, u32[]{:S(2)}, u32[]{:S(2)}) %collective-permute-start.36) | collective-permute-done | bytes 1572896 | tf_op jit(solution)/shard_map/ppermute | solution.py:441
  458.0 31.6 %collective-permute-done.33 = bf16[512,1536]{1,0:T(8,128)(2,1)S(1)} collective-permute-done((bf16[512,1536]{1,0:T(8,128)(2,1)S(1)}, bf16[512,1536]{1,0:T(8,128)(2,1)S(1)}, u32[]{:S(2)}, u32[]{:S(2)}) %collective-permute-start.33) | collective-permute-done | bytes 1572896 | tf_op jit(solution)/shard_map/ppermute | solution.py:441
  489.6 5.2 fusion.82
  497.4 34.5 %collective-permute-done.39.refs_0_.refs_2_ = bf16[512,1536]{1,0:T(8,128)(2,1)} collective-permute-done((bf16[512,1536]{1,0:T(8,128)(2,1)S(1)}, bf16[512,1536]{1,0:T(8,128)(2,1)}, u32[]{:S(2)}, u32[]{:S(2)}) %collective-permute-start.39) | collective-permute-done | bytes 1572896 | tf_op jit(solution)/shard_map/ppermute | solution.py:441
  535.8 27.3 %attention_backward.3 = (bf16[1024,1024]{1,0:T(8,128)(2,1)}, bf16[512,1536]{1,0:T(8,128)(2,1)}, bf16[512,1536]{1,0:T(8,128)(2,1)}) custom-call(s32[2]{0:T(128)} %pad_add_fusion.2.info, bf16[512,1536]{1,0:T(8,128)(2,1)} %collective-permute-done.39.refs_0_.refs_2_, bf16[512,1536]{1,0:T(8,128)(2,1)} %collective-permute-done.40.refs_1_.refs_3_, ...), custom_call_target="tpu_custom_call" | custom-call | flops 15569256448 | bytes 20971520 | tf_op jit(solution)/shard_map/attention_backward/pallas_call | solution.py:282
  564.3 26.2 %attention_backward.2 = (bf16[1024,1024]{1,0:T(8,128)(2,1)}, bf16[512,1536]{1,0:T(8,128)(2,1)}, bf16[512,1536]{1,0:T(8,128)(2,1)}) custom-call(s32[2]{0:T(128)} %pad_add_fusion.info, bf16[512,1536]{1,0:T(8,128)(2,1)} %copy-done.31, bf16[512,1536]{1,0:T(8,128)(2,1)} %copy-done.67, bf16[1536,1024]{1,0:T(8,128)(2,1)} %assemble_weights.2.refs_3_.refs_2_, ...), custom_call_target="tpu_custom_call" | custom-call | flops 15569256448 | bytes 20971520 | tf_op jit(solution)/shard_map/attention_backward/pallas_call | solution.py:282
  591.0 10.4 %attention_weight_gradient.5 = (bf16[4,192,384]{2,1,0:T(8,128)(2,1)}, bf16[4,192,384]{2,1,0:T(8,128)(2,1)}) custom-call(s32[6]{0:T(128)} %concatenate.23.info, bf16[384,512]{1,0:T(8,128)(2,1)} %fusion.31.spread, bf16[512,1536]{1,0:T(8,128)(2,1)} %copy-done.31, bf16[512,1536]{1,0:T(8,128)(2,1)} %copy-done.67, ...), custom_call_target="tpu_custom_call" | custom-call | flops 3221225472 | bytes 12582912 | tf_op jit(solution)/shard_map/attention_weight_gradient/pallas_call | solution.py:339
  603.9 9.8 %attention_weight_gradient.3 = (bf16[4,192,384]{2,1,0:T(8,128)(2,1)}, bf16[4,192,384]{2,1,0:T(8,128)(2,1)}) custom-call(s32[2]{0:T(128)} %pad_add_fusion.1.info, bf16[384,512]{1,0:T(8,128)(2,1)} %fusion.31.spread, bf16[1024,1536]{1,0:T(8,128)(2,1)} %get-tuple-element.78.refs_0_, bf16[1024,1536]{1,0:T(8,128)(2,1)} %get-tuple-element.79.refs_1_, ...), custom_call_target="tpu_custom_call" | custom-call | flops 3221225472 | bytes 12582912 | tf_op jit(solution)/shard_map/attention_weight_gradient/pallas_call | solution.py:339
  616.6 9.6 %attention_weight_gradient.4 = (bf16[4,192,384]{2,1,0:T(8,128)(2,1)}, bf16[4,192,384]{2,1,0:T(8,128)(2,1)}) custom-call(s32[2]{0:T(128)} %pad_add_fusion.1.info, bf16[384,512]{1,0:T(8,128)(2,1)} %fusion.31.spread, bf16[1024,1536]{1,0:T(8,128)(2,1)} %get-tuple-element.78.refs_0_, bf16[1024,1536]{1,0:T(8,128)(2,1)} %get-tuple-element.79.refs_1_, ...), custom_call_target="tpu_custom_call" | custom-call | flops 3221225472 | bytes 12582912 | tf_op jit(solution)/shard_map/attention_weight_gradient/pallas_call | solution.py:339
  635.5 7.4 collective-permute-done.47
  647.5 4.0 collective-permute-done.42
  665.2 4.2 collective-permute-start.50
  676.7 5.0 collective-permute-start.58
  697.2 9.0 %stack.124 = f32[14]{0:T(128)S(1)} concatenate(f32[1]{0:T(128)} %bitcast.6, f32[1]{0:T(128)} %bitcast.7, f32[1]{0:T(128)} %bitcast.8, f32[1]{0:T(128)} %bitcast.9, f32[1]{0:T(128)} %bitcast.10, f32[1]{0:T(128)} %bitcast.11, f32[1]{0:T(128)} %bitcast.12, f32[1]{0:T(128)} %bitcast.21, f32[1]{0:T(128)} %bitcast.29, f32[1]{0:T(128)} %bitcast.34, f32[1]{0:T(128)} %bitcast.39, ...), dimensions={0} | concatenate | bytes 112 | tf_op jit(solution)/shard_map/stack | solution.py:705
  720.9 6.3 fusion.1
  (340 shorter events, 169.0 us)
Async XLA Ops:
  7.2 315.8 %all-gather.2.cloned.1.call-start = ((), (), s32[]{:S(2)}) async-start(), calls=%async_computation.1 | async-start | bytes 10616832 | tf_op jit(solution)/shard_map/all_gather | solution.py:581
  10.2 679.5 %reduce-scatter.2.cloned.1.call-start = ((), (), s32[]{:S(2)}) async-start(), calls=%async_computation.2 | async-start | bytes 10616832 | tf_op jit(solution)/shard_map/reduce_scatter | solution.py:602
  10.7 43.3 %collective-permute-start.21 = (bf16[512,1536]{1,0:T(8,128)(2,1)S(1)}, bf16[512,1536]{1,0:T(8,128)(2,1)}, u32[]{:S(2)}, u32[]{:S(2)}) collective-permute-start(bf16[512,1536]{1,0:T(8,128)(2,1)S(1)} %copy-done.3), channel_id=1, source_target_pairs={{0,2},{1,3},{2,0},{3,1},{4,6},{5,7},{6,4},{7,5},{8,10},{9,11},{10,... | collective-permute-start | bytes 4718600 | tf_op jit(solution)/shard_map/ppermute | solution.py:441
  15.3 33.1 %collective-permute-start.2 = (f32[2,1536]{1,0:T(2,128)S(1)}, f32[2,1536]{1,0:T(2,128)S(1)}, u32[]{:S(2)}, u32[]{:S(2)}) collective-permute-start(f32[2,1536]{1,0:T(2,128)S(1)} %add.351), channel_id=1, source_target_pairs={{0,2},{1,3},{2,0},{3,1},{4,6},{5,7},{6,4},{7,5},{8,10},{9,11},{10,... | collective-permute-start | bytes 36872 | tf_op jit(solution)/shard_map/ppermute | solution.py:441
  15.6 48.4 %collective-permute-start.13 = (bf16[192,384]{1,0:T(8,128)(2,1)S(1)}, bf16[192,384]{1,0:T(8,128)(2,1)S(1)}, u32[]{:S(2)}, u32[]{:S(2)}) collective-permute-start(bf16[192,384]{1,0:T(8,128)(2,1)S(1)} %convert_bitcast_fusion.1.refs_0_), channel_id=1, source_target_pairs={{0,8},{4,12},{8,16},{12,20},{16,24},{20,28},{24,0},{28,4},{1,9},{5... | collective-permute-start | bytes 442376 | tf_op jit(solution)/shard_map/ppermute | solution.py:445
  17.7 48.4 %collective-permute-start.14 = (bf16[192,384]{1,0:T(8,128)(2,1)S(1)}, bf16[192,384]{1,0:T(8,128)(2,1)S(1)}, u32[]{:S(2)}, u32[]{:S(2)}) collective-permute-start(bf16[192,384]{1,0:T(8,128)(2,1)S(1)} %convert_bitcast_fusion.1.refs_0_), channel_id=1, source_target_pairs={{0,16},{4,20},{8,24},{12,28},{16,0},{20,4},{24,8},{28,12},{1,17},{... | collective-permute-start | bytes 442376 | tf_op jit(solution)/shard_map/ppermute | solution.py:445
  20.3 64.3 %collective-permute-start.6 = (bf16[192,768]{1,0:T(8,128)(2,1)S(1)}, bf16[192,768]{1,0:T(8,128)(2,1)S(1)}, u32[]{:S(2)}, u32[]{:S(2)}) collective-permute-start(bf16[192,768]{1,0:T(8,128)(2,1)S(1)} %convert_element_type.201.refs_0_), channel_id=1, source_target_pairs={{0,8},{4,12},{8,16},{12,20},{16,24},{20,28},{24,0},{28,4},{1,9},{5... | collective-permute-start | bytes 884744 | tf_op jit(solution)/shard_map/ppermute | solution.py:445
  54.0 101.6 %collective-permute-start.22 = (bf16[512,1536]{1,0:T(8,128)(2,1)}, bf16[512,1536]{1,0:T(8,128)(2,1)}, u32[]{:S(2)}, u32[]{:S(2)}) collective-permute-start(bf16[512,1536]{1,0:T(8,128)(2,1)} %collective-permute-done.21.refs_0_), channel_id=1, source_target_pairs={{0,1},{1,0},{2,3},{3,2},{4,5},{5,4},{6,7},{7,6},{8,9},{9,8},{10,11... | collective-permute-start | bytes 4718600 | tf_op jit(solution)/shard_map/ppermute | solution.py:441
  61.3 26.0 %collective-permute-start.7 = (bf16[192,768]{1,0:T(8,128)(2,1)S(1)}, bf16[192,768]{1,0:T(8,128)(2,1)S(1)}, u32[]{:S(2)}, u32[]{:S(2)}) collective-permute-start(bf16[192,768]{1,0:T(8,128)(2,1)S(1)} %convert_element_type.201.refs_0_), channel_id=1, source_target_pairs={{0,16},{4,20},{8,24},{12,28},{16,0},{20,4},{24,8},{28,12},{1,17},{... | collective-permute-start | bytes 884744 | tf_op jit(solution)/shard_map/ppermute | solution.py:445
  78.7 20.0 %collective-permute-start.8 = (bf16[192,768]{1,0:T(8,128)(2,1)S(1)}, bf16[192,768]{1,0:T(8,128)(2,1)S(1)}, u32[]{:S(2)}, u32[]{:S(2)}) collective-permute-start(bf16[192,768]{1,0:T(8,128)(2,1)S(1)} %convert_element_type.201.refs_0_), channel_id=1, source_target_pairs={{0,24},{4,28},{8,0},{12,4},{16,8},{20,12},{24,16},{28,20},{1,25},{... | collective-permute-start | bytes 884744 | tf_op jit(solution)/shard_map/ppermute | solution.py:445
  100.0 26.0 %collective-permute-start.10 = (bf16[192,768]{1,0:T(8,128)(2,1)S(1)}, bf16[192,768]{1,0:T(8,128)(2,1)S(1)}, u32[]{:S(2)}, u32[]{:S(2)}) collective-permute-start(bf16[192,768]{1,0:T(8,128)(2,1)S(1)} %collective-permute-done.6.refs_1_), channel_id=1, source_target_pairs={{0,4},{4,0},{8,12},{12,8},{16,20},{20,16},{24,28},{28,24},{1,5},{5... | collective-permute-start | bytes 884744 | tf_op jit(solution)/shard_map/ppermute | solution.py:441
  100.7 38.0 %collective-permute-start.11 = (bf16[192,768]{1,0:T(8,128)(2,1)S(1)}, bf16[192,768]{1,0:T(8,128)(2,1)S(1)}, u32[]{:S(2)}, u32[]{:S(2)}) collective-permute-start(bf16[192,768]{1,0:T(8,128)(2,1)S(1)} %collective-permute-done.7.refs_2_), channel_id=1, source_target_pairs={{0,4},{4,0},{8,12},{12,8},{16,20},{20,16},{24,28},{28,24},{1,5},{5... | collective-permute-start | bytes 884744 | tf_op jit(solution)/shard_map/ppermute | solution.py:441
  102.1 47.6 %collective-permute-start.12 = (bf16[192,768]{1,0:T(8,128)(2,1)S(1)}, bf16[192,768]{1,0:T(8,128)(2,1)S(1)}, u32[]{:S(2)}, u32[]{:S(2)}) collective-permute-start(bf16[192,768]{1,0:T(8,128)(2,1)S(1)} %collective-permute-done.8.refs_3_), channel_id=1, source_target_pairs={{0,4},{4,0},{8,12},{12,8},{16,20},{20,16},{24,28},{28,24},{1,5},{5... | collective-permute-start | bytes 884744 | tf_op jit(solution)/shard_map/ppermute | solution.py:441
  113.4 70.6 %collective-permute-start = (bf16[512,1536]{1,0:T(8,128)(2,1)S(1)}, bf16[512,1536]{1,0:T(8,128)(2,1)S(1)}, u32[]{:S(2)}, u32[]{:S(2)}) collective-permute-start(bf16[512,1536]{1,0:T(8,128)(2,1)S(1)} %copy-done.3), channel_id=1, source_target_pairs={{0,1},{1,0},{2,3},{3,2},{4,5},{5,4},{6,7},{7,6},{8,9},{9,8},{10,11... | collective-permute-start | bytes 4718600 | tf_op jit(solution)/shard_map/ppermute | solution.py:441
  182.8 30.3 %collective-permute-start.23 = (bf16[512,1536]{1,0:T(8,128)(2,1)}, bf16[512,1536]{1,0:T(8,128)(2,1)S(1)}, u32[]{:S(2)}, u32[]{:S(2)}) collective-permute-start(bf16[512,1536]{1,0:T(8,128)(2,1)} %get-tuple-element.61), channel_id=1, source_target_pairs={{0,1},{1,0},{2,3},{3,2},{4,5},{5,4},{6,7},{7,6},{8,9},{9,8},{10,11... | collective-permute-start | bytes 4718600 | tf_op jit(solution)/shard_map/ppermute | solution.py:441
  213.5 37.3 %collective-permute-start.24 = (bf16[512,1536]{1,0:T(8,128)(2,1)S(1)}, bf16[512,1536]{1,0:T(8,128)(2,1)S(1)}, u32[]{:S(2)}, u32[]{:S(2)}) collective-permute-start(bf16[512,1536]{1,0:T(8,128)(2,1)S(1)} %add_convert_fusion.7), channel_id=1, source_target_pairs={{0,2},{1,3},{2,0},{3,1},{4,6},{5,7},{6,4},{7,5},{8,10},{9,11},{10,... | collective-permute-start | bytes 4718600 | tf_op jit(solution)/shard_map/ppermute | solution.py:441
  214.9 69.6 %collective-permute-start.30 = (bf16[512,1536]{1,0:T(8,128)(2,1)}, bf16[512,1536]{1,0:T(8,128)(2,1)S(1)}, u32[]{:S(2)}, u32[]{:S(2)}) collective-permute-start(bf16[512,1536]{1,0:T(8,128)(2,1)} %refs_4_.1), channel_id=1, source_target_pairs={{0,2},{1,3},{2,0},{3,1},{4,6},{5,7},{6,4},{7,5},{8,10},{9,11},{10,... | collective-permute-start | bytes 4718600 | tf_op jit(solution)/shard_map/ppermute | solution.py:441
  253.5 63.8 %collective-permute-start.28 = (bf16[512,1536]{1,0:T(8,128)(2,1)}, bf16[512,1536]{1,0:T(8,128)(2,1)S(1)}, u32[]{:S(2)}, u32[]{:S(2)}) collective-permute-start(bf16[512,1536]{1,0:T(8,128)(2,1)} %multiply_convert_fusion.refs_0_), channel_id=1, source_target_pairs={{0,2},{1,3},{2,0},{3,1},{4,6},{5,7},{6,4},{7,5},{8,10},{9,11},{10,... | collective-permute-start | bytes 4718600 | tf_op jit(solution)/shard_map/ppermute | solution.py:441
  285.6 32.2 %collective-permute-start.31 = (bf16[512,1536]{1,0:T(8,128)(2,1)S(1)}, bf16[512,1536]{1,0:T(8,128)(2,1)S(1)}, u32[]{:S(2)}, u32[]{:S(2)}) collective-permute-start(bf16[512,1536]{1,0:T(8,128)(2,1)S(1)} %collective-permute-done.30.refs_2_.refs_6_), channel_id=1, source_target_pairs={{0,1},{1,0},{2,3},{3,2},{4,5},{5,4},{6,7},{7,6},{8,9},{9,8},{10,11... | collective-permute-start | bytes 4718600 | tf_op jit(solution)/shard_map/ppermute | solution.py:441
  317.3 33.9 %collective-permute-start.26 = (bf16[512,1536]{1,0:T(8,128)(2,1)}, bf16[512,1536]{1,0:T(8,128)(2,1)}, u32[]{:S(2)}, u32[]{:S(2)}) collective-permute-start(bf16[512,1536]{1,0:T(8,128)(2,1)} %refs_4_.1), channel_id=1, source_target_pairs={{0,1},{1,0},{2,3},{3,2},{4,5},{5,4},{6,7},{7,6},{8,9},{9,8},{10,11... | collective-permute-start | bytes 4718600 | tf_op jit(solution)/shard_map/ppermute | solution.py:441
  317.8 33.3 %collective-permute-start.25 = (bf16[512,1536]{1,0:T(8,128)(2,1)}, bf16[512,1536]{1,0:T(8,128)(2,1)}, u32[]{:S(2)}, u32[]{:S(2)}) collective-permute-start(bf16[512,1536]{1,0:T(8,128)(2,1)} %multiply_convert_fusion.refs_0_), channel_id=1, source_target_pairs={{0,1},{1,0},{2,3},{3,2},{4,5},{5,4},{6,7},{7,6},{8,9},{9,8},{10,11... | collective-permute-start | bytes 4718600 | tf_op jit(solution)/shard_map/ppermute | solution.py:441
  419.4 37.3 %collective-permute-start.36 = (bf16[512,1536]{1,0:T(8,128)(2,1)S(1)}, bf16[512,1536]{1,0:T(8,128)(2,1)S(1)}, u32[]{:S(2)}, u32[]{:S(2)}) collective-permute-start(bf16[512,1536]{1,0:T(8,128)(2,1)S(1)} %add_convert_fusion.2), channel_id=1, source_target_pairs={{0,2},{1,3},{2,0},{3,1},{4,6},{5,7},{6,4},{7,5},{8,10},{9,11},{10,... | collective-permute-start | bytes 4718600 | tf_op jit(solution)/shard_map/ppermute | solution.py:441
  420.8 37.2 %collective-permute-start.27 = (bf16[512,1536]{1,0:T(8,128)(2,1)S(1)}, bf16[512,1536]{1,0:T(8,128)(2,1)S(1)}, u32[]{:S(2)}, u32[]{:S(2)}) collective-permute-start(bf16[512,1536]{1,0:T(8,128)(2,1)S(1)} %copy-done.62), channel_id=1, source_target_pairs={{0,1},{1,0},{2,3},{3,2},{4,5},{5,4},{6,7},{7,6},{8,9},{9,8},{10,11... | collective-permute-start | bytes 4718600 | tf_op jit(solution)/shard_map/ppermute | solution.py:441
  421.2 68.4 %collective-permute-start.33 = (bf16[512,1536]{1,0:T(8,128)(2,1)S(1)}, bf16[512,1536]{1,0:T(8,128)(2,1)S(1)}, u32[]{:S(2)}, u32[]{:S(2)}) collective-permute-start(bf16[512,1536]{1,0:T(8,128)(2,1)S(1)} %add_convert_fusion.5), channel_id=1, source_target_pairs={{0,2},{1,3},{2,0},{3,1},{4,6},{5,7},{6,4},{7,5},{8,10},{9,11},{10,... | collective-permute-start | bytes 4718600 | tf_op jit(solution)/shard_map/ppermute | solution.py:441
  496.0 35.8 %collective-permute-start.39 = (bf16[512,1536]{1,0:T(8,128)(2,1)S(1)}, bf16[512,1536]{1,0:T(8,128)(2,1)}, u32[]{:S(2)}, u32[]{:S(2)}) collective-permute-start(bf16[512,1536]{1,0:T(8,128)(2,1)S(1)} %get-tuple-element.134.refs_0_), channel_id=1, source_target_pairs={{0,2},{1,3},{2,0},{3,1},{4,6},{5,7},{6,4},{7,5},{8,10},{9,11},{10,... | collective-permute-start | bytes 4718600 | tf_op jit(solution)/shard_map/ppermute | solution.py:441
  535.3 27.9 %collective-permute-start.37 = (bf16[512,1536]{1,0:T(8,128)(2,1)S(1)}, bf16[512,1536]{1,0:T(8,128)(2,1)S(1)}, u32[]{:S(2)}, u32[]{:S(2)}) collective-permute-start(bf16[512,1536]{1,0:T(8,128)(2,1)S(1)} %copy-done.32), channel_id=1, source_target_pairs={{0,1},{1,0},{2,3},{3,2},{4,5},{5,4},{6,7},{7,6},{8,9},{9,8},{10,11... | collective-permute-start | bytes 4718600 | tf_op jit(solution)/shard_map/ppermute | solution.py:441
  563.1 50.5 %collective-permute-start.41 = (bf16[512,1536]{1,0:T(8,128)(2,1)}, bf16[512,1536]{1,0:T(8,128)(2,1)S(1)}, u32[]{:S(2)}, u32[]{:S(2)}) collective-permute-start(bf16[512,1536]{1,0:T(8,128)(2,1)} %get-tuple-element.77), channel_id=1, source_target_pairs={{0,1},{1,0},{2,3},{3,2},{4,5},{5,4},{6,7},{7,6},{8,9},{9,8},{10,11... | collective-permute-start | bytes 4718600 | tf_op jit(solution)/shard_map/ppermute | solution.py:441
  590.5 55.7 %collective-permute-start.38 = (bf16[512,1536]{1,0:T(8,128)(2,1)}, bf16[512,1536]{1,0:T(8,128)(2,1)S(1)}, u32[]{:S(2)}, u32[]{:S(2)}) collective-permute-start(bf16[512,1536]{1,0:T(8,128)(2,1)} %get-tuple-element.73), channel_id=1, source_target_pairs={{0,1},{1,0},{2,3},{3,2},{4,5},{5,4},{6,7},{7,6},{8,9},{9,8},{10,11... | collective-permute-start | bytes 4718600 | tf_op jit(solution)/shard_map/ppermute | solution.py:441
  601.4 26.8 %collective-permute-start.51 = (bf16[4,192,384]{2,1,0:T(8,128)(2,1)}, bf16[4,192,384]{2,1,0:T(8,128)(2,1)S(1)}, u32[]{:S(2)}, u32[]{:S(2)}) collective-permute-start(bf16[4,192,384]{2,1,0:T(8,128)(2,1)} %get-tuple-element.89), channel_id=1, source_target_pairs={{0,4},{4,0},{8,12},{12,8},{16,20},{20,16},{24,28},{28,24},{1,5},{5... | collective-permute-start | bytes 1769480 | tf_op jit(solution)/shard_map/ppermute | solution.py:441
  615.2 36.3 %collective-permute-start.42 = (bf16[512,1536]{1,0:T(8,128)(2,1)}, bf16[512,1536]{1,0:T(8,128)(2,1)S(1)}, u32[]{:S(2)}, u32[]{:S(2)}) collective-permute-start(bf16[512,1536]{1,0:T(8,128)(2,1)} %add_convert_fusion), channel_id=1, source_target_pairs={{0,2},{1,3},{2,0},{3,1},{4,6},{5,7},{6,4},{7,5},{8,10},{9,11},{10,... | collective-permute-start | bytes 4718600 | tf_op jit(solution)/shard_map/ppermute | solution.py:441
  628.4 58.8 %collective-permute-start.52 = (bf16[192,384]{1,0:T(8,128)(2,1)S(1)}, bf16[192,384]{1,0:T(8,128)(2,1)S(1)}, u32[]{:S(2)}, u32[]{:S(2)}) collective-permute-start(bf16[192,384]{1,0:T(8,128)(2,1)S(1)} %get-tuple-element.149), channel_id=1, source_target_pairs={{0,8},{4,12},{8,16},{12,20},{16,24},{20,28},{24,0},{28,4},{1,9},{5... | collective-permute-start | bytes 442376 | tf_op jit(solution)/shard_map/ppermute | solution.py:445
  631.7 55.5 %collective-permute-start.53 = (bf16[192,384]{1,0:T(8,128)(2,1)S(1)}, bf16[192,384]{1,0:T(8,128)(2,1)S(1)}, u32[]{:S(2)}, u32[]{:S(2)}) collective-permute-start(bf16[192,384]{1,0:T(8,128)(2,1)S(1)} %get-tuple-element.151), channel_id=1, source_target_pairs={{0,16},{4,20},{8,24},{12,28},{16,0},{20,4},{24,8},{28,12},{1,17},{... | collective-permute-start | bytes 442376 | tf_op jit(solution)/shard_map/ppermute | solution.py:445
  (103 other events, 1272.3 us)
Sparse Core Ops, SparseCore 0:
  10.3 196.8 all-gather.1
  413.9 167.4 reduce-scatter.1

commit v2 on v1

--- a/solution.py
+++ b/solution.py
@@ -34,6 +34,8 @@
 BF16 = jnp.bfloat16
 VM = pl.BlockSpec(memory_space=pltpu.VMEM)
 SM = pl.BlockSpec(memory_space=pltpu.SMEM)
+ANY = pl.BlockSpec(memory_space=pl.ANY)
+MESH = pl.DeviceIdType.MESH
 
 
 def dot_nn(a, b):
@@ -48,12 +50,79 @@
     return lax.dot_general(a, b, (((0,), (0,)), ((), ())), preferred_element_type=F32)
 
 
-def params():
-    return pltpu.CompilerParams(vmem_limit_bytes=VMEM_LIMIT)
-
-
 def cost(flops, moved):
     return pl.CostEstimate(flops=int(flops), bytes_accessed=int(moved), transcendentals=0)
+
+
+def permuted(axis, bit):
+    return {axis: lax.axis_index(axis) ^ bit}
+
+
+def carrying_kernel(body, counts, sends, meets, *refs):
+    n_in, n_deps, n_out, n_scratch = counts
+    n_sends = len(sends)
+    refs = list(refs)
+
+    def take(n):
+        taken = refs[:n]
+        del refs[:n]
+        return taken
+
+    inputs, sources, _, outputs, targets = (
+        take(n_in),
+        take(n_sends),
+        take(n_deps),
+        take(n_out),
+        take(n_sends),
+    )
+    scratch = take(n_scratch)
+    copies = []
+    if sends:
+        send_sem, recv_sem = refs
+        barrier = pltpu.get_barrier_semaphore()
+        peers = sorted(set(sends) | set(meets))
+        for peer in peers:
+            pl.semaphore_signal(barrier, inc=1, device_id=permuted(*peer), device_id_type=MESH)
+        pl.semaphore_wait(barrier, len(peers))
+        for i, peer in enumerate(sends):
+            copy = pltpu.make_async_remote_copy(
+                src_ref=sources[i],
+                dst_ref=targets[i],
+                send_sem=send_sem.at[i],
+                recv_sem=recv_sem.at[i],
+                device_id=permuted(*peer),
+                device_id_type=MESH,
+            )
+            copy.start()
+            copies.append(copy)
+    body(*inputs, *outputs, *scratch)
+    for copy in copies:
+        copy.wait()
+
+
+def call(body, name, inputs, outs, flops, scratch=(), sends=(), deps=(), meets=(), collective_id=None, specs=None):
+    n_sends = len(sends)
+    specs = [VM] * len(inputs) if specs is None else specs
+    arrays = [array for array, _ in sends]
+    dma = pltpu.SemaphoreType.DMA
+    moved = sum(a.size * a.dtype.itemsize for a in list(inputs) + list(outs))
+    extra = dict(collective_id=collective_id, has_side_effects=True) if sends else {}
+    return pl.pallas_call(
+        functools.partial(
+            carrying_kernel,
+            body,
+            (len(inputs), len(deps), len(outs), len(scratch)),
+            [peer for _, peer in sends],
+            meets,
+        ),
+        out_shape=list(outs) + [jax.ShapeDtypeStruct(a.shape, a.dtype) for a in arrays],
+        in_specs=specs + [ANY] * (n_sends + len(deps)),
+        out_specs=[VM] * len(outs) + [ANY] * n_sends,
+        scratch_shapes=list(scratch) + ([dma((n_sends,)), dma((n_sends,))] if sends else []),
+        compiler_params=pltpu.CompilerParams(vmem_limit_bytes=VMEM_LIMIT, **extra),
+        cost_estimate=cost(flops, moved),
+        name=name,
+    )(*inputs, *arrays, *deps)
 
 
 def spread_matrix():
@@ -62,35 +131,18 @@
     return ((target // PAD) * HEAD + target % PAD == source) & (target % PAD < HEAD)
 
 
-def assemble_kernel(n_z, blk, info, spread, *refs):
-    n_blocks = 2 * n_z
-    blocks, out, rows = refs[:n_blocks], refs[n_blocks], refs[n_blocks + 1]
-    z, x = info[0], info[1]
-    for j in range(2):
-        for k in range(n_z):
-            source = (lax.rem(z + n_z - k, n_z)) * 2 + (x ^ j)
-            rows[pl.ds(pl.multiple_of(source * blk, 16), blk), :] = blocks[j * n_z + k][...]
-    groups = out.shape[1] // G_PAD
-    for g in range(groups):
-        out[:, g * G_PAD : (g + 1) * G_PAD] = dot_nn(
-            rows[:, g * G_COLS : (g + 1) * G_COLS], spread[...]
-        ).astype(BF16)
-
-
-def assemble(blocks, info, spread, n_z):
-    blk, cols = blocks[0].shape
-    depth = blk * len(blocks)
-    wide = cols // G_COLS * G_PAD
-    return pl.pallas_call(
-        functools.partial(assemble_kernel, n_z, blk),
-        out_shape=jax.ShapeDtypeStruct((depth, wide), BF16),
-        in_specs=[SM, VM] + [VM] * len(blocks),
-        out_specs=VM,
-        scratch_shapes=[pltpu.VMEM((depth, cols), BF16)],
-        compiler_params=params(),
-        cost_estimate=cost(2 * depth * cols * G_PAD, 4 * depth * cols),
-        name="assemble_weights",
-    )(info, spread, *blocks)
+def pad_kernel(spread, wq, wo, wq_pad, wo_pad):
+    for source, target in ((wq, wq_pad), (wo, wo_pad)):
+        for g in range(target.shape[1] // G_PAD):
+            target[:, g * G_PAD : (g + 1) * G_PAD] = dot_nn(
+                source[:, g * G_COLS : (g + 1) * G_COLS], spread[...]
+            ).astype(BF16)
+
+
+def pad_weights(wq, wo, spread):
+    depth = wq.shape[0]
+    outs = [jax.ShapeDtypeStruct((depth, w.shape[1] // G_COLS * G_PAD), BF16) for w in (wq, wo)]
+    return call(pad_kernel, "pad_weights", [spread, wq, wo], outs, 6 * depth * G_COLS * G_PAD)
 
 
 def swap_halves(values):
@@ -117,7 +169,7 @@
     gain, w_qkv, w_out, cos_t, sin_t = refs[nb : nb + 5]
     normed, qkvp, att, lse = refs[nb + 5 : nb + 9]
     parts = refs[nb + 9 : nb + 9 + nb]
-    length, local = info[0], info[1]
+    length, local = info[0], lax.rem(lax.axis_index("tensor"), nb)
     seq_len = nb * rows_each
     chunk = 32
     for r in range(nb):
@@ -177,28 +229,27 @@
         store_relative(parts, rows_each, i * Q_ROWS, local, part)
 
 
-def attn_fwd(xs, info, gain, w_qkv, w_out, cos_t, sin_t):
+def attn_fwd(xs, info, gain, w_qkv, w_out, cos_t, sin_t, **more):
     nb = len(xs)
     rows_each, width = xs[0].shape
     seq_len = nb * rows_each
     kv = w_qkv.shape[1] // G_PAD
     heads = kv * GROUP
-    flops = 2 * seq_len * width * (kv * G_PAD + heads * PAD) + heads * seq_len * seq_len * 4 * 256
-    return pl.pallas_call(
+    outs = [
+        jax.ShapeDtypeStruct((seq_len, width), BF16),
+        jax.ShapeDtypeStruct((seq_len, kv * G_PAD), BF16),
+        jax.ShapeDtypeStruct((seq_len, heads * PAD), BF16),
+        jax.ShapeDtypeStruct((seq_len, PAD), F32),
+    ] + [jax.ShapeDtypeStruct((rows_each, width), BF16)] * nb
+    return call(
         functools.partial(attn_fwd_kernel, nb, rows_each, kv),
-        out_shape=[
-            jax.ShapeDtypeStruct((seq_len, width), BF16),
-            jax.ShapeDtypeStruct((seq_len, kv * G_PAD), BF16),
-            jax.ShapeDtypeStruct((seq_len, heads * PAD), BF16),
-            jax.ShapeDtypeStruct((seq_len, PAD), F32),
-        ]
-        + [jax.ShapeDtypeStruct((rows_each, width), BF16)] * nb,
-        in_specs=[SM] + [VM] * (nb + 5),
-        out_specs=[VM] * (4 + nb),
-        compiler_params=params(),
-        cost_estimate=cost(flops, 20 << 20),
-        name="attention_forward",
-    )(info, *xs, gain, w_qkv, w_out, cos_t, sin_t)
+        "attention_forward",
+        [info, *xs, gain, w_qkv, w_out, cos_t, sin_t],
+        outs,
+        2 * seq_len * width * (kv * G_PAD + heads * PAD) + heads * seq_len * seq_len * 4 * 256,
+        specs=[SM] + [VM] * (nb + 5),
+        **more,
+    )
 
 
 def attn_bwd_kernel(nb, rows_each, kv, info, *refs):
@@ -207,7 +258,7 @@
     dproj = refs[nb + 6]
     parts = refs[nb + 7 : nb + 7 + nb]
     datt, dk_acc, dv_acc = refs[nb + 7 + nb :]
-    length, local = info[0], info[1]
+    length, local = info[0], lax.rem(lax.axis_index("tensor"), nb)
     seq_len = nb * rows_each
     heads = kv * GROUP
     for r in range(nb):
@@ -272,80 +323,155 @@
         store_relative(parts, rows_each, i * Q_ROWS, local, part)
 
 
-def attn_bwd(ags, info, w_qkv, w_out, qkvp, lse, cos_t, sin_t):
+def attn_bwd(ags, info, w_qkv, w_out, qkvp, lse, cos_t, sin_t, **more):
     nb = len(ags)
     rows_each, width = ags[0].shape
     seq_len = nb * rows_each
     kv = w_qkv.shape[1] // G_PAD
     heads = kv * GROUP
-    flops = 2 * seq_len * width * (kv * G_PAD + heads * PAD) + heads * seq_len * seq_len * 10 * 256
-    return pl.pallas_call(
+    outs = [jax.ShapeDtypeStruct((seq_len, kv * G_PAD), BF16)] + [
+        jax.ShapeDtypeStruct((rows_each, width), BF16)
+    ] * nb
+    return call(
         functools.partial(attn_bwd_kernel, nb, rows_each, kv),
-        out_shape=[jax.ShapeDtypeStruct((seq_len, kv * G_PAD), BF16)]
-        + [jax.ShapeDtypeStruct((rows_each, width), BF16)] * nb,
-        in_specs=[SM] + [VM] * (nb + 6),
-        out_specs=[VM] * (1 + nb),
-        scratch_shapes=[
+        "attention_backward",
+        [info, *ags, w_qkv, w_out, qkvp, lse, cos_t, sin_t],
+        outs,
+        2 * seq_len * width * (kv * G_PAD + heads * PAD) + heads * seq_len * seq_len * 10 * 256,
+        scratch=[
             pltpu.VMEM((seq_len, heads * PAD), BF16),
             pltpu.VMEM((seq_len, PAD), F32),
             pltpu.VMEM((seq_len, PAD), F32),
         ],
-        compiler_params=params(),
-        cost_estimate=cost(flops, 20 << 20),
-        name="attention_backward",
-    )(info, *ags, w_qkv, w_out, qkvp, lse, cos_t, sin_t)
-
-
-def weight_grad_kernel(n_z, blk, n_pairs, row_counts, info, spread, *refs):
-    lefts, rights = refs[:n_pairs], refs[n_pairs : 2 * n_pairs]
-    same, other = refs[2 * n_pairs :]
-    z, x = info[0], info[1]
-    width = lefts[0].shape[1]
-    for c in range(width // G_COLS):
-        cols = slice(c * G_COLS, (c + 1) * G_COLS)
-        total = None
-        for p in range(n_pairs):
-            if row_counts is None:
-                right = rights[p][...]
+        specs=[SM] + [VM] * (nb + 6),
+        **more,
+    )
+
+
+def weight_grad_kernel(n_z, blk, nb, kv, spread, *refs):
+    ags, refs = refs[: 2 * nb], refs[2 * nb :]
+    atts, normeds, dprojs, refs = refs[:2], refs[2:4], refs[4:6], refs[6:]
+    sames, others, arrived, send_sem, recv_sem = refs[0], refs[1], refs[2], refs[3], refs[4]
+    d, t = lax.axis_index("dp"), lax.axis_index("tensor")
+    z, x = d // 2, lax.rem(d, 2)
+    local = lax.rem(t, nb)
+    rows_each, width = ags[0].shape
+    copies = []
+    for which in range(kv + 1):
+
+        def chunk(c, carry):
+            cols = pl.ds(pl.multiple_of(c * G_COLS, G_COLS), G_COLS)
+            if which == 0:
+                wide = atts[0].shape[1]
+                total = jnp.zeros((G_COLS, wide), F32)
+                for r in range(2 * nb):
+                    start = pl.multiple_of((local ^ (r % nb)) * rows_each, rows_each)
+                    total += dot_tn(ags[r][:, cols], atts[r // nb][pl.ds(start, rows_each), :])
+                compact = dot_nt(total.astype(BF16), spread[:, :wide])
             else:
-                start = pl.multiple_of(info[2 + p], 16)
-                right = rights[p][pl.ds(start, lefts[p].shape[0]), :]
-            term = dot_tn(lefts[p][:, cols], right)
-            total = term if total is None else total + term
-        compact = dot_nt(total.astype(BF16), spread[...]).astype(BF16)
-        for b in range(G_COLS // blk):
-            owner = c * (G_COLS // blk) + b
-            shift = lax.rem(owner // 2 + n_z - z, n_z)
-            value = compact[b * blk : (b + 1) * blk, :]
-
-            @pl.when(x == owner % 2)
-            def _():
-                same[shift, :, :] = value
-
-            @pl.when(x != owner % 2)
-            def _():
-                other[shift, :, :] = value
-
-
-def weight_grad(lefts, rights, info, spread, n_z, blk, right_cols, offsets):
-    n_pairs = len(lefts)
-    rows, width = lefts[0].shape
-    out = jax.ShapeDtypeStruct((n_z, blk, G_COLS), BF16)
-    right_specs = [
-        pl.BlockSpec((right.shape[0], G_PAD), functools.partial(lambda c, i: (0, c), right_cols))
-        for right in rights
-    ]
-    full = lambda a: pl.BlockSpec(a.shape, lambda i: (0,) * a.ndim)
+                part = slice((which - 1) * G_PAD, which * G_PAD)
+                total = dot_tn(normeds[0][:, cols], dprojs[0][:, part])
+                total += dot_tn(normeds[1][:, cols], dprojs[1][:, part])
+                compact = dot_nt(total.astype(BF16), spread[...])
+            compact = compact.astype(BF16)
+            for b in range(G_COLS // blk):
+                owner = c * (G_COLS // blk) + b
+                shift = lax.rem(owner // 2 + n_z - z, n_z)
+                value = compact[b * blk : (b + 1) * blk, :]
+
+                @pl.when(x == lax.rem(owner, 2))
+                def _():
+                    sames[which, shift, :, :] = value
+
+                @pl.when(x != lax.rem(owner, 2))
+                def _():
+                    others[which, shift, :, :] = value
+
+            return carry
+
+        lax.fori_loop(0, width // G_COLS, chunk, 0)
+        copy = pltpu.make_async_remote_copy(
+            src_ref=others.at[which],
+            dst_ref=arrived.at[which],
+            send_sem=send_sem.at[which],
+            recv_sem=recv_sem.at[which],
+            device_id=permuted("dp", 1),
+            device_id_type=MESH,
+        )
+        copy.start()
+        copies.append(copy)
+    for copy in copies:
+        copy.wait()
+
+
+def weight_grad(ags, atts, normeds, dprojs, spread, n_z, blk, **more):
+    nb = len(ags) // 2
+    rows, width = ags[0].shape
+    kv = dprojs[0].shape[1] // G_PAD
+    out = jax.ShapeDtypeStruct((kv + 1, n_z, blk, G_COLS), BF16)
+    return call(
+        functools.partial(weight_grad_kernel, n_z, blk, nb, kv),
+        "attention_weight_gradients",
+        [spread, *ags, *atts, *normeds, *dprojs],
+        [out, out, out],
+        4 * nb * rows * width * G_PAD * (kv + 1),
+        scratch=[pltpu.SemaphoreType.DMA((kv + 1,)), pltpu.SemaphoreType.DMA((kv + 1,))],
+        **more,
+    )
+
+
+def z_sum_kernel(n_z, same, other, out, narrow, arrived, send_sem, recv_sem):
+    d = lax.axis_index("dp")
+    z, x = d // 2, lax.rem(d, 2)
+    barrier = pltpu.get_barrier_semaphore()
+    peers = [{"dp": lax.rem(z + k, n_z) * 2 + x} for k in range(1, n_z)]
+    for peer in peers:
+        pl.semaphore_signal(barrier, inc=1, device_id=peer, device_id_type=MESH)
+    pl.semaphore_wait(barrier, n_z - 1)
+    copies = []
+    n_which = same.shape[0]
+    for which in range(n_which):
+        for k in range(1, n_z):
+            held = same[which, k, :, :].astype(F32) + other[which, k, :, :].astype(F32)
+            narrow[which, k, :, :] = held.astype(BF16)
+            copy = pltpu.make_async_remote_copy(
+                src_ref=narrow.at[which, k],
+                dst_ref=arrived.at[which, k],
+                send_sem=send_sem.at[which, k],
+                recv_sem=recv_sem.at[which, k],
+                device_id=peers[k - 1],
+                device_id_type=MESH,
+            )
+            copy.start()
+            copies.append(copy)
+    for which in range(n_which):
+        total = same[which, 0, :, :].astype(F32) + other[which, 0, :, :].astype(F32)
+        for k in range(1, n_z):
+            copies[which * (n_z - 1) + k - 1].wait()
+            total = total + arrived[which, k, :, :].astype(F32)
+        out[which, :, :] = total
+
+
+def z_sum(same, other, n_z, collective_id, deps=()):
+    n_which, _, blk, cols = same.shape
+    dma = pltpu.SemaphoreType.DMA
     return pl.pallas_call(
-        functools.partial(weight_grad_kernel, n_z, blk, n_pairs, offsets),
-        grid=(1,),
-        out_shape=[out, out],
-        in_specs=[SM, full(spread)] + [full(left) for left in lefts] + right_specs,
-        out_specs=[pl.BlockSpec(out.shape, lambda i: (0, 0, 0))] * 2,
-        compiler_params=params(),
-        cost_estimate=cost(2 * n_pairs * rows * width * G_PAD, 12 << 20),
-        name="attention_weight_gradient",
-    )(info, spread, *lefts, *rights)
+        lambda a, b, *rest: z_sum_kernel(n_z, a, b, *rest[len(deps) :]),
+        out_shape=jax.ShapeDtypeStruct((n_which, blk, cols), F32),
+        in_specs=[VM, VM] + [ANY] * len(deps),
+        out_specs=VM,
+        scratch_shapes=[
+            pltpu.VMEM(same.shape, BF16),
+            pltpu.VMEM(same.shape, BF16),
+            dma((n_which, n_z)),
+            dma((n_which, n_z)),
+        ],
+        compiler_params=pltpu.CompilerParams(
+            collective_id=collective_id, has_side_effects=True, vmem_limit_bytes=24 << 20
+        ),
+        cost_estimate=cost(0, 40 << 20),
+        name="sum_attention_gradients",
+    )(same, other, *deps)
 
 
 def ffn_kernel(nb, rows_each, *refs):
@@ -378,21 +504,20 @@
         lax.fori_loop(0, rows_each // Q_ROWS, rows_step, 0)
 
 
-def ffn(ns, ups, w):
+def ffn(ns, ups, w, **more):
     nb = len(ns)
     rows_each, width = ns[0].shape
     units = w.shape[2]
     kept = jax.ShapeDtypeStruct((nb * rows_each, units), BF16)
     part = jax.ShapeDtypeStruct((rows_each, width), BF16)
-    return pl.pallas_call(
+    return call(
         functools.partial(ffn_kernel, nb, rows_each),
-        out_shape=[kept] * 3 + [part] * (2 * nb),
-        in_specs=[VM] * (2 * nb + 1),
-        out_specs=[VM] * (3 + 2 * nb),
-        compiler_params=params(),
-        cost_estimate=cost(12 * nb * rows_each * width * units, 28 << 20),
-        name="feed_forward",
-    )(*ns, *ups, w)
+        "feed_forward",
+        [*ns, *ups, w],
+        [kept] * 3 + [part] * (2 * nb),
+        12 * nb * rows_each * width * units,
+        **more,
+    )
 
 
 def ffn_grad_kernel(n_blocks, n_halves, rows_each, *refs):
@@ -421,30 +546,224 @@
         lax.fori_loop(0, width // tile, col_step, 0)
 
 
-def ffn_grad(ns, ups, kept):
+def ffn_grad(ns, ups, kept, **more):
     n_blocks = len(ns)
     rows_each, width = ns[0].shape
     units = kept[0].shape[1]
+    return call(
+        functools.partial(ffn_grad_kernel, n_blocks, len(kept) // 3, rows_each),
+        "feed_forward_weight_gradient",
+        [*ns, *ups, *kept],
+        [jax.ShapeDtypeStruct((3, width, units), BF16)],
+        6 * n_blocks * rows_each * width * units,
+        **more,
+    )
+
+
+def prologue_kernel(n_z, n_t, blk, *refs):
+    tokens, qkv, outw, gains = refs[:4]
+    xs, wq, wo, gain_sum = refs[4:8]
+    held, got, own_sem, tok_send, tok_recv, z_send, z_recv, x_send, x_recv, g_send, g_recv = refs[8:]
+    d, t = lax.axis_index("dp"), lax.axis_index("tensor")
+    z, x = d // 2, lax.rem(d, 2)
+    bits = bits_down(n_t)
+
+    def at_z(k):
+        return {"dp": lax.rem(z + k, n_z) * 2 + x}
+
+    other_x = {"dp": z * 2 + (1 - x)}
+
+    def at_t(bit):
+        return {"tensor": t ^ bit}
+
+    barrier = pltpu.get_barrier_semaphore()
+    peers = [at_z(k) for k in range(1, n_z)] + [other_x] + [at_t(bit) for bit in bits]
+    for peer in peers:
+        pl.semaphore_signal(barrier, inc=1, device_id=peer, device_id_type=MESH)
+    pl.semaphore_wait(barrier, len(peers))
+
+    def send(src, dst, send_sem, recv_sem, peer):
+        copy = pltpu.make_async_remote_copy(
+            src_ref=src,
+            dst_ref=dst,
+            send_sem=send_sem,
+            recv_sem=recv_sem,
+            device_id=peer,
+            device_id_type=MESH,
+        )
+        copy.start()
+        return copy
+
+    def owned(k):
+        return pl.ds(pl.multiple_of((lax.rem(z + n_z - k, n_z) * 2 + x) * blk, 16), blk)
+
+    pending = []
+    held[0, :, :] = gains[...]
+    stages = [at_t(bit) for bit in bits] + [other_x]
+    gain_copy = send(held.at[0], got.at[0], g_send.at[0], g_recv.at[0], stages[0])
+    token_copies = {}
+    for bit in bits:
+        token_copies[bit] = send(
+            tokens, xs.at[bit - 1], tok_send.at[bit], tok_recv.at[bit], at_t(bit)
+        )
+    locals_ = [
+        pltpu.make_async_copy(qkv, wq.at[owned(0)], own_sem.at[0]),
+        pltpu.make_async_copy(outw, wo.at[owned(0)], own_sem.at[1]),
+    ]
+    for copy in locals_:
+        copy.start()
+    z_copies, x_copies = {}, {}
+    for k in range(1, n_z):
+        z_copies[0, k] = send(qkv, wq.at[owned(0)], z_send.at[0, k], z_recv.at[0, k], at_z(k))
+    x_copies[0, 0] = send(qkv, wq.at[owned(0)], x_send.at[0, 0], x_recv.at[0, 0], other_x)
+    for stage in range(len(stages)):
+        gain_copy.wait()
+        held[stage + 1, :, :] = held[stage, :, :] + got[stage, :, :]
+        if stage + 1 < len(stages):
+            gain_copy = send(
+                held.at[stage + 1],
+                got.at[stage + 1],
+                g_send.at[stage + 1],
+                g_recv.at[stage + 1],
+                stages[stage + 1],
+            )
+    last = len(stages)
+    gain_z = [
+        send(held.at[last], got.at[last + k - 1], g_send.at[last + k - 1], g_recv.at[last + k - 1], at_z(k))
+        for k in range(1, n_z)
+    ]
+    for k in range(1, n_z):
+        z_copies[1, k] = send(outw, wo.at[owned(0)], z_send.at[1, k], z_recv.at[1, k], at_z(k))
+    for which, whole in ((0, wq), (1, wo)):
+        if which == 1:
+            x_copies[1, 0] = send(outw, wo.at[owned(0)], x_send.at[1, 0], x_recv.at[1, 0], other_x)
+        for k in range(1, n_z):
+            z_copies[which, k].wait_recv()
+            x_copies[which, k] = send(
+                whole.at[owned(k)],
+                whole.at[owned(k)],
+                x_send.at[which, k],
+                x_recv.at[which, k],
+                other_x,
+            )
+    arrived = [0]
+    for bit in bits:
+        for r in list(arrived):
+            if r:
+                token_copies[r ^ bit] = send(
+                    xs.at[r - 1], xs.at[(r ^ bit) - 1], tok_send.at[r ^ bit], tok_recv.at[r ^ bit], at_t(bit)
+                )
+        for r in list(arrived):
+            token_copies[r ^ bit].wait_recv()
+            arrived.append(r ^ bit)
+    total = held[last, :, :]
+    for k in range(1, n_z):
+        gain_z[k - 1].wait()
+        total = total + got[last + k - 1, :, :]
+    gain_sum[...] = total
+    for copy in token_copies.values():
+        copy.wait_send()
+    for copy in z_copies.values():
+        copy.wait_send()
+    for copy in x_copies.values():
+        copy.wait()
+    for copy in locals_:
+        copy.wait()
+
+
+def prologue(tokens, qkv, outw, gains, n_z, n_t, n_dp):
+    blk = qkv.shape[0]
+    n_gain = len(bits_down(n_t)) + 1 + n_z - 1
+    dma = pltpu.SemaphoreType.DMA
     return pl.pallas_call(
-        functools.partial(ffn_grad_kernel, n_blocks, len(kept) // 3, rows_each),
-        out_shape=jax.ShapeDtypeStruct((3, width, units), BF16),
-        in_specs=[VM] * (2 * n_blocks + len(kept)),
+        functools.partial(prologue_kernel, n_z, n_t, blk),
+        out_shape=[
+            jax.ShapeDtypeStruct((n_t - 1,) + tokens.shape, BF16),
+            jax.ShapeDtypeStruct((blk * n_dp, qkv.shape[1]), BF16),
+            jax.ShapeDtypeStruct((blk * n_dp, outw.shape[1]), BF16),
+            jax.ShapeDtypeStruct(gains.shape, F32),
+        ],
+        in_specs=[ANY, ANY, ANY, VM],
+        out_specs=[ANY, ANY, ANY, VM],
+        scratch_shapes=[
+            pltpu.VMEM((n_gain + 1,) + gains.shape, F32),
+            pltpu.VMEM((n_gain,) + gains.shape, F32),
+            dma((2,)),
+            dma((n_t,)),
+            dma((n_t,)),
+            dma((2, n_z)),
+            dma((2, n_z)),
+            dma((2, n_z)),
+            dma((2, n_z)),
+            dma((n_gain,)),
+            dma((n_gain,)),
+        ],
+        compiler_params=pltpu.CompilerParams(
+            collective_id=0, has_side_effects=True, vmem_limit_bytes=4 << 20
+        ),
+        cost_estimate=cost(0, 60 << 20),
+        name="gather_tokens_and_weights",
+    )(tokens, qkv, outw, gains)
+
+
+def sum_kernel(n_dp, n_t, value, out, first, second, send_sem, recv_sem):
+    d, t = lax.axis_index("dp"), lax.axis_index("tensor")
+    peers = [{"tensor": lax.rem(t + k, n_t)} for k in range(1, n_t)]
+    peers += [{"dp": lax.rem(d + k, n_dp)} for k in range(1, n_dp)]
+    barrier = pltpu.get_barrier_semaphore()
+    for peer in peers:
+        pl.semaphore_signal(barrier, inc=1, device_id=peer, device_id_type=MESH)
+    pl.semaphore_wait(barrier, len(peers))
+
+    def exchange(buffer, me, targets, base):
+        copies = []
+        for k, peer in enumerate(targets):
+            copy = pltpu.make_async_remote_copy(
+                src_ref=buffer.at[me],
+                dst_ref=buffer.at[me],
+                send_sem=send_sem.at[base + k],
+                recv_sem=recv_sem.at[base + k],
+                device_id=peer,
+                device_id_type=MESH,
+            )
+            copy.start()
+            copies.append(copy)
+        for copy in copies:
+            copy.wait()
+        total = buffer[0, :, :]
+        for i in range(1, len(targets) + 1):
+            total = total + buffer[i, :, :]
+        return total
+
+    first[t, :, :] = value[...]
+    second[d, :, :] = exchange(first, t, peers[: n_t - 1], 0)
+    out[...] = exchange(second, d, peers[n_t - 1 :], n_t - 1)
+
+
+def sum_all(value, n_dp, n_t, collective_id, name):
+    dma = pltpu.SemaphoreType.DMA
+    return pl.pallas_call(
+        functools.partial(sum_kernel, n_dp, n_t),
+        out_shape=jax.ShapeDtypeStruct(value.shape, F32),
+        in_specs=[VM],
         out_specs=VM,
-        compiler_params=params(),
-        cost_estimate=cost(6 * n_blocks * rows_each * width * units, 34 << 20),
-        name="feed_forward_weight_gradient",
-    )(*ns, *ups, *kept)
+        scratch_shapes=[
+            pltpu.VMEM((n_t,) + value.shape, F32),
+            pltpu.VMEM((n_dp,) + value.shape, F32),
+            dma((n_t + n_dp,)),
+            dma((n_t + n_dp,)),
+        ],
+        compiler_params=pltpu.CompilerParams(
+            collective_id=collective_id, has_side_effects=True, vmem_limit_bytes=8 << 20
+        ),
+        cost_estimate=cost(0, 8 << 20),
+        name=name,
+    )(value)
 
 
 def permute_xor(value, axis, bit):
     size = lax.axis_size(axis)
     return lax.ppermute(value, axis, [(i, i ^ bit) for i in range(size)])
-
-
-def shift_z(value, k, n_z):
-    return lax.ppermute(
-        value, "dp", [(z * 2 + x, ((z + k) % n_z) * 2 + x) for z in range(n_z) for x in range(2)]
-    )
 
 
 def bits_down(size):
@@ -456,46 +775,25 @@
     return bits
 
 
-def gather_relative(block):
-    size = lax.axis_size("tensor")
+def after(value, *earlier):
+    return lax.optimization_barrier((value,) + earlier)[0]
+
+
+def gather_group(block):
     have = {0: block}
-    for bit in bits_down(size):
+    for bit in bits_down(lax.axis_size("tensor") // 2):
         for r in list(have):
             have[r ^ bit] = permute_xor(have[r], "tensor", bit)
-    return [have[r] for r in range(size)]
-
-
-def scatter_relative(parts):
-    size = lax.axis_size("tensor")
+    return [have[r] for r in range(len(have))]
+
+
+def reduce_group(parts):
     have = dict(enumerate(parts))
-    for bit in reversed(bits_down(size)):
+    for bit in reversed(bits_down(len(parts))):
         for r in [r for r in have if r & bit]:
-            received = permute_xor(have.pop(r), "tensor", bit)
-            summed = have[r ^ bit].astype(F32) + received.astype(F32)
-            have[r ^ bit] = summed if bit == size // 2 else summed.astype(BF16)
+            received = permute_xor(have.pop(r).astype(BF16), "tensor", bit)
+            have[r ^ bit] = have[r ^ bit].astype(F32) + received.astype(F32)
     return have[0].astype(F32)
-
-
-def gather_dp(block, n_z):
-    same = [block] + [shift_z(block, k, n_z) for k in range(1, n_z)]
-    return same + [permute_xor(b, "dp", 1) for b in same]
-
-
-def scatter_dp(same, other, n_z):
-    received = permute_xor(other, "dp", 1)
-    held = same.astype(F32) + received.astype(F32)
-    total = held[0]
-    narrow = held.astype(BF16)
-    for k in range(1, n_z):
-        total = total + shift_z(narrow[k], k, n_z).astype(F32)
-    return total
-
-
-def sum_everywhere(value):
-    for axis in ("tensor", "dp"):
-        for bit in reversed(bits_down(lax.axis_size(axis))):
-            value = value + permute_xor(value, axis, bit)
-    return value
 
 
 def rms_norm(values, gain_row):
@@ -545,16 +843,13 @@
     nb = n_t // 2
     t = lax.axis_index("tensor")
     d = lax.axis_index("dp")
-    local = lax.rem(t, nb)
     mine = t // nb
-    place = jnp.stack([d // 2, lax.rem(d, 2)]).astype(jnp.int32)
-    info = [
-        jnp.stack([lengths[mine], local]).astype(jnp.int32),
-        jnp.stack([lengths[1 - mine], local]).astype(jnp.int32),
-    ]
+    info = [lengths[mine][None], lengths[1 - mine][None]]
     spread = spread_matrix().astype(BF16)
     blk = qkv_weight.shape[0]
     kv = qkv_weight.shape[1] // G_COLS
+
+    over = ("tensor", nb)
 
     gain_cols = norm_gains.shape[1]
     gain_start = (d * n_t + t) * gain_cols
@@ -563,93 +858,123 @@
         norm_gains.astype(BF16).astype(F32),
         (0, gain_start),
     )
-    gain_work = sum_everywhere(gain_rows)
+    out_half = out_weight.astype(BF16).T
+    x_rest, wq, wo, gain_work = prologue(
+        tokens, qkv_weight.astype(BF16), out_half, gain_rows, n_z, n_t, n_dp
+    )
     attention_gain, feedforward_gain = gain_work[0:1], gain_work[1:2]
-
-    qkv_half = qkv_weight.astype(BF16)
-    out_half = out_weight.astype(BF16).T
-    w_qkv = assemble(gather_dp(qkv_half, n_z), place, spread, n_z)
     w_out_cols = out_half.shape[1]
-    out_fill = -w_out_cols % G_COLS
-    out_blocks = gather_dp(out_half, n_z)
-    if out_fill:
-        out_blocks = [jnp.pad(b, ((0, 0), (0, out_fill))) for b in out_blocks]
-    w_out = assemble(out_blocks, place, spread, n_z)[:, : kv * GROUP * PAD]
+    if w_out_cols % G_COLS:
+        wo = jnp.pad(wo, ((0, 0), (0, -w_out_cols % G_COLS)))
+    w_qkv, w_out = pad_weights(wq, wo, spread)
+    w_out = w_out[:, : kv * GROUP * PAD]
     ffn_half = jnp.concatenate(
         [gate_up_weight.astype(BF16), down_weight.astype(BF16).T[None]], axis=0
     )
     w_ffn = lax.all_gather(ffn_half, "dp", axis=1, tiled=True)
 
     inputs = tokens.astype(F32)
-    x_blocks = gather_relative(tokens)
+    x_blocks = [tokens] + [x_rest[r] for r in range(n_t - 1)]
     cos_t, sin_t = rotary_tables()
-    fwd = [
-        attn_fwd(
-            x_blocks[s * nb : (s + 1) * nb], info[s], attention_gain, w_qkv, w_out, cos_t, sin_t
-        )
-        for s in range(2)
-    ]
-    residual = inputs + scatter_relative(list(fwd[0][4:]) + list(fwd[1][4:]))
-
-    n_blocks = gather_relative(rms_norm(residual, feedforward_gain).astype(BF16))
-    c_blocks = gather_relative(cotangent)
-    far = ffn(n_blocks[nb:], c_blocks[nb:], w_ffn)
-    near = ffn(n_blocks[:nb], c_blocks[:nb], w_ffn)
-    normed_two_grad = scatter_relative(list(near[3 + nb :]) + list(far[3 + nb :]))
-    out_sum = scatter_relative(list(near[3 : 3 + nb]) + list(far[3 : 3 + nb]))
-    layer_out = (residual + out_sum).astype(BF16)
-    ffn_grads = ffn_grad(n_blocks, c_blocks, list(near[:3]) + list(far[:3]))
+    *far_fwd, c_far = attn_fwd(
+        x_blocks[nb:],
+        info[1],
+        attention_gain,
+        w_qkv,
+        w_out,
+        cos_t,
+        sin_t,
+        sends=[(cotangent, over)],
+        collective_id=3,
+    )
+    far_sum = reduce_group(far_fwd[4:]).astype(BF16)
+    *near_fwd, far_sum = attn_fwd(
+        x_blocks[:nb],
+        info[0],
+        attention_gain,
+        w_qkv,
+        w_out,
+        cos_t,
+        sin_t,
+        sends=[(far_sum, over)],
+        collective_id=4,
+    )
+    residual = inputs + (reduce_group(near_fwd[4:]) + far_sum.astype(F32))
+
+    normed_two = rms_norm(residual, feedforward_gain).astype(BF16)
+    n_near = gather_group(normed_two)
+    c_near = gather_group(cotangent)
+    c_far = gather_group(c_far)
+    *near, n_far = ffn(n_near, c_near, w_ffn, sends=[(normed_two, over)], collective_id=5)
+    n_far = gather_group(n_far)
+    far = ffn(n_far, c_far, w_ffn)
+    far_grad = reduce_group(far[3 + nb :]).astype(BF16)
+    ffn_grads, far_grad = ffn_grad(
+        n_near + n_far,
+        c_near + c_far,
+        list(near[:3]) + list(far[:3]),
+        sends=[(far_grad, over)],
+        collective_id=6,
+    )
+    normed_two_grad = reduce_group(near[3 + nb :]) + far_grad.astype(F32)
     ffn_sum = lax.psum_scatter(ffn_grads, "dp", scatter_dimension=1, tiled=True).astype(F32)
 
     _, norm_pull = jax.vjp(rms_norm, residual, feedforward_gain)
     residual_part, ffn_gain_grad = norm_pull(normed_two_grad)
     residual_grad = cotangent.astype(F32) + residual_part
-    a_blocks = gather_relative(residual_grad.astype(BF16))
-    bwd = [
-        attn_bwd(
-            a_blocks[s * nb : (s + 1) * nb],
-            info[s],
-            w_qkv,
-            w_out,
-            fwd[s][1],
-            fwd[s][3],
-            cos_t,
-            sin_t,
-        )
-        for s in range(2)
-    ]
-    starts = [(local ^ r) * rows_each for r in range(nb)] * 2
-    out_info = jnp.concatenate([place, jnp.stack(starts).astype(jnp.int32)])
-    att = [fwd[0][2]] * nb + [fwd[1][2]] * nb
-    att_fill = -att[0].shape[1] % G_PAD
-    if att_fill:
-        att = [jnp.pad(a, ((0, 0), (0, att_fill))) for a in att]
-    out_pair = weight_grad(a_blocks, att, out_info, spread, n_z, blk, 0, True)
-    out_grad_sum = scatter_dp(*out_pair, n_z)[:, :w_out_cols].T
-    qkv_grad_sum = jnp.concatenate(
-        [
-            scatter_dp(
-                *weight_grad(
-                    [fwd[0][0], fwd[1][0]],
-                    [bwd[0][0], bwd[1][0]],
-                    place,
-                    spread,
-                    n_z,
-                    blk,
-                    j,
-                    None,
-                ),
-                n_z,
-            )
-            for j in range(kv)
-        ],
-        axis=1,
-    )
-    normed_grad = scatter_relative(list(bwd[0][1:]) + list(bwd[1][1:]))
+    attention_grad = residual_grad.astype(BF16)
+    a_near = gather_group(attention_grad)
+    *near_bwd, a_far = attn_bwd(
+        a_near,
+        info[0],
+        w_qkv,
+        w_out,
+        near_fwd[1],
+        near_fwd[3],
+        cos_t,
+        sin_t,
+        sends=[(attention_grad, over)],
+        collective_id=7,
+    )
+    a_far = gather_group(a_far)
+    far_out = reduce_group(far[3 : 3 + nb]).astype(BF16)
+    *far_bwd, far_out = attn_bwd(
+        a_far,
+        info[1],
+        w_qkv,
+        w_out,
+        far_fwd[1],
+        far_fwd[3],
+        cos_t,
+        sin_t,
+        sends=[(far_out, over)],
+        collective_id=8,
+    )
+    layer_out = (residual + (reduce_group(near[3 : 3 + nb]) + far_out.astype(F32))).astype(BF16)
+    far_sum = reduce_group(far_bwd[1:]).astype(BF16)
+    same, _, other, far_sum = weight_grad(
+        a_near + a_far,
+        [near_fwd[2], far_fwd[2]],
+        [near_fwd[0], far_fwd[0]],
+        [near_bwd[0], far_bwd[0]],
+        spread,
+        n_z,
+        blk,
+        sends=[(far_sum, over)],
+        meets=[("dp", 1)],
+        collective_id=9,
+    )
+    normed_grad = reduce_group(near_bwd[1:]) + far_sum.astype(F32)
+    attention_sum = z_sum(same, other, n_z, 10)
+    out_grad_sum = attention_sum[0, :, :w_out_cols].T
+    qkv_grad_sum = jnp.concatenate([attention_sum[1 + j] for j in range(kv)], axis=1)
     _, first_pull = jax.vjp(rms_norm, inputs, attention_gain)
     input_part, attention_gain_grad = first_pull(normed_grad)
     grad_tokens = residual_grad + input_part
-    gain_all = sum_everywhere(jnp.concatenate([attention_gain_grad, ffn_gain_grad], axis=0))
+    gain_grads = jnp.concatenate([attention_gain_grad, ffn_gain_grad], axis=0)
+    gain_all = sum_all(
+        gain_grads.reshape(-1, PAD), n_dp, n_t, 1, "sum_gain_gradients"
+    ).reshape(2, width)
     gain_sums = lax.dynamic_slice(gain_all, (0, gain_start), (2, gain_cols))
 
     masters = (
@@ -706,7 +1031,8 @@
         [jnp.sum(master * master) for master in masters]
         + [jnp.sum(update * update) for update in updates]
     )
-    norms = jnp.sqrt(sum_everywhere(squares[None])[0])
+    squares = jnp.pad(squares[None], ((0, 7), (0, PAD - 14)))
+    norms = jnp.sqrt(sum_all(squares, n_dp, n_t, 2, "sum_squares")[0, :14])
     weight_norms, all_update_norms = norms[:7], norms[7:]
     new_weights = [
         masters[number]

time: 762 us -> 666 us (0.87)
  waiting for transfers between devices: 325 us -> 24.9 us
  Pallas kernels: 238 us -> 512 us
  starting transfers between devices: 91 us -> 3.21 us
    ppermute x50 -> x14, waiting for transfers between devices: 301 us -> 24.9 us  [permute_xor(): return lax.ppermute(value, axis, [(i, i ^ bit) for i in range(size)])]
    pallas_call x12 -> x13, Pallas kernels: 238 us -> 512 us  [the longest x9 368 us: call(): pl.pallas_call(functools.partial(carrying_kernel, body, (len(inputs), len...]
    ppermute x50 -> x14, starting transfers between devices: 53.6 us -> 3.13 us  [permute_xor(): return lax.ppermute(value, axis, [(i, i ^ bit) for i in range(size)])]
    ppermute x15 -> x0, starting transfers between devices: 37.3 us -> none  [shift_z(): lax.ppermute(value, 'dp', [(z * 2 + x, (z + k) % n_z * 2 + x) for z in ra...]
    ppermute x15 -> x0, waiting for transfers between devices: 23.8 us -> none  [shift_z(): lax.ppermute(value, 'dp', [(z * 2 + x, (z + k) % n_z * 2 + x) for z in ra...]
    convert_element_type x9 -> x8, other arithmetic: 11.3 us -> 17.3 us  [the longest x1 3.56 us: shards(): (residual + (reduce_group(near[3:3 + nb]) + far_out.astype(F32))).astype(...]
    unnamed x136 -> x112, local copies, waits for them, and re-layouts: 10.4 us -> 15.3 us
  transfers between devices with their start and end apart: 67 -> 16, of which waited for: 32 -> 8; matrix products, arithmetic and copies ran while one was open for 5% -> 6% of each run, Pallas kernels for 23% -> 65%
where the time goes in v2:
time: 666 us; the launch traced here: 656 us
  Pallas kernels  512 us (77%)
  other arithmetic  61.3 us (9%)
  local copies, waits for them, and re-layouts  30.6 us (5%)
  waiting for transfers between devices  24.9 us (4%)
  between operations  24.2 us (4%)
    pallas_call x9, Pallas kernels, call(): pl.pallas_call(functools.partial(carrying_kernel, body, (len(inputs), len...  368 us
    pallas_call x1, Pallas kernels, prologue(): pl.pallas_call(functools.partial(prologue_kernel, n_z, n_t, blk), out_sha...  83.6 us
    pallas_call x1, Pallas kernels, z_sum(): pl.pallas_call(lambda a, b, *rest: z_sum_kernel(n_z, a, b, *rest[len(deps...  39.5 us
    ppermute x14, waiting for transfers between devices, permute_xor(): return lax.ppermute(value, axis, [(i, i ^ bit) for i in range(size)])  24.9 us
    pallas_call x2, Pallas kernels, sum_all(): pl.pallas_call(functools.partial(sum_kernel, n_dp, n_t), out_shape=jax.Sh...  21.2 us
    unnamed x112, local copies, waits for them, and re-layouts  15.3 us
  transfers between devices with their start and end apart: 16, of which 8 were waited for; matrix products, arithmetic and copies ran while one was open for 6% of the time, Pallas kernels for 65%

profile of v2, /device:TPU:0, one launch (start us, length us, event | category | flops | bytes accessed | tf_op | source)
XLA Modules:
  0.0 656.5 jit_solution(18136702720566299098)
XLA Ops:
  11.6 83.6 %gather_tokens_and_weights.1 = (bf16[3,512,1536]{2,1,0:T(8,128)(2,1)S(1)}, bf16[1536,768]{1,0:T(8,128)(2,1)S(1)}, bf16[1536,384]{1,0:T(8,128)(2,1)S(1)}, f32[2,1536]{1,0:T(2,128)S(1)}) custom-call(bf16[512,1536]{1,0:T(8,128)(2,1)S(1)} %copy-done, bf16[192,768]{1,0:T(8,128)(2,1)S(1)} %convert_element_type.116.refs_1_, ...), custom_call_target="tpu_custom_call" | custom-call | bytes 62914560 | tf_op jit(solution)/shard_map/gather_tokens_and_weights/pallas_call | solution.py:678
  99.1 6.6 %pad_weights.1 = (bf16[1536,1024]{1,0:T(8,128)(2,1)}, bf16[1536,512]{1,0:T(8,128)(2,1)}) custom-call(bf16[384,512]{1,0:T(8,128)(2,1)} %fusion.29.refs_0_, bf16[1536,768]{1,0:T(8,128)(2,1)} %copy-done.4, bf16[1536,384]{1,0:T(8,128)(2,1)} %copy-done.5), custom_call_target="tpu_custom_call" | custom-call | flops 1811939328 | bytes 8650752 | tf_op jit(solution)/shard_map/pad_weights/pallas_call | solution.py:110
  109.5 2.3 slice_bitcast_fusion
  111.8 41.9 %attention_forward.2 = (bf16[1024,1536]{1,0:T(8,128)(2,1)}, bf16[1024,1024]{1,0:T(8,128)(2,1)}, bf16[1024,512]{1,0:T(8,128)(2,1)}, f32[1024,128]{1,0:T(8,128)}, ...) custom-call(s32[1]{0:T(128)} %get-tuple-element.185.refs_0_, ...), custom_call_target="tpu_custom_call" | custom-call | flops 9126805504 | bytes 18880516 | tf_op jit(solution)/shard_map/attention_forward/pallas_call | solution.py:110
  153.8 3.6 collective-permute-done
  157.4 2.9 add_convert_fusion.4.refs_8_
  160.4 45.0 %attention_forward.3 = (bf16[1024,1536]{1,0:T(8,128)(2,1)}, bf16[1024,1024]{1,0:T(8,128)(2,1)}, bf16[1024,512]{1,0:T(8,128)(2,1)}, f32[1024,128]{1,0:T(8,128)}, ...) custom-call(s32[1]{0:T(128)} %get-tuple-element.186.refs_0_, ...), custom_call_target="tpu_custom_call" | custom-call | flops 9126805504 | bytes 18880516 | tf_op jit(solution)/shard_map/attention_forward/pallas_call | solution.py:110
  205.9 4.5 collective-permute-done.1
  210.4 3.1 multiply_reduce_fusion.2
  217.5 2.1 collective-permute-done.2.refs_1_
  219.6 46.9 %feed_forward.2 = (bf16[1024,1024]{1,0:T(8,128)(2,1)}, bf16[1024,1024]{1,0:T(8,128)(2,1)}, bf16[1024,1024]{1,0:T(8,128)(2,1)}, bf16[512,1536]{1,0:T(8,128)(2,1)}...) custom-call(bf16[512,1536]{1,0:T(8,128)(2,1)} %copy-done.38, ...), custom_call_target="tpu_custom_call" | custom-call | flops 19327352832 | bytes 28311552 | tf_op jit(solution)/shard_map/feed_forward/pallas_call | solution.py:110
  266.6 3.6 collective-permute-done.6.refs_1_.refs_3_
  271.3 28.3 %feed_forward.3 = (bf16[1024,1024]{1,0:T(8,128)(2,1)}, bf16[1024,1024]{1,0:T(8,128)(2,1)}, bf16[1024,1024]{1,0:T(8,128)(2,1)}, bf16[512,1536]{1,0:T(8,128)(2,1)}...) custom-call(bf16[512,1536]{1,0:T(8,128)(2,1)} %get-tuple-element.83.refs_0_.refs_2_, ...), custom_call_target="tpu_custom_call" | custom-call | flops 19327352832 | bytes 28311552 | tf_op jit(solution)/shard_map/feed_forward/pallas_call | solution.py:110
  299.7 3.5 collective-permute-done.8
  303.2 3.0 add_convert_fusion.3.refs_14_
  306.2 48.7 %feed_forward_weight_gradient.1 = (bf16[3,1536,1024]{2,1,0:T(8,128)(2,1)}, bf16[512,1536]{1,0:T(8,128)(2,1)}) custom-call(bf16[512,1536]{1,0:T(8,128)(2,1)} %copy-done.38, bf16[512,1536]{1,0:T(8,128)(2,1)} %collective-permute-done.2.refs_1_, bf16[512,1536]{1,0:T(8,128)(2,1)} %get-tuple-element.83.refs_0_.refs_2_, bf16[512,1536]{1,0:T(8,128)(2,1)} %copy-done.55, ...), custom_call_target="tpu_custom_call" | custom-call | flops 19327352832 | bytes 34603008 | tf_op jit(solution)/shard_map/feed_forward_weight_gradient/pallas_call | solution.py:110
  354.9 3.6 collective-permute-done.5
  358.6 3.7 multiply_reduce_fusion
  362.8 3.0 fusion.68
  367.4 3.8 collective-permute-done.9.refs_2_
  372.3 44.2 %attention_backward.2 = (bf16[1024,1024]{1,0:T(8,128)(2,1)}, bf16[512,1536]{1,0:T(8,128)(2,1)}, bf16[512,1536]{1,0:T(8,128)(2,1)}, bf16[512,1536]{1,0:T(8,128)(2,1)}) custom-call(s32[1]{0:T(128)} %get-tuple-element.186.refs_0_, bf16[512,1536]{1,0:T(8,128)(2,1)} %copy-done.36, bf16[512,1536]{1,0:T(8,128)(2,1)} %copy-done.52, ...), custom_call_target="tpu_custom_call" | custom-call | flops 15569256448 | bytes 16777220 | tf_op jit(solution)/shard_map/attention_backward/pallas_call | solution.py:110
  417.2 3.0 add_convert_fusion.2.refs_9_
  421.4 44.3 %attention_backward.3 = (bf16[1024,1024]{1,0:T(8,128)(2,1)}, bf16[512,1536]{1,0:T(8,128)(2,1)}, bf16[512,1536]{1,0:T(8,128)(2,1)}, bf16[512,1536]{1,0:T(8,128)(2,1)}) custom-call(s32[1]{0:T(128)} %get-tuple-element.185.refs_0_, bf16[512,1536]{1,0:T(8,128)(2,1)} %get-tuple-element.96.refs_1_.refs_3_, bf16[512,1536]{1,0:T(8,128)(2,1)} %copy-done.53, ...), custom_call_target="tpu_custom_call" | custom-call | flops 15569256448 | bytes 16777220 | tf_op jit(solution)/shard_map/attention_backward/pallas_call | solution.py:110
  467.8 3.6 add_convert_fusion.1
  472.9 62.3 %attention_weight_gradients.1 = (bf16[3,4,192,384]{3,2,1,0:T(8,128)(2,1)}, bf16[3,4,192,384]{3,2,1,0:T(8,128)(2,1)}, bf16[3,4,192,384]{3,2,1,0:T(8,128)(2,1)}, bf16[512,1536]{1,0:T(8,128)(2,1)}) custom-call(bf16[384,512]{1,0:T(8,128)(2,1)} %fusion.29.refs_0_, bf16[512,1536]{1,0:T(8,128)(2,1)} %copy-done.36, bf16[512,1536]{1,0:T(8,128)(2,1)} %copy-done.52, ...), custom_call_target="tpu_custom_call" | custom-call | flops 9663676416 | bytes 24576000 | tf_op jit(solution)/shard_map/attention_weight_gradients/pallas_call | solution.py:110
  535.3 3.4 fusion.5
  538.8 10.6 %sum_gain_gradients.1 = f32[24,128]{1,0:T(8,128)S(1)} custom-call(f32[24,128]{1,0:T(8,128)S(1)} %reshape.187.value), custom_call_target="tpu_custom_call" | custom-call | bytes 8388608 | tf_op jit(solution)/shard_map/sum_gain_gradients/pallas_call | solution.py:745
  550.9 39.5 %sum_attention_gradients.1 = f32[3,192,384]{2,1,0:T(8,128)S(1)} custom-call(bf16[3,4,192,384]{3,2,1,0:T(8,128)(2,1)S(1)} %copy-done.2, bf16[3,4,192,384]{3,2,1,0:T(8,128)(2,1)S(1)} %copy-done.3), custom_call_target="tpu_custom_call" | custom-call | bytes 41943040 | tf_op jit(solution)/shard_map/sum_attention_gradients/pallas_call | solution.py:458
  595.3 2.9 fusion.1
  605.5 9.1 %stack.89 = f32[14]{0:T(128)S(1)} concatenate(f32[1]{0:T(128)} %bitcast.6, f32[1]{0:T(128)} %bitcast.7, f32[1]{0:T(128)} %bitcast.8, f32[1]{0:T(128)} %bitcast.9, f32[1]{0:T(128)} %bitcast.10, f32[1]{0:T(128)} %bitcast.11, f32[1]{0:T(128)} %bitcast.12, f32[1]{0:T(128)} %bitcast.15, f32[1]{0:T(128)} %bitcast.19, f32[1]{0:T(128)} %bitcast.24, f32[1]{0:T(128)} %bitcast.29, ...), dimensions={0} | concatenate | bytes 112 | tf_op jit(solution)/shard_map/stack | solution.py:1030
  614.6 10.6 %sum_squares.1 = f32[8,128]{1,0:T(8,128)S(1)} custom-call(f32[8,128]{1,0:T(8,128)S(1)} %pad.4.value), custom_call_target="tpu_custom_call" | custom-call | bytes 8388608 | tf_op jit(solution)/shard_map/sum_squares/pallas_call | solution.py:745
  637.5 3.5 multiply_subtract_fusion.2
  (195 shorter events, 51.9 us)
Async XLA Ops:
  7.2 212.4 %all-gather.2.cloned.1.call-start = ((), (), s32[]{:S(2)}) async-start(), calls=%async_computation.1 | async-start | bytes 10616832 | tf_op jit(solution)/shard_map/all_gather | solution.py:874
  10.1 588.1 %reduce-scatter.2.cloned.1.call-start = ((), (), s32[]{:S(2)}) async-start(), calls=%async_computation.2 | async-start | bytes 10616832 | tf_op jit(solution)/shard_map/reduce_scatter | solution.py:920
  10.2 87.4 %copy-start.51 = (s32[2]{0:T(128)S(1)}, s32[2]{0:T(128)}, u32[]{:S(2)}) copy-start(s32[2]{0:T(128)} %param.20) | copy-start | bytes 28
  153.8 3.7 collective-permute-start
  160.4 45.0 %copy-start.33 = (bf16[512,1536]{1,0:T(8,128)(2,1)S(1)}, bf16[512,1536]{1,0:T(8,128)(2,1)}, u32[]{:S(2)}) copy-start(bf16[512,1536]{1,0:T(8,128)(2,1)} %refs_4_.1) | copy-start | bytes 4718596
  160.4 50.0 %copy-start.1 = (bf16[512,1536]{1,0:T(8,128)(2,1)S(1)}, bf16[512,1536]{1,0:T(8,128)(2,1)}, u32[]{:S(2)}) copy-start(bf16[512,1536]{1,0:T(8,128)(2,1)} %refs_1_.1) | copy-start | bytes 4718596
  205.3 5.1 collective-permute-start.1
  205.4 10.3 %collective-permute-start.3 = (bf16[512,1536]{1,0:T(8,128)(2,1)S(1)}, bf16[512,1536]{1,0:T(8,128)(2,1)S(1)}, u32[]{:S(2)}, u32[]{:S(2)}) collective-permute-start(bf16[512,1536]{1,0:T(8,128)(2,1)S(1)} %copy-done.33), channel_id=1, source_target_pairs={{0,1},{1,0},{2,3},{3,2},{4,5},{5,4},{6,7},{7,6},{8,9},{9,8},{10,11... | collective-permute-start | bytes 4718600 | tf_op jit(solution)/shard_map/ppermute | solution.py:766
  215.2 4.4 collective-permute-start.2
  215.3 51.2 %collective-permute-start.7 = (bf16[512,1536]{1,0:T(8,128)(2,1)}, bf16[512,1536]{1,0:T(8,128)(2,1)}, u32[]{:S(2)}, u32[]{:S(2)}) collective-permute-start(bf16[512,1536]{1,0:T(8,128)(2,1)} %get-tuple-element.84.refs_2_.refs_6_), channel_id=1, source_target_pairs={{0,1},{1,0},{2,3},{3,2},{4,5},{5,4},{6,7},{7,6},{8,9},{9,8},{10,11... | collective-permute-start | bytes 4718600 | tf_op jit(solution)/shard_map/ppermute | solution.py:766
  266.5 3.7 collective-permute-start.6
  299.6 3.6 collective-permute-start.8
  354.9 3.7 collective-permute-start.5
  366.9 4.3 collective-permute-start.9
  367.0 50.1 %collective-permute-start.11 = (bf16[512,1536]{1,0:T(8,128)(2,1)}, bf16[512,1536]{1,0:T(8,128)(2,1)}, u32[]{:S(2)}, u32[]{:S(2)}) collective-permute-start(bf16[512,1536]{1,0:T(8,128)(2,1)} %get-tuple-element.100), channel_id=1, source_target_pairs={{0,1},{1,0},{2,3},{3,2},{4,5},{5,4},{6,7},{7,6},{8,9},{9,8},{10,11... | collective-permute-start | bytes 4718600 | tf_op jit(solution)/shard_map/ppermute | solution.py:766
  372.3 44.8 %copy-start.37 = (bf16[512,1536]{1,0:T(8,128)(2,1)S(1)}, bf16[512,1536]{1,0:T(8,128)(2,1)}, u32[]{:S(2)}) copy-start(bf16[512,1536]{1,0:T(8,128)(2,1)} %get-tuple-element.99) | copy-start | bytes 4718596
  416.6 3.7 collective-permute-start.10
  416.7 51.1 %collective-permute-start.4 = (bf16[512,1536]{1,0:T(8,128)(2,1)}, bf16[512,1536]{1,0:T(8,128)(2,1)S(1)}, u32[]{:S(2)}, u32[]{:S(2)}) collective-permute-start(bf16[512,1536]{1,0:T(8,128)(2,1)} %get-tuple-element.80), channel_id=1, source_target_pairs={{0,1},{1,0},{2,3},{3,2},{4,5},{5,4},{6,7},{7,6},{8,9},{9,8},{10,11... | collective-permute-start | bytes 4718600 | tf_op jit(solution)/shard_map/ppermute | solution.py:766
  421.4 45.0 %copy-start.8 = (f32[2,192,1024]{2,1,0:T(8,128)S(1)}, f32[2,192,1024]{2,1,0:T(8,128)}, u32[]{:S(2)}) copy-start(f32[2,192,1024]{2,1,0:T(8,128)} %param.23) | copy-start | bytes 4718596
  465.7 5.7 collective-permute-start.13
  467.2 68.0 %collective-permute-start.12 = (bf16[512,1536]{1,0:T(8,128)(2,1)}, bf16[512,1536]{1,0:T(8,128)(2,1)S(1)}, u32[]{:S(2)}, u32[]{:S(2)}) collective-permute-start(bf16[512,1536]{1,0:T(8,128)(2,1)} %get-tuple-element.103), channel_id=1, source_target_pairs={{0,1},{1,0},{2,3},{3,2},{4,5},{5,4},{6,7},{7,6},{8,9},{9,8},{10,11... | collective-permute-start | bytes 4718600 | tf_op jit(solution)/shard_map/ppermute | solution.py:766
  472.9 62.3 %copy-start.16 = (bf16[512,1536]{1,0:T(8,128)(2,1)S(1)}, bf16[512,1536]{1,0:T(8,128)(2,1)}, u32[]{:S(2)}) copy-start(bf16[512,1536]{1,0:T(8,128)(2,1)} %get-tuple-element.102) | copy-start | bytes 4718596
  550.8 39.6 %copy-start.50 = (f32[2,48]{1,0:T(2,128)S(1)}, f32[2,48]{1,0:T(2,128)}, u32[]{:S(2)}) copy-start(f32[2,48]{1,0:T(2,128)} %param.35) | copy-start | bytes 1156
  550.9 40.3 %copy-start.29 = (f32[384,192]{0,1:T(8,128)S(1)}, f32[384,192]{0,1:T(8,128)}, u32[]{:S(2)}) copy-start(f32[384,192]{0,1:T(8,128)} %param.22) | copy-start | bytes 884740
  550.9 40.3 %copy-start.46 = (f32[384,192]{0,1:T(8,128)S(1)}, f32[384,192]{0,1:T(8,128)}, u32[]{:S(2)}) copy-start(f32[384,192]{0,1:T(8,128)} %param.27) | copy-start | bytes 884740
  550.9 40.4 %copy-start.47 = (f32[384,192]{0,1:T(8,128)S(1)}, f32[384,192]{0,1:T(8,128)}, u32[]{:S(2)}) copy-start(f32[384,192]{0,1:T(8,128)} %param.32) | copy-start | bytes 884740
  550.9 41.9 %copy-start.24 = (f32[192,768]{1,0:T(8,128)S(1)}, f32[192,768]{1,0:T(8,128)}, u32[]{:S(2)}) copy-start(f32[192,768]{1,0:T(8,128)} %param.21) | copy-start | bytes 1769476
  550.9 41.9 %copy-start.44 = (f32[192,768]{1,0:T(8,128)S(1)}, f32[192,768]{1,0:T(8,128)}, u32[]{:S(2)}) copy-start(f32[192,768]{1,0:T(8,128)} %param.26) | copy-start | bytes 1769476
  550.9 41.9 %copy-start.45 = (f32[192,768]{1,0:T(8,128)S(1)}, f32[192,768]{1,0:T(8,128)}, u32[]{:S(2)}) copy-start(f32[192,768]{1,0:T(8,128)} %param.31) | copy-start | bytes 1769476
  550.9 44.0 %copy-start.20 = (bf16[512,1536]{1,0:T(8,128)(2,1)S(1)}, bf16[512,1536]{1,0:T(8,128)(2,1)}, u32[]{:S(2)}) copy-start(bf16[512,1536]{1,0:T(8,128)(2,1)} %get-tuple-element.112) | copy-start | bytes 4718596
  592.8 54.6 %copy-start.40 = (f32[384,192]{0,1:T(8,128)}, f32[384,192]{0,1:T(8,128)S(1)}, u32[]{:S(2)}) copy-start(f32[384,192]{0,1:T(8,128)S(1)} %get-tuple-element.150) | copy-start | bytes 884740
  603.7 42.4 %copy-start.26 = (f32[1024,192]{0,1:T(8,128)}, f32[1024,192]{0,1:T(8,128)S(1)}, u32[]{:S(2)}) copy-start(f32[1024,192]{0,1:T(8,128)S(1)} %get-tuple-element.148) | copy-start | bytes 2359300
  (40 other events, 134.1 us)
Sparse Core Ops, SparseCore 0:
  10.2 172.3 all-gather.1
  355.0 167.9 reduce-scatter.1

commit v3 on v0

v3 whole, which is shorter than its diff:
```python
import functools

import jax
import jax.numpy as jnp
import numpy as np
from jax import lax
from jax.experimental import pallas as pl
from jax.experimental.pallas import tpu as pltpu
from jax.sharding import PartitionSpec as P

HEAD = 96
PAD = 128
SEQ_LEN = 1024
SEQS_DEV = 2
STEP = 10
GROUP = 2

NORM_EPSILON = 1e-05
ROPE_THETA = 100000.0
BETA_ONE = 0.9
BETA_TWO = 0.999
ADAM_EPSILON = 1e-06
WEIGHT_DECAY = 0.01
LEARN_RATE = 0.3
NEGATIVE = -1e30
LOG2E = 1.4426950408889634
SCALE = HEAD ** (-0.5)
Q_ROWS = 256
G_COLS = 4 * HEAD
G_PAD = 4 * PAD
VMEM_LIMIT = 56 << 20

F32 = jnp.float32
BF16 = jnp.bfloat16
VM = pl.BlockSpec(memory_space=pltpu.VMEM)
SM = pl.BlockSpec(memory_space=pltpu.SMEM)
ANY = pl.BlockSpec(memory_space=pl.ANY)
MESH = pl.DeviceIdType.MESH


def dot_nn(a, b):
    return lax.dot_general(a, b, (((1,), (0,)), ((), ())), preferred_element_type=F32)


def dot_nt(a, b):
    return lax.dot_general(a, b, (((1,), (1,)), ((), ())), preferred_element_type=F32)


def dot_tn(a, b):
    return lax.dot_general(a, b, (((0,), (0,)), ((), ())), preferred_element_type=F32)


def cost(flops, moved):
    return pl.CostEstimate(flops=int(flops), bytes_accessed=int(moved), transcendentals=0)


def spread_matrix():
    source = lax.broadcasted_iota(jnp.int32, (G_COLS, G_PAD), 0)
    target = lax.broadcasted_iota(jnp.int32, (G_COLS, G_PAD), 1)
    return ((target // PAD) * HEAD + target % PAD == source) & (target % PAD < HEAD)


def pad_kernel(spread, wq, wo, wq_pad, wo_pad):
    for source, target in ((wq, wq_pad), (wo, wo_pad)):
        for g in range(target.shape[1] // G_PAD):
            target[:, g * G_PAD : (g + 1) * G_PAD] = dot_nn(
                source[:, g * G_COLS : (g + 1) * G_COLS], spread[...]
            ).astype(BF16)


def pad_weights(wq, wo, spread):
    depth = wq.shape[0]
    return pl.pallas_call(
        pad_kernel,
        out_shape=[
            jax.ShapeDtypeStruct((depth, w.shape[1] // G_COLS * G_PAD), BF16) for w in (wq, wo)
        ],
        in_specs=[VM] * 3,
        out_specs=[VM] * 2,
        compiler_params=pltpu.CompilerParams(vmem_limit_bytes=VMEM_LIMIT),
        cost_estimate=cost(6 * depth * G_COLS * G_PAD, 8 << 20),
        name="pad_weights",
    )(spread, wq, wo)


def swap_halves(values):
    lane = lax.broadcasted_iota(jnp.int32, values.shape, 1)
    return jnp.where(
        lane < HEAD // 2,
        pltpu.roll(values, PAD - HEAD // 2, 1),
        pltpu.roll(values, HEAD // 2, 1),
    )


def permuted(axis, bit):
    return {axis: lax.axis_index(axis) ^ bit}


class Remote:
    def __init__(self, copy):
        self.copy = copy
        self.landed = False

    def wait_recv(self):
        if not self.landed:
            self.copy.wait_recv()
        self.landed = True


class Frame:
    def __init__(self, names, refs):
        self.refs = dict(zip(names, refs))
        self.loading, self.remotes, self.storing = {}, [], []
        self.next_local = 0

    def __getitem__(self, name):
        return self.refs[name]

    def meet(self, peers):
        barrier = pltpu.get_barrier_semaphore()
        for peer in peers:
            pl.semaphore_signal(barrier, inc=1, device_id=peer, device_id_type=MESH)
        pl.semaphore_wait(barrier, len(peers))

    def local(self, source, target):
        copy = pltpu.make_async_copy(source, target, self.refs["local_sem"].at[self.next_local])
        self.next_local += 1
        copy.start()
        return copy

    def load(self, *names):
        for name in names:
            self.loading[name] = self.local(self.refs["any_" + name], self.refs[name])

    def ready(self, *names):
        for name in names:
            if name in self.loading:
                self.loading.pop(name).wait()

    def store(self, source, target):
        self.storing.append(self.local(source, target))

    def flush(self, name):
        self.store(self.refs[name], self.refs["any_" + name])

    def remote(self, source, target, peer):
        n = len(self.remotes)
        copy = pltpu.make_async_remote_copy(
            src_ref=source,
            dst_ref=target,
            send_sem=self.refs["send_sem"].at[n],
            recv_sem=self.refs["recv_sem"].at[n],
            device_id=peer,
            device_id_type=MESH,
        )
        copy.start()
        self.remotes.append(Remote(copy))
        return self.remotes[-1]

    def finish(self):
        for remote in self.remotes:
            remote.copy.wait_send()
            remote.wait_recv()
        for copy in self.storing:
            copy.wait()


def frame_call(body, name, inputs, outputs, scratch, flops, collective_id, n_sems=40):
    names, specs, arrays = [], [], []
    spec_of = {"vmem": VM, "smem": SM, "any": ANY, "load": ANY, "flush": ANY}
    for key, (array, kind) in inputs.items():
        names.append("any_" + key if kind == "load" else key)
        specs.append(spec_of[kind])
        arrays.append(array)
    out_specs, out_shapes = [], []
    for key, (shape, kind) in outputs.items():
        names.append("any_" + key if kind == "flush" else key)
        out_specs.append(spec_of[kind])
        out_shapes.append(shape)
    shapes = []
    for table, kind_of in ((inputs, "load"), (outputs, "flush")):
        for key, (array, kind) in table.items():
            if kind == kind_of:
                names.append(key)
                shapes.append(pltpu.VMEM(array.shape, array.dtype))
    for key, shape in scratch.items():
        names.append(key)
        shapes.append(shape)
    for key in ("local_sem", "send_sem", "recv_sem"):
        names.append(key)
        shapes.append(pltpu.SemaphoreType.DMA((n_sems,)))

    def kernel(*refs):
        frame = Frame(names, refs)
        body(frame)
        frame.finish()

    moved = sum(a.size * a.dtype.itemsize for a in arrays)
    results = pl.pallas_call(
        kernel,
        out_shape=out_shapes,
        in_specs=specs,
        out_specs=out_specs,
        scratch_shapes=shapes,
        compiler_params=pltpu.CompilerParams(
            vmem_limit_bytes=VMEM_LIMIT, collective_id=collective_id, has_side_effects=True
        ),
        cost_estimate=cost(flops, moved),
        name=name,
    )(*arrays)
    return dict(zip(outputs, results))


def half_peers(nb):
    return [(r, permuted("tensor", r)) for r in range(1, nb)]


def rows_of(c):
    return pl.ds(c * Q_ROWS, Q_ROWS)


def bits_down(size):
    bits = []
    bit = size // 2
    while bit:
        bits.append(bit)
        bit //= 2
    return bits


def prologue_kernel(n_z, n_t, blk, *refs):
    tokens, cotangent, qkv, outw, gains = refs[:5]
    xs, c_far, wq, wo, gain_sum = refs[5:10]
    held, got, own_sem, tok_send, tok_recv, z_send, z_recv, x_send, x_recv, g_send, g_recv = refs[10:]
    d, t = lax.axis_index("dp"), lax.axis_index("tensor")
    z, x = d // 2, lax.rem(d, 2)
    bits = bits_down(n_t)

    def at_z(k):
        return {"dp": lax.rem(z + k, n_z) * 2 + x}

    other_x = {"dp": z * 2 + (1 - x)}

    def at_t(bit):
        return {"tensor": t ^ bit}

    barrier = pltpu.get_barrier_semaphore()
    peers = [at_z(k) for k in range(1, n_z)] + [other_x] + [at_t(bit) for bit in bits]
    for peer in peers:
        pl.semaphore_signal(barrier, inc=1, device_id=peer, device_id_type=MESH)
    pl.semaphore_wait(barrier, len(peers))

    def send(src, dst, send_sem, recv_sem, peer):
        copy = pltpu.make_async_remote_copy(
            src_ref=src,
            dst_ref=dst,
            send_sem=send_sem,
            recv_sem=recv_sem,
            device_id=peer,
            device_id_type=MESH,
        )
        copy.start()
        return copy

    def owned(k):
        return pl.ds(pl.multiple_of((lax.rem(z + n_z - k, n_z) * 2 + x) * blk, 16), blk)

    pending = []
    held[0, :, :] = gains[...]
    stages = [at_t(bit) for bit in bits] + [other_x]
    gain_copy = send(held.at[0], got.at[0], g_send.at[0], g_recv.at[0], stages[0])
    token_copies = {}
    for bit in bits:
        token_copies[bit] = send(
            tokens, xs.at[bit], tok_send.at[bit], tok_recv.at[bit], at_t(bit)
        )
    locals_ = [
        pltpu.make_async_copy(qkv, wq.at[owned(0)], own_sem.at[0]),
        pltpu.make_async_copy(outw, wo.at[owned(0)], own_sem.at[1]),
        pltpu.make_async_copy(tokens, xs.at[0], own_sem.at[2]),
    ]
    for copy in locals_:
        copy.start()
    z_copies, x_copies = {}, {}
    for k in range(1, n_z):
        z_copies[0, k] = send(qkv, wq.at[owned(0)], z_send.at[0, k], z_recv.at[0, k], at_z(k))
    x_copies[0, 0] = send(qkv, wq.at[owned(0)], x_send.at[0, 0], x_recv.at[0, 0], other_x)
    for stage in range(len(stages)):
        gain_copy.wait()
        held[stage + 1, :, :] = held[stage, :, :] + got[stage, :, :]
        if stage + 1 < len(stages):
            gain_copy = send(
                held.at[stage + 1],
                got.at[stage + 1],
                g_send.at[stage + 1],
                g_recv.at[stage + 1],
                stages[stage + 1],
            )
    last = len(stages)
    gain_z = [
        send(held.at[last], got.at[last + k - 1], g_send.at[last + k - 1], g_recv.at[last + k - 1], at_z(k))
        for k in range(1, n_z)
    ]
    for k in range(1, n_z):
        z_copies[1, k] = send(outw, wo.at[owned(0)], z_send.at[1, k], z_recv.at[1, k], at_z(k))
    for which, whole in ((0, wq), (1, wo)):
        if which == 1:
            x_copies[1, 0] = send(outw, wo.at[owned(0)], x_send.at[1, 0], x_recv.at[1, 0], other_x)
        for k in range(1, n_z):
            z_copies[which, k].wait_recv()
            x_copies[which, k] = send(
                whole.at[owned(k)],
                whole.at[owned(k)],
                x_send.at[which, k],
                x_recv.at[which, k],
                other_x,
            )
    arrived = [0]
    for bit in bits:
        for r in list(arrived):
            if r:
                token_copies[r ^ bit] = send(
                    xs.at[r], xs.at[r ^ bit], tok_send.at[r ^ bit], tok_recv.at[r ^ bit], at_t(bit)
                )
        for r in list(arrived):
            token_copies[r ^ bit].wait_recv()
            arrived.append(r ^ bit)
    c_copy = send(cotangent, c_far, tok_send.at[0], tok_recv.at[0], at_t(n_t // 2))
    total = held[last, :, :]
    for k in range(1, n_z):
        gain_z[k - 1].wait()
        total = total + got[last + k - 1, :, :]
    gain_sum[...] = total
    for copy in token_copies.values():
        copy.wait_send()
    for copy in z_copies.values():
        copy.wait_send()
    for copy in x_copies.values():
        copy.wait()
    for copy in locals_:
        copy.wait()
    c_copy.wait()


def prologue(tokens, cotangent, qkv, outw, gains, n_z, n_t, n_dp):
    blk = qkv.shape[0]
    n_gain = len(bits_down(n_t)) + 1 + n_z - 1
    dma = pltpu.SemaphoreType.DMA
    return pl.pallas_call(
        functools.partial(prologue_kernel, n_z, n_t, blk),
        out_shape=[
            jax.ShapeDtypeStruct((n_t,) + tokens.shape, BF16),
            jax.ShapeDtypeStruct(cotangent.shape, BF16),
            jax.ShapeDtypeStruct((blk * n_dp, qkv.shape[1]), BF16),
            jax.ShapeDtypeStruct((blk * n_dp, outw.shape[1]), BF16),
            jax.ShapeDtypeStruct(gains.shape, F32),
        ],
        in_specs=[ANY, ANY, ANY, ANY, VM],
        out_specs=[ANY, ANY, ANY, ANY, VM],
        scratch_shapes=[
            pltpu.VMEM((n_gain + 1,) + gains.shape, F32),
            pltpu.VMEM((n_gain,) + gains.shape, F32),
            dma((3,)),
            dma((n_t,)),
            dma((n_t,)),
            dma((2, n_z)),
            dma((2, n_z)),
            dma((2, n_z)),
            dma((2, n_z)),
            dma((n_gain,)),
            dma((n_gain,)),
        ],
        compiler_params=pltpu.CompilerParams(
            collective_id=0, has_side_effects=True, vmem_limit_bytes=4 << 20
        ),
        cost_estimate=cost(0, 60 << 20),
        name="gather_tokens_and_weights",
    )(tokens, cotangent, qkv, outw, gains)


def attention_rows(k, tag, i, length, kv):
    qkvp, att, lse = k[tag + "qkvp"], k[tag + "att"], k[tag + "lse"]
    n = (i + 1) * Q_ROWS
    rows = slice(i * Q_ROWS, n)
    lane = lax.broadcasted_iota(jnp.int32, (Q_ROWS, PAD), 1)

    def one_head(h, log_totals):
        group = h // GROUP
        q_col = pl.ds(pl.multiple_of((4 * group + h % GROUP) * PAD, PAD), PAD)
        k_col = pl.ds(pl.multiple_of((4 * group + 2) * PAD, PAD), PAD)
        v_col = pl.ds(pl.multiple_of((4 * group + 3) * PAD, PAD), PAD)
        a_col = pl.ds(pl.multiple_of(h * PAD, PAD), PAD)
        s = dot_nt(qkvp[rows, q_col], qkvp[0:n, k_col])
        row_ids = lax.broadcasted_iota(jnp.int32, (Q_ROWS, 1), 0) + i * Q_ROWS + 1
        limit = jnp.minimum(row_ids, length)
        col_ids = lax.broadcasted_iota(jnp.int32, (Q_ROWS, n), 1)
        s = jnp.where(col_ids < limit, s, NEGATIVE)
        top = jnp.max(s, axis=-1, keepdims=True)
        e = jnp.exp2((s - top) * (SCALE * LOG2E))
        total = jnp.sum(e, axis=-1, keepdims=True)
        p = (e * (1.0 / total)).astype(BF16)
        att[rows, a_col] = dot_nn(p, qkvp[0:n, v_col]).astype(BF16)
        log_total = top * (SCALE * LOG2E) + jnp.log2(total)
        return jnp.where(lane == h, log_total, log_totals)

    lse[rows, :] = lax.fori_loop(0, kv * GROUP, one_head, jnp.zeros((Q_ROWS, PAD), F32))


def attention_forward_body(nb, rows_each, kv, k):
    local = lax.rem(lax.axis_index("tensor"), nb)
    seq_len = nb * rows_each
    per_block = rows_each // Q_ROWS
    over = permuted("tensor", nb)
    far_load = k.local(k["xs"].at[pl.ds(nb, nb)], k["far_x"])
    k.load("w_qkv", "cos_t", "sin_t", "w_out")
    near_load = k.local(k["xs"].at[pl.ds(0, nb)], k["near_x"])
    k.meet([over] + [peer for _, peer in half_peers(nb)])
    landing = []
    waiting = []
    chunk = 32
    for tag, length in (("far_", k["lengths"][1]), ("near_", k["lengths"][0])):
        x_ref, normed, qkvp = k[tag + "x"], k[tag + "normed"], k[tag + "qkvp"]
        parts, got = k[tag + "parts"], k[tag + "got"]
        (far_load if tag == "far_" else near_load).wait()
        for r in range(nb):
            base = (local ^ r) * rows_each

            def norm_rows(i, carry):
                v = x_ref[r, pl.ds(pl.multiple_of(i * chunk, chunk), chunk), :].astype(F32)
                inv = lax.rsqrt(jnp.mean(v * v, axis=-1, keepdims=True) + NORM_EPSILON)
                normed[pl.ds(pl.multiple_of(base + i * chunk, chunk), chunk), :] = (
                    v * inv * k["gain_one"][...]
                ).astype(BF16)
                return carry

            lax.fori_loop(0, rows_each // chunk, norm_rows, 0)
        k.flush(tag + "normed")
        k.ready("w_qkv", "cos_t", "sin_t")
        for i in range(seq_len // Q_ROWS):
            rows = slice(i * Q_ROWS, (i + 1) * Q_ROWS)
            for j in range(kv):
                proj = dot_nn(normed[rows, :], k["w_qkv"][:, j * G_PAD : (j + 1) * G_PAD])
                for h in range(4):
                    part = proj[:, h * PAD : (h + 1) * PAD]
                    if h < 3:
                        part = part * k["cos_t"][rows, :] + swap_halves(part) * k["sin_t"][rows, :]
                    qkvp[rows, (4 * j + h) * PAD : (4 * j + h + 1) * PAD] = part.astype(BF16)
        k.flush(tag + "qkvp")
        k.ready("w_out")
        for c in range(per_block):
            rows = slice(c * Q_ROWS, (c + 1) * Q_ROWS)
            for b in range(nb):
                i = b * per_block + c
                attention_rows(k, tag, i, length, kv)
                part = dot_nt(k[tag + "att"][i * Q_ROWS : (i + 1) * Q_ROWS, :], k["w_out"][...])
                parts[local ^ b, rows, :] = part.astype(BF16)
                if waiting:
                    waiting.pop()()
            copies = [
                k.remote(parts.at[r, rows_of(c)], got.at[r - 1, rows_of(c)], peer)
                for r, peer in half_peers(nb)
            ]

            def complete(rows=rows, c=c, copies=copies, parts=parts, got=got, tag=tag):
                total = parts[0, rows, :].astype(F32)
                for r, copy in enumerate(copies):
                    copy.wait_recv()
                    total = total + got[r, rows, :].astype(F32)
                if tag == "far_":
                    parts[0, rows, :] = total.astype(BF16)
                    landing.append(
                        k.remote(parts.at[0, rows_of(c)], k["landed"].at[rows_of(c)], over)
                    )
                else:
                    k["residual"][rows, :] = k["near_x"][0, rows, :].astype(F32) + total

            waiting.append(complete)
        k.flush(tag + "att")
        k.flush(tag + "lse")
    waiting.pop()()
    for c in range(per_block):
        landing[c].wait_recv()

        def residual_rows(i, carry):
            rows = pl.ds(pl.multiple_of(c * Q_ROWS + i * chunk, chunk), chunk)
            v = k["residual"][rows, :] + k["landed"][rows, :].astype(F32)
            k["residual"][rows, :] = v
            inv = lax.rsqrt(jnp.mean(v * v, axis=-1, keepdims=True) + NORM_EPSILON)
            k["normed_two"][rows, :] = (v * inv * k["gain_two"][...]).astype(BF16)
            return carry

        lax.fori_loop(0, Q_ROWS // chunk, residual_rows, 0)
    k.flush("residual")
    k.flush("normed_two")


def attention_forward(xs, lengths, gains, w_qkv, w_out, cos_t, sin_t, collective_id):
    n_t, rows_each, width = xs.shape
    nb = n_t // 2
    seq_len = nb * rows_each
    kv = w_qkv.shape[1] // G_PAD
    heads = kv * GROUP
    sds = jax.ShapeDtypeStruct
    outputs = {}
    for tag in ("far_", "near_"):
        outputs[tag + "normed"] = (sds((seq_len, width), BF16), "flush")
        outputs[tag + "qkvp"] = (sds((seq_len, kv * G_PAD), BF16), "flush")
        outputs[tag + "att"] = (sds((seq_len, heads * PAD), BF16), "flush")
        outputs[tag + "lse"] = (sds((seq_len, PAD), F32), "flush")
    outputs["residual"] = (sds((rows_each, width), F32), "flush")
    outputs["normed_two"] = (sds((rows_each, width), BF16), "flush")
    block = pltpu.VMEM((nb, rows_each, width), BF16)
    others = pltpu.VMEM((nb - 1, rows_each, width), BF16)
    return frame_call(
        functools.partial(attention_forward_body, nb, rows_each, kv),
        "attention_forward",
        {
            "lengths": (lengths, "smem"),
            "gain_one": (gains[0:1], "vmem"),
            "gain_two": (gains[1:2], "vmem"),
            "xs": (xs, "any"),
            "w_qkv": (w_qkv, "load"),
            "w_out": (w_out, "load"),
            "cos_t": (cos_t, "load"),
            "sin_t": (sin_t, "load"),
        },
        outputs,
        {
            "near_x": block,
            "far_x": block,
            "far_parts": block,
            "near_parts": block,
            "far_got": others,
            "near_got": others,
            "landed": pltpu.VMEM((rows_each, width), BF16),
        },
        4 * seq_len * width * (kv * G_PAD + heads * PAD) + heads * seq_len * seq_len * 8 * 256,
        collective_id,
    )


def feed_forward_body(nb, rows_each, k):
    over = permuted("tensor", nb)
    peers = half_peers(nb)
    per_block = rows_each // Q_ROWS
    w = k["w"]
    width = w.shape[1]
    near_n, near_c, far_n, far_c = k["near_n"], k["near_c"], k["far_n"], k["far_c"]
    own_n = k.local(k["own_n"], near_n.at[0])
    own_c = k.local(k["own_c"], near_c.at[0])
    k.load("w")
    own_far_c = k.local(k["own_far_c"], far_c.at[0])
    k.meet([over] + [peer for _, peer in peers])
    far_first = [
        k.remote(k["own_n"].at[rows_of(c)], far_n.at[0, rows_of(c)], over) for c in range(per_block)
    ]
    n_copies = [k.remote(k["own_n"], near_n.at[r], peer) for r, peer in peers]
    c_copies = [k.remote(k["own_c"], near_c.at[r], peer) for r, peer in peers]
    far_c_copies = [k.remote(k["own_far_c"], far_c.at[r], peer) for r, peer in peers]
    own_n.wait()
    own_c.wait()
    k.ready("w")

    def rows_step(side, r, c):
        rows = slice(c * Q_ROWS, (c + 1) * Q_ROWS)
        start = (0 if side == "near_" else nb * rows_each) + r * rows_each + c * Q_ROWS
        kept = slice(start, start + Q_ROWS)
        n = k[side + "n"][r, rows, :]
        gate = dot_nn(n, w[0])
        up = dot_nn(n, w[1])
        sig = 1.0 / (1.0 + jnp.exp(-gate))
        silu = gate * sig
        hid = (silu * up).astype(BF16)
        k["hidden"][kept, :] = hid
        dh = dot_nn(k[side + "c"][r, rows, :], w[2])
        dg = (dh * up * sig * (1.0 + gate * (1.0 - sig))).astype(BF16)
        du = (dh * silu).astype(BF16)
        k["d_gate"][kept, :] = dg
        k["d_up"][kept, :] = du
        k[side + "grad"][r, rows, :] = (dot_nt(dg, w[0]) + dot_nt(du, w[1])).astype(BF16)
        k[side + "out"][r, rows, :] = dot_nt(hid, w[2]).astype(BF16)

    for r in range(nb):
        if r:
            n_copies[r - 1].wait_recv()
            c_copies[r - 1].wait_recv()
        for c in range(per_block):
            rows_step("near_", r, c)
        for name in ("grad", "out"):
            part = k["near_" + name].at[r]
            if r:
                k.remote(part, k["near_got_" + name].at[r - 1], peers[r - 1][1])
            else:
                k.store(part, k["near_own_" + name])
    own_far_c.wait()
    for copy in far_c_copies:
        copy.wait_recv()
    landing = []
    for c in range(per_block):
        rows = slice(c * Q_ROWS, (c + 1) * Q_ROWS)
        far_first[c].wait_recv()
        passed = [
            k.remote(far_n.at[0, rows_of(c)], far_n.at[r, rows_of(c)], peer) for r, peer in peers
        ]
        rows_step("far_", 0, c)
        copies = []
        for r, peer in peers:
            passed[r - 1].wait_recv()
            rows_step("far_", r, c)
            copies.append(
                k.remote(
                    k["far_grad"].at[r, rows_of(c)], k["far_got_grad"].at[r - 1, rows_of(c)], peer
                )
            )
        total = k["far_grad"][0, rows, :].astype(F32)
        for r, copy in enumerate(copies):
            copy.wait_recv()
            total = total + k["far_got_grad"][r, rows, :].astype(F32)
        k["far_grad"][0, rows, :] = total.astype(BF16)
        landing.append(k.remote(k["far_grad"].at[0, rows_of(c)], k["landed"].at[rows_of(c)], over))
    k.store(k["far_out"].at[0], k["far_own_out"])
    for r, peer in peers:
        k.remote(k["far_out"].at[r], k["far_got_out"].at[r - 1], peer)
    half = nb * rows_each
    for which in (2, 0, 1):
        name = "c" if which == 2 else "n"
        right = k[("d_gate", "d_up", "hidden")[which]]

        def col_step(i, carry):
            cols = pl.ds(pl.multiple_of(i * G_COLS, G_COLS), G_COLS)
            total = None
            for s, side in enumerate(("near_", "far_")):
                for r in range(nb):
                    start = s * half + r * rows_each
                    term = dot_tn(k[side + name][r, :, cols], right[start : start + rows_each, :])
                    total = term if total is None else total + term
            w[which, cols, :] = total.astype(BF16)
            return carry

        lax.fori_loop(0, width // G_COLS, col_step, 0)
        k.store(w.at[which], k["grads"].at[which])


def feed_forward(normed_two, cotangent, c_far, w, nb, collective_id):
    rows_each, width = normed_two.shape
    units = w.shape[2]
    sds = jax.ShapeDtypeStruct
    block = pltpu.VMEM((nb, rows_each, width), BF16)
    kept = pltpu.VMEM((2 * nb * rows_each, units), BF16)
    own = (sds((rows_each, width), BF16), "any")
    got = (sds((nb - 1, rows_each, width), BF16), "any")
    return frame_call(
        functools.partial(feed_forward_body, nb, rows_each),
        "feed_forward",
        {
            "own_n": (normed_two, "any"),
            "own_c": (cotangent, "any"),
            "own_far_c": (c_far, "any"),
            "w": (w, "load"),
        },
        {
            "grads": (sds(w.shape, BF16), "any"),
            "near_own_grad": own,
            "near_got_grad": got,
            "landed": own,
            "near_own_out": own,
            "near_got_out": got,
            "far_own_out": own,
            "far_got_out": got,
        },
        {
            "near_n": block,
            "far_n": block,
            "near_c": block,
            "far_c": block,
            "hidden": kept,
            "d_gate": kept,
            "d_up": kept,
            "near_grad": block,
            "far_grad": block,
            "near_out": block,
            "far_out": block,
            "far_got_grad": pltpu.VMEM((nb - 1, rows_each, width), BF16),
        },
        36 * nb * rows_each * width * units,
        collective_id,
    )


def attention_backward_rows(k, tag, i, length, kv):
    qkvp, dproj, datt, lse = k[tag + "qkvp"], k[tag + "dproj"], k["datt"], k[tag + "lse"]
    n = (i + 1) * Q_ROWS
    rows = slice(i * Q_ROWS, n)
    lane = lax.broadcasted_iota(jnp.int32, (Q_ROWS, PAD), 1)

    def one_head(h, carry):
        group = h // GROUP
        q_col = pl.ds(pl.multiple_of((4 * group + h % GROUP) * PAD, PAD), PAD)
        k_col = pl.ds(pl.multiple_of((4 * group + 2) * PAD, PAD), PAD)
        v_col = pl.ds(pl.multiple_of((4 * group + 3) * PAD, PAD), PAD)
        a_col = pl.ds(pl.multiple_of(h * PAD, PAD), PAD)
        q = qkvp[rows, q_col]
        keys = qkvp[0:n, k_col]
        do = datt[rows, a_col]
        row_lse = jnp.sum(jnp.where(lane == h, lse[rows, :], 0.0), axis=-1, keepdims=True)
        s = dot_nt(q, keys)
        row_ids = lax.broadcasted_iota(jnp.int32, (Q_ROWS, 1), 0) + i * Q_ROWS + 1
        limit = jnp.minimum(row_ids, length)
        col_ids = lax.broadcasted_iota(jnp.int32, (Q_ROWS, n), 1)
        s = jnp.where(col_ids < limit, s, NEGATIVE)
        p = jnp.exp2(s * (SCALE * LOG2E) - row_lse)
        dp = dot_nt(do, qkvp[0:n, v_col])
        inner = jnp.sum(p * dp, axis=-1, keepdims=True)
        ds = (p * (dp - inner)).astype(BF16)
        k["dv"][group, 0:n, :] += dot_tn(p.astype(BF16), do)
        k["dk"][group, 0:n, :] += dot_tn(ds, q)
        dq = dot_nn(ds, keys) * SCALE
        dproj[rows, q_col] = unrotate(k, dq, rows).astype(BF16)
        return carry

    lax.fori_loop(0, kv * GROUP, one_head, 0)


def unrotate(k, grad, rows):
    return grad * k["cos_t"][rows, :] - swap_halves(grad) * k["sin_t"][rows, :]


def attention_backward_body(nb, rows_each, kv, n_z, blk, k):
    d = lax.axis_index("dp")
    z, x = d // 2, lax.rem(d, 2)
    local = lax.rem(lax.axis_index("tensor"), nb)
    seq_len = nb * rows_each
    per_block = rows_each // Q_ROWS
    over = permuted("tensor", nb)
    other_x = permuted("dp", 1)
    peers = half_peers(nb)
    own_a = k.local(k["own_a"], k["near_a"].at[0])
    k.load("w_out", "near_qkvp", "near_lse", "cos_t", "sin_t", "w_qkv", "far_qkvp", "far_lse")
    k.load("spread", "near_att", "far_att", "near_normed", "far_normed")
    k.meet([over, other_x] + [peer for _, peer in peers])
    far_first = [
        k.remote(k["own_a"].at[rows_of(c)], k["far_a"].at[0, rows_of(c)], over)
        for c in range(per_block)
    ]
    near_copies = [k.remote(k["own_a"], k["near_a"].at[r], peer) for r, peer in peers]
    own_a.wait()
    for copy in near_copies:
        copy.wait_recv()
    for tag, length in (("near_", k["lengths"][0]), ("far_", k["lengths"][1])):
        blocks, parts, dproj = k[tag + "a"], k[tag + "parts"], k[tag + "dproj"]
        k["dk"][...] = jnp.zeros_like(k["dk"])
        k["dv"][...] = jnp.zeros_like(k["dv"])
        k.ready("w_out", "cos_t", "sin_t", tag + "qkvp", tag + "lse")
        for c in range(per_block):
            rows = slice(c * Q_ROWS, (c + 1) * Q_ROWS)
            if tag == "far_":
                far_first[c].wait_recv()
                passed = [
                    k.remote(blocks.at[0, rows_of(c)], blocks.at[r, rows_of(c)], peer)
                    for r, peer in peers
                ]
                for copy in passed:
                    copy.wait_recv()
            for b in range(nb):
                i = b * per_block + c
                k["datt"][i * Q_ROWS : (i + 1) * Q_ROWS, :] = dot_nn(
                    blocks[local ^ b, rows, :], k["w_out"][...]
                ).astype(BF16)
                attention_backward_rows(k, tag, i, length, kv)
        for j in range(kv):
            k_col = slice((4 * j + 2) * PAD, (4 * j + 3) * PAD)
            v_col = slice((4 * j + 3) * PAD, (4 * j + 4) * PAD)
            for i in range(seq_len // Q_ROWS):
                rows = slice(i * Q_ROWS, (i + 1) * Q_ROWS)
                dproj[rows, k_col] = unrotate(k, k["dk"][j, rows, :] * SCALE, rows).astype(BF16)
                dproj[rows, v_col] = k["dv"][j, rows, :].astype(BF16)
        k.ready("w_qkv")
        for c in range(per_block):
            rows = slice(c * Q_ROWS, (c + 1) * Q_ROWS)
            for b in range(nb):
                i = b * per_block + c
                part = dot_nt(dproj[i * Q_ROWS : (i + 1) * Q_ROWS, :], k["w_qkv"][...])
                parts[local ^ b, rows, :] = part.astype(BF16)
            if tag == "near_":
                for r, peer in peers:
                    k.remote(parts.at[r, rows_of(c)], k["near_got"].at[r - 1, rows_of(c)], peer)
            else:
                copies = [
                    k.remote(parts.at[r, rows_of(c)], k["far_got"].at[r - 1, rows_of(c)], peer)
                    for r, peer in peers
                ]
                total = parts[0, rows, :].astype(F32)
                for r, copy in enumerate(copies):
                    copy.wait_recv()
                    total = total + k["far_got"][r, rows, :].astype(F32)
                parts[0, rows, :] = total.astype(BF16)
                k.remote(parts.at[0, rows_of(c)], k["landed"].at[rows_of(c)], over)
        if tag == "near_":
            k.store(parts.at[0], k["near_own"])
    k.ready("spread", "near_att", "far_att", "near_normed", "far_normed")
    width = k["w_qkv"].shape[0]
    for which in range(kv + 1):

        def chunk(c, carry):
            cols = pl.ds(pl.multiple_of(c * G_COLS, G_COLS), G_COLS)
            total = None
            if which == 0:
                wide = k["near_att"].shape[1]
                for tag in ("near_", "far_"):
                    for r in range(nb):
                        start = pl.multiple_of((local ^ r) * rows_each, rows_each)
                        term = dot_tn(
                            k[tag + "a"][r, :, cols], k[tag + "att"][pl.ds(start, rows_each), :]
                        )
                        total = term if total is None else total + term
                compact = dot_nt(total.astype(BF16), k["spread"][:, :wide])
            else:
                part = slice((which - 1) * G_PAD, which * G_PAD)
                total = dot_tn(k["near_normed"][:, cols], k["near_dproj"][:, part])
                total += dot_tn(k["far_normed"][:, cols], k["far_dproj"][:, part])
                compact = dot_nt(total.astype(BF16), k["spread"][...])
            compact = compact.astype(BF16)
            for b in range(G_COLS // blk):
                owner = c * (G_COLS // blk) + b
                shift = lax.rem(owner // 2 + n_z - z, n_z)
                value = compact[b * blk : (b + 1) * blk, :]

                @pl.when(x == lax.rem(owner, 2))
                def _():
                    k["same"][which, shift, :, :] = value

                @pl.when(x != lax.rem(owner, 2))
                def _():
                    k["other"][which, shift, :, :] = value

            return carry

        lax.fori_loop(0, width // G_COLS, chunk, 0)
        k.remote(k["other"].at[which], k["arrived"].at[which], other_x)
    k.flush("same")


def attention_backward(attention_grad, lengths, fwd, w_qkv, w_out, tables, spread, nb, n_z, blk, collective_id):
    rows_each, width = attention_grad.shape
    seq_len = nb * rows_each
    kv = w_qkv.shape[1] // G_PAD
    heads = kv * GROUP
    sds = jax.ShapeDtypeStruct
    inputs = {
        "lengths": (lengths, "smem"),
        "own_a": (attention_grad, "any"),
        "w_qkv": (w_qkv, "load"),
        "w_out": (w_out, "load"),
        "cos_t": (tables[0], "load"),
        "sin_t": (tables[1], "load"),
        "spread": (spread, "load"),
    }
    for tag in ("near_", "far_"):
        for key in ("qkvp", "lse", "att", "normed"):
            inputs[tag + key] = (fwd[tag + key], "load")
    block = pltpu.VMEM((nb, rows_each, width), BF16)
    sums = sds((kv + 1, n_z, blk, G_COLS), BF16)
    own = (sds((rows_each, width), BF16), "any")
    return frame_call(
        functools.partial(attention_backward_body, nb, rows_each, kv, n_z, blk),
        "attention_backward",
        inputs,
        {
            "near_own": own,
            "near_got": (sds((nb - 1, rows_each, width), BF16), "any"),
            "landed": own,
            "same": (sums, "flush"),
            "arrived": (sums, "any"),
        },
        {
            "near_a": block,
            "far_a": block,
            "near_parts": block,
            "far_parts": block,
            "far_got": pltpu.VMEM((nb - 1, rows_each, width), BF16),
            "near_dproj": pltpu.VMEM((seq_len, kv * G_PAD), BF16),
            "far_dproj": pltpu.VMEM((seq_len, kv * G_PAD), BF16),
            "datt": pltpu.VMEM((seq_len, heads * PAD), BF16),
            "dk": pltpu.VMEM((kv, seq_len, PAD), F32),
            "dv": pltpu.VMEM((kv, seq_len, PAD), F32),
            "other": pltpu.VMEM(sums.shape, BF16),
        },
        8 * seq_len * width * (kv * G_PAD + heads * PAD) + heads * seq_len * seq_len * 20 * 256,
        collective_id,
    )


def all_peers(n_dp, n_t):
    d, t = lax.axis_index("dp"), lax.axis_index("tensor")
    return (
        [{"tensor": lax.rem(t + i, n_t)} for i in range(1, n_t)],
        [{"dp": lax.rem(d + i, n_dp)} for i in range(1, n_dp)],
    )


def share(k, buffer, me, peers):
    return [k.remote(buffer.at[me], buffer.at[me], peer) for peer in peers]


def sum_slots(buffer, copies):
    for copy in copies:
        copy.wait_recv()
    total = buffer[0, :, :]
    for i in range(1, len(copies) + 1):
        total = total + buffer[i, :, :]
    return total


def closing_sums_body(n_z, n_dp, n_t, nb, k):
    d, t = lax.axis_index("dp"), lax.axis_index("tensor")
    tensor_peers, dp_peers = all_peers(n_dp, n_t)
    at_z = [{"dp": lax.rem(d + 2 * i, n_dp)} for i in range(1, n_z)]
    same, other, narrow, arrived = k["same"], k["other"], k["narrow"], k["arrived"]
    k.load("same", "other")
    k["first"][t, :, :] = k["gains"][...]
    k.meet(tensor_peers + dp_peers)
    gain_copies = share(k, k["first"], t, tensor_peers)
    k.remote(k["far_out"], k["landed"], permuted("tensor", nb))
    k.ready("same", "other")
    n_which = same.shape[0]
    copies = {}
    for which in range(n_which):
        for i in range(1, n_z):
            held = same[which, i, :, :].astype(F32) + other[which, i, :, :].astype(F32)
            narrow[which, i, :, :] = held.astype(BF16)
            copies[which, i] = k.remote(
                narrow.at[which, i], arrived.at[which, i], at_z[i - 1]
            )
        if which == 0:
            k["second"][d, :, :] = sum_slots(k["first"], gain_copies)
            gain_copies = share(k, k["second"], d, dp_peers)
    for which in range(n_which):
        total = same[which, 0, :, :].astype(F32) + other[which, 0, :, :].astype(F32)
        for i in range(1, n_z):
            copies[which, i].wait_recv()
            total = total + arrived[which, i, :, :].astype(F32)
        k["sums"][which, :, :] = total
    k["gain_sums"][...] = sum_slots(k["second"], gain_copies)


def closing_sums(same, other, far_out, gains, n_z, n_dp, n_t, collective_id):
    n_which, _, blk, cols = same.shape
    sds = jax.ShapeDtypeStruct
    block = pltpu.VMEM(same.shape, BF16)
    return frame_call(
        functools.partial(closing_sums_body, n_z, n_dp, n_t, n_t // 2),
        "sum_attention_gradients",
        {
            "same": (same, "load"),
            "other": (other, "load"),
            "far_out": (far_out, "any"),
            "gains": (gains, "vmem"),
        },
        {
            "sums": (sds((n_which, blk, cols), F32), "vmem"),
            "landed": (sds(far_out.shape, BF16), "any"),
            "gain_sums": (sds(gains.shape, F32), "vmem"),
        },
        {
            "narrow": block,
            "arrived": block,
            "first": pltpu.VMEM((n_t,) + gains.shape, F32),
            "second": pltpu.VMEM((n_dp,) + gains.shape, F32),
        },
        0,
        collective_id,
        n_sems=n_which * n_z + n_dp + n_t + 4,
    )


def moments_kernel(names, kv, *refs):
    keys = [key + suffix for suffix in ("", "_first", "_second") for key in names] + ["gradient"]
    keys += ["gain_sum"] if "gains" in names else []
    keys += ["next_" + key + suffix for suffix in ("_first", "_second") for key in names]
    keys += ["update_" + key for key in names] + ["squares"]
    k = dict(zip(keys, refs))
    correct_one = 1.0 / (1.0 - BETA_ONE**STEP)
    correct_two = 1.0 / (1.0 - BETA_TWO**STEP)
    row = lax.broadcasted_iota(jnp.int32, (8, PAD), 0)
    lane = lax.broadcasted_iota(jnp.int32, (8, PAD), 1)
    squares = jnp.zeros((8, PAD), F32)
    gradient = k["gradient"]

    def step(name, index, gradient_of, rows, cols, number):
        tile = rows if rows % 32 else 32

        def one(i, carry):
            at = index + (pl.ds(pl.multiple_of(i * tile, tile) if rows > tile else 0, tile), slice(None))
            g = gradient_of(at)
            w = k[name][at]
            moment = BETA_ONE * k[name + "_first"][at] + (1.0 - BETA_ONE) * g
            square = BETA_TWO * k[name + "_second"][at] + (1.0 - BETA_TWO) * g * g
            k["next_" + name + "_first"][at] = moment
            k["next_" + name + "_second"][at] = square
            update = (moment * correct_one) / (
                jnp.sqrt(square * correct_two) + ADAM_EPSILON
            ) + WEIGHT_DECAY * w
            k["update_" + name][at] = update
            return (
                carry[0] + jnp.sum(w * w, axis=0, keepdims=True),
                carry[1] + jnp.sum(update * update, axis=0, keepdims=True),
            )

        zero = jnp.zeros((1, cols), F32)
        w_sum, u_sum = lax.fori_loop(0, rows // tile, one, (zero, zero))
        w_sum = jnp.sum(w_sum, axis=1, keepdims=True)
        u_sum = jnp.sum(u_sum, axis=1, keepdims=True)
        mark = lane == number
        return jnp.where(mark & (row == 0), w_sum, 0.0) + jnp.where(mark & (row == 1), u_sum, 0.0)

    def qkv_gradient(at):
        return jnp.concatenate([gradient[(1 + j,) + at] for j in range(kv)], axis=1)

    if "qkv" in names:
        squares += step("qkv", (), qkv_gradient, *k["qkv"].shape, 0)
    if "out" in names:
        rows, cols = k["out"].shape
        squares += step("out", (), lambda at: gradient[0, at[0], :cols], rows, cols, 1)
    if "gate_up" in names:
        for which in range(2):
            squares += step(
                "gate_up", (which,), lambda at: gradient[at].astype(F32), *k["gate_up"].shape[1:], 2 + which
            )
    if "down" in names:
        squares += step(
            "down", (), lambda at: gradient[(2,) + at].astype(F32), *k["down"].shape, 4
        )
    if "gains" in names:
        for which in range(2):
            squares += step(
                "gains", (which,), lambda at: k["gain_sum"][at], *k["gains"].shape[1:], 5 + which
            )
    k["squares"][...] = squares


def moments(weights, firsts, seconds, gradient, gain_sum, kv):
    names = list(weights)
    arrays = [table[key] for table in (weights, firsts, seconds) for key in names] + [gradient]
    arrays += [] if gain_sum is None else [gain_sum]
    sds = jax.ShapeDtypeStruct
    shapes = [sds(weights[key].shape, F32) for key in names]
    results = pl.pallas_call(
        functools.partial(moments_kernel, names, kv),
        out_shape=shapes * 3 + [sds((8, PAD), F32)],
        in_specs=[VM] * len(arrays),
        out_specs=[VM] * (3 * len(names) + 1),
        compiler_params=pltpu.CompilerParams(vmem_limit_bytes=VMEM_LIMIT),
        cost_estimate=cost(0, 14 << 20),
        name="moments",
    )(*arrays)
    n = len(names)
    return (
        dict(zip(names, results[:n])),
        dict(zip(names, results[n : 2 * n])),
        dict(zip(names, results[2 * n : 3 * n])),
        results[-1],
    )


def sum_squares_body(n_dp, n_t, k):
    d, t = lax.axis_index("dp"), lax.axis_index("tensor")
    tensor_peers, dp_peers = all_peers(n_dp, n_t)
    k["first"][t, :, :] = k["squares_one"][...] + k["squares_two"][...]
    k.meet(tensor_peers + dp_peers)
    copies = share(k, k["first"], t, tensor_peers)
    k["second"][d, :, :] = sum_slots(k["first"], copies)
    copies = share(k, k["second"], d, dp_peers)
    k["norms"][...] = jnp.sqrt(sum_slots(k["second"], copies))


def sum_squares(one, two, n_dp, n_t, collective_id):
    return frame_call(
        functools.partial(sum_squares_body, n_dp, n_t),
        "sum_squares",
        {"squares_one": (one, "vmem"), "squares_two": (two, "vmem")},
        {"norms": (jax.ShapeDtypeStruct(one.shape, F32), "vmem")},
        {
            "first": pltpu.VMEM((n_t,) + one.shape, F32),
            "second": pltpu.VMEM((n_dp,) + one.shape, F32),
        },
        0,
        collective_id,
        n_sems=n_dp + n_t,
    )["norms"]


def rms_norm(values, gain_row):
    return (
        values
        * lax.rsqrt(jnp.mean(values * values, axis=-1, keepdims=True) + NORM_EPSILON)
        * gain_row
    )


def rotary_tables():
    half = HEAD // 2
    frequency = ROPE_THETA ** (-(jnp.arange(half, dtype=F32) * (2.0 / HEAD)))
    angles = jnp.arange(SEQ_LEN, dtype=F32)[:, None] * frequency[None, :]
    cosine, sine = jnp.cos(angles), jnp.sin(angles)
    empty = jnp.zeros((SEQ_LEN, PAD - HEAD), F32)
    return (
        jnp.concatenate([cosine, cosine, empty], axis=1),
        jnp.concatenate([-sine, sine, empty], axis=1),
    )


def shards(
    tokens,
    cotangent,
    lengths,
    qkv_weight,
    out_weight,
    gate_up_weight,
    down_weight,
    norm_gains,
    qkv_first,
    out_first,
    gate_up_first,
    down_first,
    gains_first,
    qkv_second,
    out_second,
    gate_up_second,
    down_second,
    gains_second,
):
    rows_each, width = tokens.shape
    n_t = lax.axis_size("tensor")
    n_dp = lax.axis_size("dp")
    n_z = n_dp // 2
    nb = n_t // 2
    t = lax.axis_index("tensor")
    d = lax.axis_index("dp")
    mine = t // nb
    lengths = jnp.stack([lengths[mine], lengths[1 - mine]])
    spread = spread_matrix().astype(BF16)
    blk = qkv_weight.shape[0]
    kv = qkv_weight.shape[1] // G_COLS

    gain_cols = norm_gains.shape[1]
    gain_start = (d * n_t + t) * gain_cols
    gain_rows = lax.dynamic_update_slice(
        jnp.zeros((2, width), F32),
        norm_gains.astype(BF16).astype(F32),
        (0, gain_start),
    )
    out_half = out_weight.astype(BF16).T
    xs, c_far, wq, wo, gain_work = prologue(
        tokens, cotangent, qkv_weight.astype(BF16), out_half, gain_rows, n_z, n_t, n_dp
    )
    attention_gain, feedforward_gain = gain_work[0:1], gain_work[1:2]
    w_out_cols = out_half.shape[1]
    if w_out_cols % G_COLS:
        wo = jnp.pad(wo, ((0, 0), (0, -w_out_cols % G_COLS)))
    w_qkv, w_out = pad_weights(wq, wo, spread)
    w_out = w_out[:, : kv * GROUP * PAD]
    ffn_half = jnp.concatenate(
        [gate_up_weight.astype(BF16), down_weight.astype(BF16).T[None]], axis=0
    )
    w_ffn = lax.all_gather(ffn_half, "dp", axis=1, tiled=True)

    inputs = tokens.astype(F32)
    tables = rotary_tables()
    fwd = attention_forward(xs, lengths, gain_work, w_qkv, w_out, *tables, 1)
    residual = fwd["residual"]

    ff = feed_forward(fwd["normed_two"], cotangent, c_far, w_ffn, nb, 2)
    ffn_sum = lax.psum_scatter(ff["grads"], "dp", scatter_dimension=1, tiled=True)

    def total(*names):
        result = 0.0
        for name in names:
            array = ff[name].astype(F32)
            result = result + (array if array.ndim == 2 else jnp.sum(array, axis=0))
        return result

    normed_two_grad = total("near_own_grad", "near_got_grad", "landed")
    _, norm_pull = jax.vjp(rms_norm, residual, feedforward_gain)
    residual_part, ffn_gain_grad = norm_pull(normed_two_grad)
    residual_grad = cotangent.astype(F32) + residual_part
    bwd = attention_backward(
        residual_grad.astype(BF16), lengths, fwd, w_qkv, w_out, tables, spread, nb, n_z, blk, 3
    )
    near_grads = jnp.sum(bwd["near_got"].astype(F32), axis=0) + bwd["near_own"].astype(F32)
    normed_grad = near_grads + bwd["landed"].astype(F32)
    _, first_pull = jax.vjp(rms_norm, inputs, attention_gain)
    input_part, attention_gain_grad = first_pull(normed_grad)
    grad_tokens = residual_grad + input_part
    gain_grads = jnp.concatenate([attention_gain_grad, ffn_gain_grad], axis=0)
    far_out = total("far_own_out", "far_got_out").astype(BF16)
    closing = closing_sums(
        bwd["same"], bwd["arrived"], far_out, gain_grads.reshape(-1, PAD), n_z, n_dp, n_t, 4
    )
    layer_out = (
        residual + (total("near_own_out", "near_got_out") + closing["landed"].astype(F32))
    ).astype(BF16)
    gain_sum = lax.dynamic_slice(
        closing["gain_sums"].reshape(2, width), (0, gain_start), (2, gain_cols)
    )

    def lift(gains):
        return gains[:, None, :]

    gate_down = moments(
        {"gate_up": gate_up_weight, "down": down_weight.T},
        {"gate_up": gate_up_first, "down": down_first.T},
        {"gate_up": gate_up_second, "down": down_second.T},
        ffn_sum,
        None,
        kv,
    )
    attention = moments(
        {"qkv": qkv_weight, "out": out_weight.T, "gains": lift(norm_gains)},
        {"qkv": qkv_first, "out": out_first.T, "gains": lift(gains_first)},
        {"qkv": qkv_second, "out": out_second.T, "gains": lift(gains_second)},
        closing["sums"],
        lift(gain_sum),
        kv,
    )
    norms = sum_squares(gate_down[3], attention[3], n_dp, n_t, 5)
    scale = LEARN_RATE * (norms[0, :7] / norms[1, :7])
    first, second, update = ({**gate_down[i], **attention[i]} for i in range(3))
    for table in (first, second, update):
        table["gains"] = table["gains"][:, 0, :]
        table["out"] = table["out"].T
        table["down"] = table["down"].T
    new = (
        qkv_weight - scale[0] * update["qkv"],
        out_weight - scale[1] * update["out"],
        gate_up_weight - scale[2:4, None, None] * update["gate_up"],
        down_weight - scale[4] * update["down"],
        norm_gains - scale[5:7, None] * update["gains"],
    )
    names = ("qkv", "out", "gate_up", "down", "gains")
    return (
        layer_out,
        grad_tokens,
        *new,
        *[first[key] for key in names],
        *[second[key] for key in names],
        norms[0, :7],
        norms[1, :5],
        norms[1, 5:7],
    )


def solution(mesh):
    rows = P(("dp", "tensor"), None)
    gains = P(None, ("dp", "tensor"))
    weights = (P("dp", "tensor"), P("tensor", "dp"), P(None, "dp", "tensor"), P("tensor", "dp"), gains)
    in_specs = (rows, rows, P("dp")) + weights * 3
    out_specs = (rows, rows) + weights * 3 + (P(), P(), P())
    return jax.shard_map(shards, mesh=mesh, in_specs=in_specs, out_specs=out_specs, check_vma=False)
```

time: 1660 us -> 581 us (0.35)
  waiting for transfers between devices: 985 us -> 0.06 us
  Pallas kernels: 0 us -> 497 us
  matrix products: 246 us -> 0 us
  local copies, waits for them, and re-layouts: 178 us -> 13.6 us
  blocking collectives: 82.4 us -> 0 us
  other arithmetic: 125 us -> 45.7 us
    reduce_scatter x8 -> x1, waiting for transfers between devices: 564 us -> 0.01 us  [shards(): lax.psum_scatter(ff['grads'], 'dp', scatter_dimension=1, tiled=True)]
    pallas_call x0 -> x9, Pallas kernels: none -> 497 us  [the longest x5 364 us: frame_call(): pl.pallas_call(kernel, out_shape=out_shapes, in_specs=specs, out_specs=ou...]
    all_gather x8 -> x1, waiting for transfers between devices: 327 us -> 0.02 us  [shards(): w_ffn = lax.all_gather(ffn_half, 'dp', axis=1, tiled=True)]
    dot_general x43 -> x0, matrix products: 246 us -> none  [the longest x5 55.3 us: contract_cols(): lax.dot_general(left, right, (((1,), (1,)), ((), ())), preferred_element_...]
    dynamic_update_slice x12 -> x1, local copies, waits for them, and re-layouts: 119 us -> 0.16 us  [shards(): lax.dynamic_update_slice(jnp.zeros((2, width), F32), norm_gains.astype(BF...]
    unnamed x18 -> x2, waiting for transfers between devices: 93.7 us -> 0.03 us
    all_gather x1 -> x0, blocking collectives: 43.1 us -> none  [shards(): lax.all_gather(norm_gains.astype(jnp.bfloat16), ('dp', 'tensor'), axis=1,...]
    psum x1 -> x0, blocking collectives: 39.3 us -> none  [shards(): lax.psum((weight_local, update_local), ('dp', 'tensor'))]
  transfers between devices with their start and end apart: 17 -> 2, of which waited for: 16 -> 0; matrix products, arithmetic and copies ran while one was open for 12% -> 6% of each run, Pallas kernels for 0% -> 70%
where the time goes in v3:
time: 581 us; the launch traced here: 572 us
  Pallas kernels  497 us (86%)
  other arithmetic  45.7 us (8%)
  between operations  14.9 us (3%)
  local copies, waits for them, and re-layouts  13.6 us (2%)
    pallas_call x5, Pallas kernels, frame_call(): pl.pallas_call(kernel, out_shape=out_shapes, in_specs=specs, out_specs=ou...  364 us
    pallas_call x1, Pallas kernels, prologue(): pl.pallas_call(functools.partial(prologue_kernel, n_z, n_t, blk), out_sha...  113 us
    pallas_call x2, Pallas kernels, moments(): pl.pallas_call(functools.partial(moments_kernel, names, kv), out_shape=sh...  14.3 us
  transfers between devices with their start and end apart: 2, of which 0 were waited for; matrix products, arithmetic and copies ran while one was open for 6% of the time, Pallas kernels for 70%

profile of v3, /device:TPU:0, one launch (start us, length us, event | category | flops | bytes accessed | tf_op | source)
XLA Modules:
  0.0 571.6 jit_solution(18021807432954825530)
XLA Ops:
  7.2 1.5 convert_element_type.68
  8.8 1.3 convert_bitcast_fusion
  10.1 1.1 pad_maximum_fusion
  11.4 1.1 convert_element_type.63.refs_2_
  13.7 113.2 %gather_tokens_and_weights.1 = (bf16[4,512,1536]{2,1,0:T(8,128)(2,1)S(1)}, bf16[512,1536]{1,0:T(8,128)(2,1)S(1)}, bf16[1536,768]{1,0:T(8,128)(2,1)S(1)}, bf16[1536,384]{1,0:T(8,128)(2,1)S(1)}, f32[2,1536]{1,0:T(2,128)S(1)}) custom-call(bf16[512,1536]{1,0:T(8,128)(2,1)S(1)} %copy-done, bf16[512,1536]{1,0:T(8,128)(2,1)S(1)} %copy-done.1, ...), custom_call_target="tpu_custom_call" | custom-call | bytes 62914560 | tf_op jit(solution)/shard_map/gather_tokens_and_weights/pallas_call | solution.py:349
  126.9 2.6 copy-done.3
  129.6 1.5 copy-done.4
  132.8 1.9 pad_add_fusion.refs_0_
  135.5 6.1 %pad_weights.1 = (bf16[1536,1024]{1,0:T(8,128)(2,1)}, bf16[1536,512]{1,0:T(8,128)(2,1)}) custom-call(bf16[384,512]{1,0:T(8,128)(2,1)} %fusion.14.spread.refs_6_, bf16[1536,768]{1,0:T(8,128)(2,1)} %copy-done.4, bf16[1536,384]{1,0:T(8,128)(2,1)} %copy-done.6), custom_call_target="tpu_custom_call" | custom-call | flops 1811939328 | bytes 8388608 | tf_op jit(solution)/shard_map/pad_weights/pallas_call | solution.py:73
  142.2 2.0 fusion.17
  144.2 1.3 maximum_maximum_fusion.1
  145.5 61.2 %attention_forward.1 = (bf16[1024,1536]{1,0:T(8,128)(2,1)}, bf16[1024,1024]{1,0:T(8,128)(2,1)}, bf16[1024,512]{1,0:T(8,128)(2,1)}, f32[1024,128]{1,0:T(8,128)}, ...) custom-call(s32[2]{0:T(128)} %pad_add_fusion.refs_0_, ...), custom_call_target="tpu_custom_call" | custom-call | flops 18253611008 | bytes 12070920 | tf_op jit(solution)/shard_map/attention_forward/pallas_call | solution.py:199
  206.7 76.7 %feed_forward.1 = (bf16[3,1536,1024]{2,1,0:T(8,128)(2,1)}, bf16[512,1536]{1,0:T(8,128)(2,1)}, bf16[1,512,1536]{2,1,0:T(8,128)(2,1)}, bf16[512,1536]{1,0:T(8,128)...) custom-call(bf16[512,1536]{1,0:T(8,128)(2,1)} %get-tuple-element.77., ...), custom_call_target="tpu_custom_call" | custom-call | flops 57982058496 | bytes 14155776 | tf_op jit(solution)/shard_map/feed_forward/pallas_call | solution.py:199
  283.9 2.4 multiply_reduce_fusion.2
  287.3 2.8 multiply_reduce_fusion
  290.1 3.5 fusion.27
  293.6 128.3 %attention_backward.1 = (bf16[512,1536]{1,0:T(8,128)(2,1)}, bf16[1,512,1536]{2,1,0:T(8,128)(2,1)}, bf16[512,1536]{1,0:T(8,128)(2,1)}, bf16[3,4,192,384]{3,2,1,0:T(8,128)(2,1)}, bf16[3,4,192,384]{3,2,1,0:T(8,128)(2,1)}) custom-call(s32[2]{0:T(128)} %pad_add_fusion.refs_0_, bf16[512,1536]{1,0:T(8,128)(2,1)} %get-tuple-element.128.refs_1_, ...), custom_call_target="tpu_custom_call" | custom-call | flops 40802189312 | bytes 21364744 | tf_op jit(solution)/shard_map/attention_backward/pallas_call | solution.py:199
  421.8 3.9 fusion.5
  426.4 2.9 fusion.7.refs_2_
  429.3 84.5 %sum_attention_gradients.1 = (f32[3,192,384]{2,1,0:T(8,128)}, bf16[512,1536]{1,0:T(8,128)(2,1)}, f32[24,128]{1,0:T(8,128)}) custom-call(bf16[3,4,192,384]{3,2,1,0:T(8,128)(2,1)} %get-tuple-element.92.refs_0_, bf16[3,4,192,384]{3,2,1,0:T(8,128)(2,1)} %get-tuple-element.93.refs_1_, bf16[512,1536]{1,0:T(8,128)(2,1)} %fusion.7.refs_2_, f32[24,128]{1,0:T(8,128)} %reshape.102.refs_3_), custom_call_target="tpu_custom_call" | custom-call | bytes 5124096 | tf_op jit(solution)/shard_map/sum_attention_gradients/pallas_call | solution.py:199
  515.2 4.9 moments.3
  520.2 4.0 fusion.11
  524.9 2.9 fusion.1
  527.9 9.4 %moments.2 = (f32[2,192,1024]{2,1,0:T(8,128)}, f32[192,1024]{1,0:T(8,128)}, f32[2,192,1024]{2,1,0:T(8,128)}, f32[192,1024]{1,0:T(8,128)}, f32[2,192,1024]{2,1,0:...) custom-call(f32[2,192,1024]{2,1,0:T(8,128)} %refs_0_.4, f32[192,1024]{1,0:T(8,128)} %bitcast.74, ...), custom_call_target="tpu_custom_call" | custom-call | bytes 14680064 | tf_op jit(solution)/shard_map/moments/pallas_call | solution.py:1047
  537.3 13.1 %sum_squares.1 = f32[8,128]{1,0:T(8,128)} custom-call(f32[8,128]{1,0:T(8,128)} %get-tuple-element.101.refs_0_, f32[8,128]{1,0:T(8,128)} %get-tuple-element.104.refs_1_), custom_call_target="tpu_custom_call" | custom-call | bytes 8192 | tf_op jit(solution)/shard_map/sum_squares/pallas_call | solution.py:199
  550.3 1.3 fusion.26
  552.4 1.3 slice_bitcast_fusion
  553.6 1.2 slice_bitcast_fusion.1
  555.5 2.8 bitcast_subtract_fusion
  558.3 3.1 multiply_subtract_fusion
  561.4 1.4 bitcast_subtract_fusion.1
  562.8 1.6 multiply_subtract_fusion.1
  (87 shorter events, 10.1 us)
Async XLA Ops:
  7.2 199.5 %all-gather.2.cloned.1.call-start = ((), (), s32[]{:S(2)}) async-start(), calls=%async_computation.1 | async-start | bytes 10616832 | tf_op jit(solution)/shard_map/all_gather | solution.py:1165
  8.8 3.8 copy-start.24
  8.8 5.0 copy-start
  8.8 4.9 copy-start.1
  11.3 120.8 %copy-start.26 = (s32[2]{0:T(128)S(1)}, s32[2]{0:T(128)}, u32[]{:S(2)}) copy-start(s32[2]{0:T(128)} %param.20) | copy-start | bytes 28
  11.3 516.6 %reduce-scatter.2.cloned.1.call-start = ((), (), s32[]{:S(2)}) async-start(), calls=%async_computation.2 | async-start | bytes 10616832 | tf_op jit(solution)/shard_map/reduce_scatter | solution.py:1173
  126.9 2.6 copy-start.3
  129.6 1.5 copy-start.4
  131.1 1.0 copy-start.6
  132.1 9.5 %copy-start.5 = (bf16[512,1536]{1,0:T(8,128)(2,1)}, bf16[512,1536]{1,0:T(8,128)(2,1)S(1)}, u32[]{:S(2)}) copy-start(bf16[512,1536]{1,0:T(8,128)(2,1)S(1)} %get-tuple-element.78.refs_2_) | copy-start | bytes 4718596
  283.5 2.8 copy-start.13
  283.5 3.3 copy-start.7
  283.5 3.7 copy-start.12
  287.3 2.8 copy-start.2
  287.3 2.8 copy-start.14
  421.8 4.5 copy-start.21
  429.3 90.8 %copy-start.20 = (bf16[512,1536]{1,0:T(8,128)(2,1)S(1)}, bf16[512,1536]{1,0:T(8,128)(2,1)}, u32[]{:S(2)}) copy-start(bf16[512,1536]{1,0:T(8,128)(2,1)} %get-tuple-element.79) | copy-start | bytes 4718596
  514.5 5.6 copy-start.8
  520.1 4.1 copy-start.10
  520.1 4.1 copy-start.15
  520.1 4.0 copy-start.16
  520.2 4.8 copy-start.17
  527.9 26.9 %copy-start.25 = (f32[2,48]{1,0:T(2,128)S(1)}, f32[2,48]{1,0:T(2,128)}, u32[]{:S(2)}) copy-start(f32[2,48]{1,0:T(2,128)} %param.25) | copy-start | bytes 1156
  527.9 26.9 %copy-start.27 = (f32[2,1,48]{2,1,0:T(1,128)S(1)}, f32[2,1,48]{2,1,0:T(1,128)}, u32[]{:S(2)}) copy-start(f32[2,1,48]{2,1,0:T(1,128)} %get-tuple-element.109) | copy-start | bytes 1156
  527.9 27.6 %copy-start.11 = (f32[1024,192]{0,1:T(8,128)S(1)}, f32[1024,192]{0,1:T(8,128)}, u32[]{:S(2)}) copy-start(f32[1024,192]{0,1:T(8,128)} %param.24) | copy-start | bytes 2359300
  537.3 21.0 %copy-start.9 = (f32[2,192,1024]{2,1,0:T(8,128)S(1)}, f32[2,192,1024]{2,1,0:T(8,128)}, u32[]{:S(2)}) copy-start(f32[2,192,1024]{2,1,0:T(8,128)} %refs_0_.4) | copy-start | bytes 4718596
  555.5 6.0 %copy-start.19 = (f32[384,192]{0,1:T(8,128)S(1)}, f32[384,192]{0,1:T(8,128)}, u32[]{:S(2)}) copy-start(f32[384,192]{0,1:T(8,128)} %param.22) | copy-start | bytes 884740
  555.5 6.0 %copy-start.23 = (f32[192,384]{1,0:T(8,128)S(1)}, f32[192,384]{1,0:T(8,128)}, u32[]{:S(2)}) copy-start(f32[192,384]{1,0:T(8,128)} %get-tuple-element.106) | copy-start | bytes 884740
  558.3 4.5 copy-start.18
  558.3 4.5 copy-start.22
Sparse Core Ops, SparseCore 0:
  11.4 173.6 all-gather.1
  283.6 228.3 reduce-scatter.1

commit v4 on v3

v4 whole, which is shorter than its diff:
```python
import functools

import jax
import jax.numpy as jnp
import numpy as np
from jax import lax
from jax.experimental import pallas as pl
from jax.experimental.pallas import tpu as pltpu
from jax.sharding import PartitionSpec as P

HEAD = 96
PAD = 128
SEQ_LEN = 1024
SEQS_DEV = 2
STEP = 10
GROUP = 2

NORM_EPSILON = 1e-05
ROPE_THETA = 100000.0
BETA_ONE = 0.9
BETA_TWO = 0.999
ADAM_EPSILON = 1e-06
WEIGHT_DECAY = 0.01
LEARN_RATE = 0.3
NEGATIVE = -1e30
LOG2E = 1.4426950408889634
SCALE = HEAD ** (-0.5)
Q_ROWS = 256
G_COLS = 4 * HEAD
G_PAD = 4 * PAD
VMEM_LIMIT = 56 << 20

F32 = jnp.float32
BF16 = jnp.bfloat16
VM = pl.BlockSpec(memory_space=pltpu.VMEM)
SM = pl.BlockSpec(memory_space=pltpu.SMEM)
ANY = pl.BlockSpec(memory_space=pl.ANY)
MESH = pl.DeviceIdType.MESH
IN_VMEM, IN_SMEM, IN_HBM, LOAD, FLUSH = range(5)
NEAR, FAR = "near_", "far_"
WINDOW, SLOTS = 4, 4
HBM = "any_"


def dot_nn(a, b):
    return lax.dot_general(a, b, (((1,), (0,)), ((), ())), preferred_element_type=F32)


def dot_nt(a, b):
    return lax.dot_general(a, b, (((1,), (1,)), ((), ())), preferred_element_type=F32)


def dot_tn(a, b):
    return lax.dot_general(a, b, (((0,), (0,)), ((), ())), preferred_element_type=F32)


def cost(flops, moved):
    return pl.CostEstimate(flops=int(flops), bytes_accessed=int(moved), transcendentals=0)


def spread_matrix():
    source = lax.broadcasted_iota(jnp.int32, (G_COLS, G_PAD), 0)
    target = lax.broadcasted_iota(jnp.int32, (G_COLS, G_PAD), 1)
    return ((target // PAD) * HEAD + target % PAD == source) & (target % PAD < HEAD)


def swap_halves(values):
    lane = lax.broadcasted_iota(jnp.int32, values.shape, 1)
    return jnp.where(
        lane < HEAD // 2,
        pltpu.roll(values, PAD - HEAD // 2, 1),
        pltpu.roll(values, HEAD // 2, 1),
    )


def permuted(axis, bit):
    return {axis: lax.axis_index(axis) ^ bit}


class Remote:
    def __init__(self, copy):
        self.copy = copy
        self.landed = self.left = False

    def wait_recv(self):
        if not self.landed:
            self.copy.wait_recv()
        self.landed = True

    def wait_send(self):
        if not self.left:
            self.copy.wait_send()
        self.left = True


class Side:
    def __init__(self, refs, side):
        self.refs, self.side = refs, side

    def __getattr__(self, name):
        return self.refs[self.side + name]

    def of(self, side):
        return Side(self.refs, self.side + side)


class Frame:
    def __init__(self, names, refs):
        self.refs = dict(zip(names, refs))
        self.loading, self.remotes, self.storing = [], [], []
        self.next_local = 0
        self.hbm = Side(self.refs, HBM)

    def __getattr__(self, name):
        return self.refs[name]

    def of(self, side):
        return Side(self.refs, side)

    def meet(self, peers):
        barrier = pltpu.get_barrier_semaphore()
        for peer in peers:
            pl.semaphore_signal(barrier, inc=1, device_id=peer, device_id_type=MESH)
        pl.semaphore_wait(barrier, len(peers))

    def local(self, source, target):
        copy = pltpu.make_async_copy(source, target, self.local_sem.at[self.next_local])
        self.next_local += 1
        copy.start()
        return copy

    def load_refs(self, source, target):
        self.loading.append(self.local(source, target))

    def ready(self):
        for copy in self.loading:
            copy.wait()
        self.loading = []

    def store(self, source, target):
        pending = [self.local(source, target)]

        def wait():
            if pending:
                pending.pop().wait()

        self.storing.append(wait)
        return wait

    def flush(self, source, target):
        self.store(source, target)

    def remote(self, source, target, peer):
        n = len(self.remotes)
        copy = pltpu.make_async_remote_copy(
            src_ref=source,
            dst_ref=target,
            send_sem=self.send_sem.at[n],
            recv_sem=self.recv_sem.at[n],
            device_id=peer,
            device_id_type=MESH,
        )
        copy.start()
        self.remotes.append(Remote(copy))
        return self.remotes[-1]

    def finish(self):
        for remote in self.remotes:
            remote.wait_send()
            remote.wait_recv()
        for wait in self.storing:
            wait()


def frame_call(body, name, inputs, outputs, scratch, flops, collective_id, n_sems=40):
    names, specs, arrays = [], [], []
    spec_of = {IN_VMEM: VM, IN_SMEM: SM, IN_HBM: ANY, LOAD: ANY, FLUSH: ANY}
    for key, (array, kind) in inputs.items():
        names.append(HBM + key if kind == LOAD else key)
        specs.append(spec_of[kind])
        arrays.append(array)
    out_specs, out_shapes = [], []
    for key, (shape, kind) in outputs.items():
        names.append(HBM + key if kind == FLUSH else key)
        out_specs.append(spec_of[kind])
        out_shapes.append(shape)
    shapes = []
    for table, kind_of in ((inputs, LOAD), (outputs, FLUSH)):
        for key, (array, kind) in table.items():
            if kind == kind_of:
                names.append(key)
                shapes.append(pltpu.VMEM(array.shape, array.dtype))
    for key, shape in scratch.items():
        names.append(key)
        shapes.append(shape)
    for key in ("local_sem", "send_sem", "recv_sem"):
        names.append(key)
        shapes.append(pltpu.SemaphoreType.DMA((n_sems,)))

    def kernel(*refs):
        frame = Frame(names, refs)
        body(frame)
        frame.finish()

    moved = sum(a.size * a.dtype.itemsize for a in arrays)
    results = pl.pallas_call(
        kernel,
        out_shape=out_shapes,
        in_specs=specs,
        out_specs=out_specs,
        scratch_shapes=shapes,
        compiler_params=pltpu.CompilerParams(
            vmem_limit_bytes=VMEM_LIMIT, collective_id=collective_id, has_side_effects=True
        ),
        cost_estimate=cost(flops, moved),
        name=name,
    )(*arrays)
    return dict(zip(outputs, results))


def half_peers(nb):
    return [(r, permuted("tensor", r)) for r in range(1, nb)]


def rows_of(c):
    return pl.ds(c * Q_ROWS, Q_ROWS)


def bits_down(size):
    bits = []
    bit = size // 2
    while bit:
        bits.append(bit)
        bit //= 2
    return bits


def attention_rows(k, tag, i, length, kv):
    qkvp, att, lse = k.of(tag).qkvp, k.of(tag).att, k.of(tag).lse
    n = (i + 1) * Q_ROWS
    rows = slice(i * Q_ROWS, n)
    lane = lax.broadcasted_iota(jnp.int32, (Q_ROWS, PAD), 1)

    def one_head(h, log_totals):
        group = h // GROUP
        q_col = pl.ds(pl.multiple_of((4 * group + h % GROUP) * PAD, PAD), PAD)
        k_col = pl.ds(pl.multiple_of((4 * group + 2) * PAD, PAD), PAD)
        v_col = pl.ds(pl.multiple_of((4 * group + 3) * PAD, PAD), PAD)
        a_col = pl.ds(pl.multiple_of(h * PAD, PAD), PAD)
        s = dot_nt(qkvp[rows, q_col], qkvp[0:n, k_col])
        row_ids = lax.broadcasted_iota(jnp.int32, (Q_ROWS, 1), 0) + i * Q_ROWS + 1
        limit = jnp.minimum(row_ids, length)
        col_ids = lax.broadcasted_iota(jnp.int32, (Q_ROWS, n), 1)
        s = jnp.where(col_ids < limit, s, NEGATIVE)
        top = jnp.max(s, axis=-1, keepdims=True)
        e = jnp.exp2((s - top) * (SCALE * LOG2E))
        total = jnp.sum(e, axis=-1, keepdims=True)
        p = (e * (1.0 / total)).astype(BF16)
        att[rows, a_col] = dot_nn(p, qkvp[0:n, v_col]).astype(BF16)
        log_total = top * (SCALE * LOG2E) + jnp.log2(total)
        return jnp.where(lane == h, log_total, log_totals)

    lse[rows, :] = lax.fori_loop(0, kv * GROUP, one_head, jnp.zeros((Q_ROWS, PAD), F32))


def z_order(n_z):
    return sorted(range(1, n_z), key=lambda i: min(i, n_z - i))


def z_peers(n_z):
    d = lax.axis_index("dp")
    return {i: {"dp": lax.rem(d + 2 * i, 2 * n_z)} for i in range(1, n_z)}


class Gather:
    def __init__(self, k, streams, n_z, blk):
        d = lax.axis_index("dp")
        self.k, self.streams = k, streams
        self.peers, self.other_x = z_peers(n_z), permuted("dp", 1)
        self.order = [(s, i) for s in range(len(streams)) for i in z_order(n_z)]
        self.rows = {
            i: pl.ds(pl.multiple_of(lax.rem(d + 2 * (n_z - i), 2 * n_z) * blk, 16), blk)
            for i in range(n_z)
        }
        self.sent, self.along_x = {}, {}
        self.next_send = self.next_arrival = 0

    def send(self):
        if self.next_send < len(self.order):
            s, i = self.order[self.next_send]
            source, target, at = self.streams[s]
            self.sent[s, i] = self.k.remote(source, target.at[at + (self.rows[0],)], self.peers[i])
            self.next_send += 1

    def own_along_x(self, s):
        source, target, at = self.streams[s]
        self.along_x[s, 0] = self.k.remote(source, target.at[at + (self.rows[0],)], self.other_x)

    def pump(self):
        if self.next_arrival < len(self.order):
            s, i = self.order[self.next_arrival]
            self.next_arrival += 1
            self.sent[s, i].wait_recv()
            self.send()
            if (s, 0) not in self.along_x:
                self.own_along_x(s)
            _, target, at = self.streams[s]
            block = target.at[at + (self.rows[i],)]
            self.along_x[s, i] = self.k.remote(block, block, self.other_x)

    def complete(self, s):
        for (stream, _), copy in self.along_x.items():
            if stream == s:
                copy.wait_recv()


def opening_body(nb, rows_each, kv, n_z, blk, k):
    t = lax.axis_index("tensor")
    local = lax.rem(t, nb)
    seq_len = nb * rows_each
    per_block = rows_each // Q_ROWS
    chunk = 32
    over, other_x = permuted("tensor", nb), permuted("dp", 1)
    peers, along_z = half_peers(nb), z_peers(n_z)
    near_x, far_x = k.near_x, k.far_x
    streams = [(k.qkv_half, k.wq, ()), (k.out_half, k.wo, ())]
    streams += [(k.ffn_half.at[i], k.w_ffn, (i,)) for i in (2, 0, 1)]
    gather = Gather(k, streams, n_z, blk)
    own_tokens = k.local(k.tokens, near_x.at[0])
    own_blocks = [
        k.local(source, target.at[at + (gather.rows[0],)]) for source, target, at in streams
    ]
    k.load_refs(k.hbm.cos_t, k.cos_t)
    k.load_refs(k.hbm.sin_t, k.sin_t)
    k.load_refs(k.hbm.spread, k.spread)
    k.held[0, :, :] = k.gains[...]
    k.meet(list(along_z.values()) + [other_x, over] + [peer for _, peer in peers])

    stages = [permuted("tensor", bit) for bit in bits_down(2 * nb)] + [other_x]
    gain_copy = k.remote(k.held.at[0], k.got.at[0], stages[0])
    far_copy = k.remote(k.tokens, far_x.at[0], over)
    near_copies = [k.remote(k.tokens, near_x.at[r], peer) for r, peer in peers]
    for _ in range(WINDOW):
        gather.send()
    for stage in range(len(stages)):
        gain_copy.wait_recv()
        k.held[stage + 1, :, :] = k.held[stage, :, :] + k.got[stage, :, :]
        if stage + 1 < len(stages):
            gain_copy = k.remote(k.held.at[stage + 1], k.got.at[stage + 1], stages[stage + 1])
    last = len(stages)
    gain_copies = [
        k.remote(k.held.at[last], k.got.at[last + i - 1], along_z[i]) for i in range(1, n_z)
    ]
    gather.own_along_x(0)
    gather.own_along_x(1)
    for _ in range(2 * (n_z - 1)):
        gather.pump()
    for s in range(2, len(streams)):
        gather.own_along_x(s)
    total = k.held[last, :, :]
    for i, copy in enumerate(gain_copies):
        copy.wait_recv()
        total = total + k.got[last + i, :, :]
    k.gain_sum[...] = total
    gain_one, gain_two = k.gain_sum.at[0:1], k.gain_sum.at[1:2]
    far_copy.wait_recv()
    far_copies = [k.remote(far_x.at[0], far_x.at[r], peer) for r, peer in peers]
    own_tokens.wait()
    for copy in near_copies + far_copies:
        copy.wait_recv()

    def normalise(tag):
        for r in range(nb):
            base = (local ^ r) * rows_each

            def norm_rows(i, carry):
                rows = pl.ds(pl.multiple_of(i * chunk, chunk), chunk)
                v = k.of(tag).x[r, rows, :].astype(F32)
                inv = lax.rsqrt(jnp.mean(v * v, axis=-1, keepdims=True) + NORM_EPSILON)
                k.of(tag).normed[pl.ds(pl.multiple_of(base + i * chunk, chunk), chunk), :] = (
                    v * inv * gain_one[...]
                ).astype(BF16)
                return carry

            lax.fori_loop(0, rows_each // chunk, norm_rows, 0)
        k.flush(k.of(tag).normed, k.hbm.of(tag).normed)

    normalise(FAR)
    normalise(NEAR)
    for copy in own_blocks:
        copy.wait()
    k.ready()
    for s, (source, target) in enumerate(((k.wq, k.w_qkv), (k.wo, k.w_out))):
        gather.complete(s)
        for g in range(-(-target.shape[1] // G_PAD)):
            wide = min(G_PAD, target.shape[1] - g * G_PAD)
            part = source[:, g * G_COLS : (g + 1) * G_COLS]
            target[:, g * G_PAD : g * G_PAD + wide] = dot_nn(
                part, k.spread[0 : part.shape[1], 0:wide]
            ).astype(BF16)
        k.flush(target, k.hbm.w_out if s else k.hbm.w_qkv)

    landing, waiting = [], []
    for tag, length in ((FAR, k.lengths[1]), (NEAR, k.lengths[0])):
        normed, qkvp = k.of(tag).normed, k.of(tag).qkvp
        parts, got = k.of(tag).parts, k.of(tag).got
        for i in range(seq_len // Q_ROWS):
            rows = slice(i * Q_ROWS, (i + 1) * Q_ROWS)
            for j in range(kv):
                proj = dot_nn(normed[rows, :], k.w_qkv[:, j * G_PAD : (j + 1) * G_PAD])
                for h in range(4):
                    part = proj[:, h * PAD : (h + 1) * PAD]
                    if h < 3:
                        part = part * k.cos_t[rows, :] + swap_halves(part) * k.sin_t[rows, :]
                    qkvp[rows, (4 * j + h) * PAD : (4 * j + h + 1) * PAD] = part.astype(BF16)
        k.flush(qkvp, k.hbm.of(tag).qkvp)
        gather.pump()
        for c in range(per_block):
            rows = slice(c * Q_ROWS, (c + 1) * Q_ROWS)
            for b in range(nb):
                i = b * per_block + c
                attention_rows(k, tag, i, length, kv)
                part = dot_nt(k.of(tag).att[i * Q_ROWS : (i + 1) * Q_ROWS, :], k.w_out[...])
                parts[local ^ b, rows, :] = part.astype(BF16)
                if waiting:
                    waiting.pop()()
                gather.pump()
            copies = [
                k.remote(parts.at[r, rows_of(c)], got.at[r - 1, rows_of(c)], peer)
                for r, peer in peers
            ]

            def complete(rows=rows, c=c, copies=copies, parts=parts, got=got, tag=tag):
                total = parts[0, rows, :].astype(F32)
                for r, copy in enumerate(copies):
                    copy.wait_recv()
                    total = total + got[r, rows, :].astype(F32)
                if tag == FAR:
                    parts[0, rows, :] = total.astype(BF16)
                    landing.append(
                        k.remote(parts.at[0, rows_of(c)], k.landed.at[rows_of(c)], over)
                    )
                    if c == per_block - 1:
                        k.remote(k.cotangent, k.c_far, over)
                else:
                    k.residual[rows, :] = near_x[0, rows, :].astype(F32) + total

            waiting.append(complete)
        k.flush(k.of(tag).att, k.hbm.of(tag).att)
        k.flush(k.of(tag).lse, k.hbm.of(tag).lse)
    waiting.pop()()
    for c in range(per_block):
        landing[c].wait_recv()

        def residual_rows(i, carry):
            rows = pl.ds(pl.multiple_of(c * Q_ROWS + i * chunk, chunk), chunk)
            v = k.residual[rows, :] + k.landed[rows, :].astype(F32)
            k.residual[rows, :] = v
            inv = lax.rsqrt(jnp.mean(v * v, axis=-1, keepdims=True) + NORM_EPSILON)
            k.normed_two[rows, :] = (v * inv * gain_two[...]).astype(BF16)
            return carry

        lax.fori_loop(0, Q_ROWS // chunk, residual_rows, 0)
    k.flush(k.residual, k.hbm.residual)
    k.flush(k.normed_two, k.hbm.normed_two)
    for _ in range(3 * (n_z - 1)):
        gather.pump()


def opening(tokens, cotangent, lengths, gains, halves, tables, spread, n_t, n_z, collective_id):
    rows_each, width = tokens.shape
    qkv_half, out_half, ffn_half = halves
    blk = qkv_half.shape[0]
    n_dp = 2 * n_z
    nb = n_t // 2
    seq_len = nb * rows_each
    kv = qkv_half.shape[1] // G_COLS
    heads = kv * GROUP
    sds = jax.ShapeDtypeStruct
    normed = (sds((seq_len, width), BF16), FLUSH)
    qkvp = (sds((seq_len, kv * G_PAD), BF16), FLUSH)
    att = (sds((seq_len, heads * PAD), BF16), FLUSH)
    lse = (sds((seq_len, PAD), F32), FLUSH)
    block = pltpu.VMEM((nb, rows_each, width), BF16)
    others = pltpu.VMEM((nb - 1, rows_each, width), BF16)
    n_gain = len(bits_down(n_t)) + 1 + n_z - 1
    return frame_call(
        functools.partial(opening_body, nb, rows_each, kv, n_z, blk),
        "attention_forward",
        dict(
            tokens=(tokens, IN_HBM),
            cotangent=(cotangent, IN_HBM),
            lengths=(lengths, IN_SMEM),
            gains=(gains, IN_VMEM),
            qkv_half=(qkv_half, IN_HBM),
            out_half=(out_half, IN_HBM),
            ffn_half=(ffn_half, IN_HBM),
            cos_t=(tables[0], LOAD),
            sin_t=(tables[1], LOAD),
            spread=(spread, LOAD),
        ),
        dict(
            near_normed=normed,
            far_normed=normed,
            near_qkvp=qkvp,
            far_qkvp=qkvp,
            near_att=att,
            far_att=att,
            near_lse=lse,
            far_lse=lse,
            residual=(sds((rows_each, width), F32), FLUSH),
            normed_two=(sds((rows_each, width), BF16), FLUSH),
            w_qkv=(sds((blk * n_dp, kv * G_PAD), BF16), FLUSH),
            w_out=(sds((blk * n_dp, heads * PAD), BF16), FLUSH),
            w_ffn=(sds((3, blk * n_dp, ffn_half.shape[2]), BF16), IN_HBM),
            c_far=(sds(cotangent.shape, BF16), IN_HBM),
            gain_sum=(sds(gains.shape, F32), IN_VMEM),
        ),
        dict(
            near_x=block,
            far_x=block,
            far_parts=block,
            near_parts=block,
            far_got=others,
            near_got=others,
            landed=pltpu.VMEM((rows_each, width), BF16),
            wq=pltpu.VMEM((blk * n_dp, qkv_half.shape[1]), BF16),
            wo=pltpu.VMEM((blk * n_dp, out_half.shape[1]), BF16),
            held=pltpu.VMEM((n_gain + 1,) + gains.shape, F32),
            got=pltpu.VMEM((n_gain,) + gains.shape, F32),
        ),
        4 * seq_len * width * (kv * G_PAD + heads * PAD) + heads * seq_len * seq_len * 8 * 256,
        collective_id,
        n_sems=12 * n_z + 48,
    )


def feed_forward_body(nb, rows_each, k):
    over = permuted("tensor", nb)
    peers = half_peers(nb)
    per_block = rows_each // Q_ROWS
    w = k.w
    width = w.shape[1]
    near_n, near_c, far_n, far_c = k.near_n, k.near_c, k.far_n, k.far_c
    own_n = k.local(k.own_n, near_n.at[0])
    own_c = k.local(k.own_c, near_c.at[0])
    k.load_refs(k.hbm.w, k.w)
    own_far_c = k.local(k.own_far_c, far_c.at[0])
    k.meet([over] + [peer for _, peer in peers])
    far_first = [
        k.remote(k.own_n.at[rows_of(c)], far_n.at[0, rows_of(c)], over) for c in range(per_block)
    ]
    n_copies = [k.remote(k.own_n, near_n.at[r], peer) for r, peer in peers]
    c_copies = [k.remote(k.own_c, near_c.at[r], peer) for r, peer in peers]
    far_c_copies = [k.remote(k.own_far_c, far_c.at[r], peer) for r, peer in peers]
    own_n.wait()
    own_c.wait()
    k.ready()

    def rows_step(side, r, c):
        rows = slice(c * Q_ROWS, (c + 1) * Q_ROWS)
        start = (0 if side == NEAR else nb * rows_each) + r * rows_each + c * Q_ROWS
        kept = slice(start, start + Q_ROWS)
        n = k.of(side).n[r, rows, :]
        gate = dot_nn(n, w[0])
        up = dot_nn(n, w[1])
        sig = 1.0 / (1.0 + jnp.exp(-gate))
        silu = gate * sig
        hid = (silu * up).astype(BF16)
        k.hidden[kept, :] = hid
        dh = dot_nn(k.of(side).c[r, rows, :], w[2])
        dg = (dh * up * sig * (1.0 + gate * (1.0 - sig))).astype(BF16)
        du = (dh * silu).astype(BF16)
        k.d_gate[kept, :] = dg
        k.d_up[kept, :] = du
        k.of(side).grad[r, rows, :] = (dot_nt(dg, w[0]) + dot_nt(du, w[1])).astype(BF16)
        k.of(side).out[r, rows, :] = dot_nt(hid, w[2]).astype(BF16)

    for r in range(nb):
        if r:
            n_copies[r - 1].wait_recv()
            c_copies[r - 1].wait_recv()
        for c in range(per_block):
            rows_step(NEAR, r, c)
        for part, own, got in (
            (k.near_grad.at[r], k.near_own_grad, k.near_got_grad),
            (k.near_out.at[r], k.near_own_out, k.near_got_out),
        ):
            if r:
                k.remote(part, got.at[r - 1], peers[r - 1][1])
            else:
                k.store(part, own)
    own_far_c.wait()
    for copy in far_c_copies:
        copy.wait_recv()
    landing = []
    for c in range(per_block):
        rows = slice(c * Q_ROWS, (c + 1) * Q_ROWS)
        far_first[c].wait_recv()
        passed = [
            k.remote(far_n.at[0, rows_of(c)], far_n.at[r, rows_of(c)], peer) for r, peer in peers
        ]
        rows_step(FAR, 0, c)
        copies = []
        for r, peer in peers:
            passed[r - 1].wait_recv()
            rows_step(FAR, r, c)
            copies.append(
                k.remote(
                    k.far_grad.at[r, rows_of(c)], k.far_got_grad.at[r - 1, rows_of(c)], peer
                )
            )
        total = k.far_grad[0, rows, :].astype(F32)
        for r, copy in enumerate(copies):
            copy.wait_recv()
            total = total + k.far_got_grad[r, rows, :].astype(F32)
        k.far_grad[0, rows, :] = total.astype(BF16)
        landing.append(k.remote(k.far_grad.at[0, rows_of(c)], k.landed.at[rows_of(c)], over))
    k.store(k.far_out.at[0], k.far_own_out)
    for r, peer in peers:
        k.remote(k.far_out.at[r], k.far_got_out.at[r - 1], peer)
    half = nb * rows_each
    for which in (2, 0, 1):
        right = (k.d_gate, k.d_up, k.hidden)[which]
        lefts = {side: k.of(side).c if which == 2 else k.of(side).n for side in (NEAR, FAR)}

        def col_step(i, carry):
            cols = pl.ds(pl.multiple_of(i * G_COLS, G_COLS), G_COLS)
            total = None
            for s, side in enumerate((NEAR, FAR)):
                for r in range(nb):
                    start = s * half + r * rows_each
                    term = dot_tn(lefts[side][r, :, cols], right[start : start + rows_each, :])
                    total = term if total is None else total + term
            w[which, cols, :] = total.astype(BF16)
            return carry

        lax.fori_loop(0, width // G_COLS, col_step, 0)
        k.store(w.at[which], k.grads.at[which])


def feed_forward(normed_two, cotangent, c_far, w, nb, collective_id):
    rows_each, width = normed_two.shape
    units = w.shape[2]
    sds = jax.ShapeDtypeStruct
    block = pltpu.VMEM((nb, rows_each, width), BF16)
    kept = pltpu.VMEM((2 * nb * rows_each, units), BF16)
    own = (sds((rows_each, width), BF16), IN_HBM)
    got = (sds((nb - 1, rows_each, width), BF16), IN_HBM)
    return frame_call(
        functools.partial(feed_forward_body, nb, rows_each),
        "feed_forward",
        dict(
            own_n=(normed_two, IN_HBM),
            own_c=(cotangent, IN_HBM),
            own_far_c=(c_far, IN_HBM),
            w=(w, LOAD),
        ),
        dict(
            grads=(sds(w.shape, BF16), IN_HBM),
            near_own_grad=own,
            near_got_grad=got,
            landed=own,
            near_own_out=own,
            near_got_out=got,
            far_own_out=own,
            far_got_out=got,
        ),
        dict(
            near_n=block,
            far_n=block,
            near_c=block,
            far_c=block,
            hidden=kept,
            d_gate=kept,
            d_up=kept,
            near_grad=block,
            far_grad=block,
            near_out=block,
            far_out=block,
            far_got_grad=pltpu.VMEM((nb - 1, rows_each, width), BF16),
        ),
        36 * nb * rows_each * width * units,
        collective_id,
    )


def attention_backward_rows(k, tag, i, length, kv):
    qkvp, dproj, datt, lse = k.of(tag).qkvp, k.of(tag).dproj, k.datt, k.of(tag).lse
    n = (i + 1) * Q_ROWS
    rows = slice(i * Q_ROWS, n)
    lane = lax.broadcasted_iota(jnp.int32, (Q_ROWS, PAD), 1)

    def one_head(h, carry):
        group = h // GROUP
        q_col = pl.ds(pl.multiple_of((4 * group + h % GROUP) * PAD, PAD), PAD)
        k_col = pl.ds(pl.multiple_of((4 * group + 2) * PAD, PAD), PAD)
        v_col = pl.ds(pl.multiple_of((4 * group + 3) * PAD, PAD), PAD)
        a_col = pl.ds(pl.multiple_of(h * PAD, PAD), PAD)
        q = qkvp[rows, q_col]
        keys = qkvp[0:n, k_col]
        do = datt[rows, a_col]
        row_lse = jnp.sum(jnp.where(lane == h, lse[rows, :], 0.0), axis=-1, keepdims=True)
        s = dot_nt(q, keys)
        row_ids = lax.broadcasted_iota(jnp.int32, (Q_ROWS, 1), 0) + i * Q_ROWS + 1
        limit = jnp.minimum(row_ids, length)
        col_ids = lax.broadcasted_iota(jnp.int32, (Q_ROWS, n), 1)
        s = jnp.where(col_ids < limit, s, NEGATIVE)
        p = jnp.exp2(s * (SCALE * LOG2E) - row_lse)
        dp = dot_nt(do, qkvp[0:n, v_col])
        inner = jnp.sum(p * dp, axis=-1, keepdims=True)
        ds = (p * (dp - inner)).astype(BF16)
        k.dv[group, 0:n, :] += dot_tn(p.astype(BF16), do)
        k.dk[group, 0:n, :] += dot_tn(ds, q)
        dq = dot_nn(ds, keys) * SCALE
        dproj[rows, q_col] = unrotate(k, dq, rows).astype(BF16)
        return carry

    lax.fori_loop(0, kv * GROUP, one_head, 0)


def unrotate(k, grad, rows):
    return grad * k.cos_t[rows, :] - swap_halves(grad) * k.sin_t[rows, :]


class Scatter:
    def __init__(self, k, n_z, blk):
        d = lax.axis_index("dp")
        self.k, self.peers, self.other_x = k, z_peers(n_z), permuted("dp", 1)
        self.order = [(which, i) for which in (2, 0, 1) for i in z_order(n_z) + [0]]

        def rows(owner):
            return pl.ds(pl.multiple_of(owner * blk, 16), blk)

        owners = {i: lax.rem(d + 2 * i, 2 * n_z) for i in range(n_z)}
        self.rows = {i: rows(owner) for i, owner in owners.items()}
        self.rows_other = {i: rows(owner ^ 1) for i, owner in owners.items()}
        self.sent, self.slots = [], [None] * SLOTS
        self.next_arrival = 0

    def send(self):
        if len(self.sent) < len(self.order):
            which, i = self.order[len(self.sent)]
            self.sent.append(
                self.k.remote(
                    self.k.grads.at[which, self.rows_other[i]],
                    self.k.x_got.at[which, i],
                    self.other_x,
                )
            )

    def pump(self):
        if self.next_arrival == len(self.order):
            return False
        k, n = self.k, self.next_arrival
        which, i = self.order[n]
        self.next_arrival += 1
        own = k.local(k.grads.at[which, self.rows[i]], k.staged.at[0])
        self.sent[n].wait_recv()
        self.send()
        other = k.local(k.x_got.at[which, i], k.staged.at[1])
        slot = n % SLOTS
        if self.slots[slot] is not None:
            self.slots[slot]()
        own.wait()
        other.wait()
        k.narrow[slot, :, :] = (
            k.staged[0, :, :].astype(F32) + k.staged[1, :, :].astype(F32)
        ).astype(BF16)
        if i:
            remote = k.remote(k.narrow.at[slot], k.ffn_sums.at[which, i], self.peers[i])
            self.slots[slot] = remote.wait_send
        else:
            self.slots[slot] = k.store(k.narrow.at[slot], k.ffn_sums.at[which, 0])
        return True


def attention_backward_body(nb, rows_each, kv, n_z, blk, k):
    d = lax.axis_index("dp")
    z, x = d // 2, lax.rem(d, 2)
    local = lax.rem(lax.axis_index("tensor"), nb)
    seq_len = nb * rows_each
    per_block = rows_each // Q_ROWS
    over = permuted("tensor", nb)
    other_x = permuted("dp", 1)
    peers = half_peers(nb)
    own_a = k.local(k.own_a, k.near_a.at[0])
    k.load_refs(k.hbm.w_out, k.w_out)
    k.load_refs(k.hbm.cos_t, k.cos_t)
    k.load_refs(k.hbm.sin_t, k.sin_t)
    for tag in (NEAR, FAR):
        k.load_refs(k.hbm.of(tag).qkvp, k.of(tag).qkvp)
        k.load_refs(k.hbm.of(tag).lse, k.of(tag).lse)
    late = [k.local(k.hbm.w_qkv, k.w_qkv), k.local(k.hbm.spread, k.spread)]
    for tag in (NEAR, FAR):
        late.append(k.local(k.hbm.of(tag).att, k.of(tag).att))
        late.append(k.local(k.hbm.of(tag).normed, k.of(tag).normed))
    k.meet([over, other_x] + [peer for _, peer in peers] + list(z_peers(n_z).values()))
    far_first = [
        k.remote(k.own_a.at[rows_of(c)], k.far_a.at[0, rows_of(c)], over)
        for c in range(per_block)
    ]
    near_copies = [k.remote(k.own_a, k.near_a.at[r], peer) for r, peer in peers]
    scatter = Scatter(k, n_z, blk)
    for _ in range(WINDOW):
        scatter.send()
    own_a.wait()
    k.ready()
    for copy in near_copies:
        copy.wait_recv()
    for tag, length in ((NEAR, k.lengths[0]), (FAR, k.lengths[1])):
        blocks, parts, dproj = k.of(tag).a, k.of(tag).parts, k.of(tag).dproj
        k.dk[...] = jnp.zeros_like(k.dk)
        k.dv[...] = jnp.zeros_like(k.dv)
        for c in range(per_block):
            rows = slice(c * Q_ROWS, (c + 1) * Q_ROWS)
            if tag == FAR:
                far_first[c].wait_recv()
                passed = [
                    k.remote(blocks.at[0, rows_of(c)], blocks.at[r, rows_of(c)], peer)
                    for r, peer in peers
                ]
                for copy in passed:
                    copy.wait_recv()
            for b in range(nb):
                i = b * per_block + c
                k.datt[i * Q_ROWS : (i + 1) * Q_ROWS, :] = dot_nn(
                    blocks[local ^ b, rows, :], k.w_out[...]
                ).astype(BF16)
                attention_backward_rows(k, tag, i, length, kv)
                scatter.pump()
        for j in range(kv):
            k_col = slice((4 * j + 2) * PAD, (4 * j + 3) * PAD)
            v_col = slice((4 * j + 3) * PAD, (4 * j + 4) * PAD)
            for i in range(seq_len // Q_ROWS):
                rows = slice(i * Q_ROWS, (i + 1) * Q_ROWS)
                dproj[rows, k_col] = unrotate(k, k.dk[j, rows, :] * SCALE, rows).astype(BF16)
                dproj[rows, v_col] = k.dv[j, rows, :].astype(BF16)
        for copy in late:
            copy.wait()
        late = []
        for c in range(per_block):
            rows = slice(c * Q_ROWS, (c + 1) * Q_ROWS)
            for b in range(nb):
                i = b * per_block + c
                part = dot_nt(dproj[i * Q_ROWS : (i + 1) * Q_ROWS, :], k.w_qkv[...])
                parts[local ^ b, rows, :] = part.astype(BF16)
            if tag == NEAR:
                for r, peer in peers:
                    k.remote(parts.at[r, rows_of(c)], k.near_got.at[r - 1, rows_of(c)], peer)
            else:
                copies = [
                    k.remote(parts.at[r, rows_of(c)], k.far_got.at[r - 1, rows_of(c)], peer)
                    for r, peer in peers
                ]
                total = parts[0, rows, :].astype(F32)
                for r, copy in enumerate(copies):
                    copy.wait_recv()
                    total = total + k.far_got[r, rows, :].astype(F32)
                parts[0, rows, :] = total.astype(BF16)
                k.remote(parts.at[0, rows_of(c)], k.landed.at[rows_of(c)], over)
        if tag == NEAR:
            k.store(parts.at[0], k.near_own)
        else:
            k.remote(k.far_out, k.out_landed, over)
        scatter.pump()
    width = k.w_qkv.shape[0]
    arriving = []
    for which in range(kv + 1):

        def chunk(c, carry):
            cols = pl.ds(pl.multiple_of(c * G_COLS, G_COLS), G_COLS)
            total = None
            if which == 0:
                wide = k.near_att.shape[1]
                for tag in (NEAR, FAR):
                    for r in range(nb):
                        start = pl.multiple_of((local ^ r) * rows_each, rows_each)
                        term = dot_tn(
                            k.of(tag).a[r, :, cols], k.of(tag).att[pl.ds(start, rows_each), :]
                        )
                        total = term if total is None else total + term
                compact = dot_nt(total.astype(BF16), k.spread[:, :wide])
            else:
                part = slice((which - 1) * G_PAD, which * G_PAD)
                total = dot_tn(k.near_normed[:, cols], k.near_dproj[:, part])
                total += dot_tn(k.far_normed[:, cols], k.far_dproj[:, part])
                compact = dot_nt(total.astype(BF16), k.spread[...])
            compact = compact.astype(BF16)
            for b in range(G_COLS // blk):
                owner = c * (G_COLS // blk) + b
                shift = lax.rem(owner // 2 + n_z - z, n_z)
                value = compact[b * blk : (b + 1) * blk, :]

                @pl.when(x == lax.rem(owner, 2))
                def _():
                    k.same[which, shift, :, :] = value

                @pl.when(x != lax.rem(owner, 2))
                def _():
                    k.other[which, shift, :, :] = value

            return carry

        lax.fori_loop(0, width // G_COLS, chunk, 0)
        arriving.append(k.remote(k.other.at[which], k.arrived.at[which], other_x))
        scatter.pump()
    while scatter.pump():
        pass
    for which in range(kv + 1):
        arriving[which].wait_recv()
        for i in z_order(n_z) + [0]:
            held = k.same[which, i, :, :].astype(F32) + k.arrived[which, i, :, :].astype(F32)
            k.same[which, i, :, :] = held.astype(BF16)
            if i:
                k.remote(k.same.at[which, i], k.sums.at[which, i], scatter.peers[i])
            else:
                k.store(k.same.at[which, 0], k.sums.at[which, 0])


def attention_backward(attention_grad, lengths, fwd, grads, far_out, tables, spread, nb, n_z, collective_id):
    rows_each, width = attention_grad.shape
    seq_len = nb * rows_each
    w_qkv, w_out = fwd["w_qkv"], fwd["w_out"]
    kv = w_qkv.shape[1] // G_PAD
    heads = kv * GROUP
    blk = width // (2 * n_z)
    units = grads.shape[2]
    sds = jax.ShapeDtypeStruct
    inputs = dict(
        lengths=(lengths, IN_SMEM),
        own_a=(attention_grad, IN_HBM),
        w_qkv=(w_qkv, LOAD),
        w_out=(w_out, LOAD),
        cos_t=(tables[0], LOAD),
        sin_t=(tables[1], LOAD),
        spread=(spread, LOAD),
        grads=(grads, IN_HBM),
        far_out=(far_out, IN_HBM),
    )
    for tag in (NEAR, FAR):
        for key in ("qkvp", "lse", "att", "normed"):
            inputs[tag + key] = (fwd[tag + key], LOAD)
    block = pltpu.VMEM((nb, rows_each, width), BF16)
    sums = sds((kv + 1, n_z, blk, G_COLS), BF16)
    own = (sds((rows_each, width), BF16), IN_HBM)
    return frame_call(
        functools.partial(attention_backward_body, nb, rows_each, kv, n_z, blk),
        "attention_backward",
        inputs,
        dict(
            near_own=own,
            near_got=(sds((nb - 1, rows_each, width), BF16), IN_HBM),
            landed=own,
            out_landed=own,
            sums=(sums, IN_HBM),
            x_got=(sds((3, n_z, blk, units), BF16), IN_HBM),
            ffn_sums=(sds((3, n_z, blk, units), BF16), IN_HBM),
        ),
        dict(
            near_a=block,
            far_a=block,
            near_parts=block,
            far_parts=block,
            far_got=pltpu.VMEM((nb - 1, rows_each, width), BF16),
            near_dproj=pltpu.VMEM((seq_len, kv * G_PAD), BF16),
            far_dproj=pltpu.VMEM((seq_len, kv * G_PAD), BF16),
            datt=pltpu.VMEM((seq_len, heads * PAD), BF16),
            dk=pltpu.VMEM((kv, seq_len, PAD), F32),
            dv=pltpu.VMEM((kv, seq_len, PAD), F32),
            same=pltpu.VMEM(sums.shape, BF16),
            other=pltpu.VMEM(sums.shape, BF16),
            arrived=pltpu.VMEM(sums.shape, BF16),
            staged=pltpu.VMEM((2, blk, units), BF16),
            narrow=pltpu.VMEM((SLOTS, blk, units), BF16),
        ),
        8 * seq_len * width * (kv * G_PAD + heads * PAD) + heads * seq_len * seq_len * 20 * 256,
        collective_id,
        n_sems=12 * n_z + 48,
    )


def all_peers(n_dp, n_t):
    d, t = lax.axis_index("dp"), lax.axis_index("tensor")
    return (
        [{"tensor": lax.rem(t + i, n_t)} for i in range(1, n_t)],
        [{"dp": lax.rem(d + i, n_dp)} for i in range(1, n_dp)],
    )


def share(k, buffer, me, peers):
    return [k.remote(buffer.at[me], buffer.at[me], peer) for peer in peers]


def sum_slots(buffer, copies):
    for copy in copies:
        copy.wait_recv()
    total = buffer[0, :, :]
    for i in range(1, len(copies) + 1):
        total = total + buffer[i, :, :]
    return total


def moments_kernel(names, kv, *refs):
    keys = [key + suffix for suffix in ("", "_first", "_second") for key in names] + ["gradient"]
    keys += ["gain_sum"] if "gains" in names else []
    keys += ["next_" + key + suffix for suffix in ("_first", "_second") for key in names]
    keys += ["update_" + key for key in names] + ["squares"]
    k = dict(zip(keys, refs))
    correct_one = 1.0 / (1.0 - BETA_ONE**STEP)
    correct_two = 1.0 / (1.0 - BETA_TWO**STEP)
    row = lax.broadcasted_iota(jnp.int32, (8, PAD), 0)
    lane = lax.broadcasted_iota(jnp.int32, (8, PAD), 1)
    squares = jnp.zeros((8, PAD), F32)
    gradient = k["gradient"]

    def step(name, index, gradient_of, rows, cols, number):
        tile = rows if rows % 32 else 32

        def one(i, carry):
            at = index + (pl.ds(pl.multiple_of(i * tile, tile) if rows > tile else 0, tile), slice(None))
            g = gradient_of(at)
            w = k[name][at]
            moment = BETA_ONE * k[name + "_first"][at] + (1.0 - BETA_ONE) * g
            square = BETA_TWO * k[name + "_second"][at] + (1.0 - BETA_TWO) * g * g
            k["next_" + name + "_first"][at] = moment
            k["next_" + name + "_second"][at] = square
            update = (moment * correct_one) / (
                jnp.sqrt(square * correct_two) + ADAM_EPSILON
            ) + WEIGHT_DECAY * w
            k["update_" + name][at] = update
            return (
                carry[0] + jnp.sum(w * w, axis=0, keepdims=True),
                carry[1] + jnp.sum(update * update, axis=0, keepdims=True),
            )

        zero = jnp.zeros((1, cols), F32)
        w_sum, u_sum = lax.fori_loop(0, rows // tile, one, (zero, zero))
        w_sum = jnp.sum(w_sum, axis=1, keepdims=True)
        u_sum = jnp.sum(u_sum, axis=1, keepdims=True)
        mark = lane == number
        return jnp.where(mark & (row == 0), w_sum, 0.0) + jnp.where(mark & (row == 1), u_sum, 0.0)

    def z_sum(which, rows, cols=slice(None)):
        total = gradient[which, 0, rows, cols].astype(F32)
        for i in range(1, gradient.shape[1]):
            total = total + gradient[which, i, rows, cols].astype(F32)
        return total

    def qkv_gradient(at):
        return jnp.concatenate([z_sum(1 + j, at[0]) for j in range(kv)], axis=1)

    if "qkv" in names:
        squares += step("qkv", (), qkv_gradient, *k["qkv"].shape, 0)
    if "out" in names:
        rows, cols = k["out"].shape
        squares += step("out", (), lambda at: z_sum(0, at[0], slice(0, cols)), rows, cols, 1)
    if "gate_up" in names:
        for which in range(2):
            squares += step(
                "gate_up", (which,), lambda at: z_sum(at[0], at[1]), *k["gate_up"].shape[1:], 2 + which
            )
    if "down" in names:
        squares += step(
            "down", (), lambda at: z_sum(2, at[0]), *k["down"].shape, 4
        )
    if "gains" in names:
        for which in range(2):
            squares += step(
                "gains", (which,), lambda at: k["gain_sum"][at], *k["gains"].shape[1:], 5 + which
            )
    k["squares"][...] = squares


def moments(weights, firsts, seconds, gradient, gain_sum, kv):
    names = list(weights)
    arrays = [table[key] for table in (weights, firsts, seconds) for key in names] + [gradient]
    arrays += [] if gain_sum is None else [gain_sum]
    sds = jax.ShapeDtypeStruct
    shapes = [sds(weights[key].shape, F32) for key in names]
    results = pl.pallas_call(
        functools.partial(moments_kernel, names, kv),
        out_shape=shapes * 3 + [sds((8, PAD), F32)],
        in_specs=[VM] * len(arrays),
        out_specs=[VM] * (3 * len(names) + 1),
        compiler_params=pltpu.CompilerParams(vmem_limit_bytes=VMEM_LIMIT),
        cost_estimate=cost(0, 14 << 20),
        name="moments",
    )(*arrays)
    n = len(names)
    return (
        dict(zip(names, results[:n])),
        dict(zip(names, results[n : 2 * n])),
        dict(zip(names, results[2 * n : 3 * n])),
        results[-1],
    )


def sum_all_body(n_dp, n_t, k):
    d, t = lax.axis_index("dp"), lax.axis_index("tensor")
    tensor_peers, dp_peers = all_peers(n_dp, n_t)
    k.first[t, :, :] = k.value[...]
    k.meet(tensor_peers + dp_peers)
    copies = share(k, k.first, t, tensor_peers)
    k.second[d, :, :] = sum_slots(k.first, copies)
    copies = share(k, k.second, d, dp_peers)
    k.total[...] = sum_slots(k.second, copies)


def sum_all(value, n_dp, n_t, collective_id):
    return frame_call(
        functools.partial(sum_all_body, n_dp, n_t),
        "sum_everywhere",
        dict(value=(value, IN_VMEM)),
        dict(total=(jax.ShapeDtypeStruct(value.shape, F32), IN_VMEM)),
        dict(
            first=pltpu.VMEM((n_t,) + value.shape, F32),
            second=pltpu.VMEM((n_dp,) + value.shape, F32),
        ),
        0,
        collective_id,
        n_sems=n_dp + n_t,
    )["total"]


def rms_norm(values, gain_row):
    return (
        values
        * lax.rsqrt(jnp.mean(values * values, axis=-1, keepdims=True) + NORM_EPSILON)
        * gain_row
    )


def rotary_tables():
    half = HEAD // 2
    frequency = ROPE_THETA ** (-(jnp.arange(half, dtype=F32) * (2.0 / HEAD)))
    angles = jnp.arange(SEQ_LEN, dtype=F32)[:, None] * frequency[None, :]
    cosine, sine = jnp.cos(angles), jnp.sin(angles)
    empty = jnp.zeros((SEQ_LEN, PAD - HEAD), F32)
    return (
        jnp.concatenate([cosine, cosine, empty], axis=1),
        jnp.concatenate([-sine, sine, empty], axis=1),
    )


def shards(
    tokens,
    cotangent,
    lengths,
    qkv_weight,
    out_weight,
    gate_up_weight,
    down_weight,
    norm_gains,
    qkv_first,
    out_first,
    gate_up_first,
    down_first,
    gains_first,
    qkv_second,
    out_second,
    gate_up_second,
    down_second,
    gains_second,
):
    rows_each, width = tokens.shape
    n_t = lax.axis_size("tensor")
    n_dp = lax.axis_size("dp")
    n_z = n_dp // 2
    nb = n_t // 2
    t = lax.axis_index("tensor")
    d = lax.axis_index("dp")
    mine = t // nb
    lengths = jnp.stack([lengths[mine], lengths[1 - mine]])
    spread = spread_matrix().astype(BF16)
    blk = qkv_weight.shape[0]
    kv = qkv_weight.shape[1] // G_COLS

    gain_cols = norm_gains.shape[1]
    gain_start = (d * n_t + t) * gain_cols
    gain_rows = lax.dynamic_update_slice(
        jnp.zeros((2, width), F32),
        norm_gains.astype(BF16).astype(F32),
        (0, gain_start),
    )
    out_half = out_weight.astype(BF16).T
    ffn_half = jnp.concatenate(
        [gate_up_weight.astype(BF16), down_weight.astype(BF16).T[None]], axis=0
    )
    halves = (qkv_weight.astype(BF16), out_half, ffn_half)
    tables = rotary_tables()
    fwd = opening(
        tokens, cotangent, lengths, gain_rows, halves, tables, spread, n_t, n_z, 0
    )
    inputs = tokens.astype(F32)
    attention_gain, feedforward_gain = fwd["gain_sum"][0:1], fwd["gain_sum"][1:2]
    residual = fwd["residual"]

    ff = feed_forward(fwd["normed_two"], cotangent, fwd["c_far"], fwd["w_ffn"], nb, 2)

    def total(*arrays):
        result = 0.0
        for array in arrays:
            array = array.astype(F32)
            result = result + (array if array.ndim == 2 else jnp.sum(array, axis=0))
        return result

    normed_two_grad = total(ff["near_own_grad"], ff["near_got_grad"], ff["landed"])
    _, norm_pull = jax.vjp(rms_norm, residual, feedforward_gain)
    residual_part, ffn_gain_grad = norm_pull(normed_two_grad)
    residual_grad = cotangent.astype(F32) + residual_part
    far_out = total(ff["far_own_out"], ff["far_got_out"]).astype(BF16)
    bwd = attention_backward(
        residual_grad.astype(BF16), lengths, fwd, ff["grads"], far_out, tables, spread, nb, n_z, 3
    )
    normed_grad = total(bwd["near_own"], bwd["near_got"], bwd["landed"])
    _, first_pull = jax.vjp(rms_norm, inputs, attention_gain)
    input_part, attention_gain_grad = first_pull(normed_grad)
    grad_tokens = residual_grad + input_part
    gain_grads = jnp.concatenate([attention_gain_grad, ffn_gain_grad], axis=0)
    gain_all = sum_all(gain_grads.reshape(-1, PAD), n_dp, n_t, 4).reshape(2, width)
    layer_out = (residual + total(ff["near_own_out"], ff["near_got_out"], bwd["out_landed"])).astype(
        BF16
    )
    gain_sum = lax.dynamic_slice(gain_all, (0, gain_start), (2, gain_cols))

    def lift(gains):
        return gains[:, None, :]

    gate_down = moments(
        dict(gate_up=gate_up_weight, down=down_weight.T),
        dict(gate_up=gate_up_first, down=down_first.T),
        dict(gate_up=gate_up_second, down=down_second.T),
        bwd["ffn_sums"],
        None,
        kv,
    )
    attention = moments(
        dict(qkv=qkv_weight, out=out_weight.T, gains=lift(norm_gains)),
        dict(qkv=qkv_first, out=out_first.T, gains=lift(gains_first)),
        dict(qkv=qkv_second, out=out_second.T, gains=lift(gains_second)),
        bwd["sums"],
        lift(gain_sum),
        kv,
    )
    norms = jnp.sqrt(sum_all(gate_down[3] + attention[3], n_dp, n_t, 5))
    scale = LEARN_RATE * (norms[0, :7] / norms[1, :7])
    first, second, update = ({**gate_down[i], **attention[i]} for i in range(3))
    for table in (first, second, update):
        table["gains"] = table["gains"][:, 0, :]
        table["out"] = table["out"].T
        table["down"] = table["down"].T
    new = (
        qkv_weight - scale[0] * update["qkv"],
        out_weight - scale[1] * update["out"],
        gate_up_weight - scale[2:4, None, None] * update["gate_up"],
        down_weight - scale[4] * update["down"],
        norm_gains - scale[5:7, None] * update["gains"],
    )
    names = ("qkv", "out", "gate_up", "down", "gains")
    return (
        layer_out,
        grad_tokens,
        *new,
        *[first[key] for key in names],
        *[second[key] for key in names],
        norms[0, :7],
        norms[1, :5],
        norms[1, 5:7],
    )


def solution(mesh):
    rows = P(("dp", "tensor"), None)
    gains = P(None, ("dp", "tensor"))
    weights = (P("dp", "tensor"), P("tensor", "dp"), P(None, "dp", "tensor"), P("tensor", "dp"), gains)
    in_specs = (rows, rows, P("dp")) + weights * 3
    out_specs = (rows, rows) + weights * 3 + (P(), P(), P())
    return jax.shard_map(shards, mesh=mesh, in_specs=in_specs, out_specs=out_specs, check_vma=False)
```

time: 581 us -> 520 us (0.90)
  Pallas kernels: 497 us -> 462 us
  between operations: 14.9 us -> 1.48 us
  local copies, waits for them, and re-layouts: 13.6 us -> 7.18 us
    pallas_call x2 -> x0, Pallas kernels: 119 us -> none  [the longest x1 113 us: prologue(): pl.pallas_call(functools.partial(prologue_kernel, n_z, n_t, blk), out_sha...]
    pallas_call x5, Pallas kernels: 364 us -> 446 us  [frame_call(): pl.pallas_call(kernel, out_shape=out_shapes, in_specs=specs, out_specs=ou...]
  transfers between devices with their start and end apart: 2 -> 0, of which waited for: 0 -> 0; matrix products, arithmetic and copies ran while one was open for 6% -> 0% of each run, Pallas kernels for 70% -> 0%
where the time goes in v4:
time: 520 us; the launch traced here: 511 us
  Pallas kernels  462 us (89%)
  other arithmetic  39.9 us (8%)
  local copies, waits for them, and re-layouts  7.18 us (1%)
    pallas_call x5, Pallas kernels, frame_call(): pl.pallas_call(kernel, out_shape=out_shapes, in_specs=specs, out_specs=ou...  446 us
    pallas_call x2, Pallas kernels, moments(): pl.pallas_call(functools.partial(moments_kernel, names, kv), out_shape=sh...  16 us

profile of v4, /device:TPU:0, one launch (start us, length us, event | category | flops | bytes accessed | tf_op | source)
XLA Modules:
  0.0 510.5 jit_solution(9658654264196115351)
XLA Ops:
  0.7 1.4 fusion.31
  2.1 1.9 pad_add_fusion.refs_2_.refs_0_
  3.9 0.7 convert_convert_fusion
  4.8 2.0 fusion.17
  6.8 1.3 maximum_maximum_fusion.1
  8.2 0.9 fusion.14.refs_9_.refs_6_
  9.2 1.1 pad_maximum_fusion.refs_6_
  10.4 0.7 convert_element_type.65.refs_4_
  11.1 0.7 convert_bitcast_fusion.1.refs_5_
  11.8 188.9 %attention_forward.1 = (bf16[1024,1536]{1,0:T(8,128)(2,1)}, bf16[1024,1536]{1,0:T(8,128)(2,1)}, bf16[1024,1024]{1,0:T(8,128)(2,1)}, bf16[1024,1024]{1,0:T(8,128)...) custom-call(bf16[512,1536]{1,0:T(8,128)(2,1)} %refs_0_.3, ...), custom_call_target="tpu_custom_call" | custom-call | flops 18253611008 | bytes 6221832 | tf_op jit(solution)/shard_map/attention_forward/pallas_call | solution.py:206
  200.7 76.4 %feed_forward.1 = (bf16[3,1536,1024]{2,1,0:T(8,128)(2,1)}, bf16[512,1536]{1,0:T(8,128)(2,1)}, bf16[1,512,1536]{2,1,0:T(8,128)(2,1)}, bf16[512,1536]{1,0:T(8,128)...) custom-call(bf16[512,1536]{1,0:T(8,128)(2,1)} %get-tuple-element.67., ...), custom_call_target="tpu_custom_call" | custom-call | flops 57982058496 | bytes 14155776 | tf_op jit(solution)/shard_map/feed_forward/pallas_call | solution.py:206
  277.1 3.6 fusion.7.refs_8_
  281.8 1.2 multiply_reduce_fusion
  283.3 3.5 fusion.27
  286.7 159.3 %attention_backward.1 = (bf16[512,1536]{1,0:T(8,128)(2,1)}, bf16[1,512,1536]{2,1,0:T(8,128)(2,1)}, bf16[512,1536]{1,0:T(8,128)(2,1)}, bf16[512,1536]{1,0:T(8,128...) custom-call(s32[2]{0:T(128)} %pad_add_fusion.refs_2_.refs_0_, ...), custom_call_target="tpu_custom_call" | custom-call | flops 40802189312 | bytes 32374792 | tf_op jit(solution)/shard_map/attention_backward/pallas_call | solution.py:206
  446.4 3.8 fusion.5
  450.2 0.6 reshape.102.refs_0_
  450.9 10.4 %sum_everywhere.2 = f32[24,128]{1,0:T(8,128)} custom-call(f32[24,128]{1,0:T(8,128)} %reshape.102.refs_0_), custom_call_target="tpu_custom_call" | custom-call | bytes 12288 | tf_op jit(solution)/shard_map/sum_everywhere/pallas_call | solution.py:206
  461.3 0.7 reshape.103
  462.0 0.6 constant_dynamic-slice_fusion
  462.6 5.0 moments.3
  467.7 10.9 %moments.2 = (f32[2,192,1024]{2,1,0:T(8,128)}, f32[192,1024]{1,0:T(8,128)}, f32[2,192,1024]{2,1,0:T(8,128)}, f32[192,1024]{1,0:T(8,128)}, f32[2,192,1024]{2,1,0:...) custom-call(f32[2,192,1024]{2,1,0:T(8,128)} %refs_0_.4, f32[192,1024]{1,0:T(8,128)} %bitcast.74, ...), custom_call_target="tpu_custom_call" | custom-call | bytes 14680064 | tf_op jit(solution)/shard_map/moments/pallas_call | solution.py:1081
  478.6 1.4 add.104.refs_0_
  480.0 11.1 %sum_everywhere.3 = f32[8,128]{1,0:T(8,128)} custom-call(f32[8,128]{1,0:T(8,128)} %add.104.refs_0_), custom_call_target="tpu_custom_call" | custom-call | bytes 4096 | tf_op jit(solution)/shard_map/sum_everywhere/pallas_call | solution.py:206
  491.2 0.7 sqrt.3
  492.5 0.6 multiply_subtract_fusion.2
  493.7 2.9 bitcast_subtract_fusion
  496.6 3.2 multiply_subtract_fusion
  499.8 1.4 bitcast_subtract_fusion.1
  501.2 2.6 multiply_subtract_fusion.1
  505.0 2.9 fusion.1
  507.9 2.2 fusion.11
  (81 shorter events, 4.6 us)
Async XLA Ops:
  0.7 8.4 %copy-start.3 = (f32[2,192,1024]{2,1,0:T(8,128)S(1)}, f32[2,192,1024]{2,1,0:T(8,128)}, u32[]{:S(2)}) copy-start(f32[2,192,1024]{2,1,0:T(8,128)} %refs_0_.4) | copy-start | bytes 4718596
  4.7 4.4 copy-start.24
  4.8 4.4 copy-start.6
  8.2 2.2 copy-start.14
  9.0 2.1 copy-start.16
  277.0 3.6 copy-start.23
  277.0 3.6 copy-start
  277.0 3.9 copy-start.8
  277.1 4.3 copy-start.9
  277.1 4.8 copy-start.10
  281.8 1.4 copy-start.18
  286.7 159.3 %copy-start.1 = (bf16[512,1536]{1,0:T(8,128)(2,1)S(1)}, bf16[512,1536]{1,0:T(8,128)(2,1)}, u32[]{:S(2)}) copy-start(bf16[512,1536]{1,0:T(8,128)(2,1)} %refs_0_.3) | copy-start | bytes 4718596
  467.7 11.0 %copy-start.26 = (f32[8,128]{1,0:T(8,128)S(1)}, f32[8,128]{1,0:T(8,128)}, u32[]{:S(2)}) copy-start(f32[8,128]{1,0:T(8,128)} %get-tuple-element.96) | copy-start | bytes 12292
  467.7 24.8 %copy-start.25 = (f32[2,48]{1,0:T(2,128)S(1)}, f32[2,48]{1,0:T(2,128)}, u32[]{:S(2)}) copy-start(f32[2,48]{1,0:T(2,128)} %param.25) | copy-start | bytes 1156
  467.7 24.8 %copy-start.27 = (f32[2,1,48]{2,1,0:T(1,128)S(1)}, f32[2,1,48]{2,1,0:T(1,128)}, u32[]{:S(2)}) copy-start(f32[2,1,48]{2,1,0:T(1,128)} %get-tuple-element.101) | copy-start | bytes 1156
  467.7 26.0 %copy-start.7 = (f32[1024,192]{0,1:T(8,128)S(1)}, f32[1024,192]{0,1:T(8,128)}, u32[]{:S(2)}) copy-start(f32[1024,192]{0,1:T(8,128)} %param.24) | copy-start | bytes 2359300
  467.7 32.1 %copy-start.22 = (f32[192,384]{1,0:T(8,128)S(1)}, f32[192,384]{1,0:T(8,128)}, u32[]{:S(2)}) copy-start(f32[192,384]{1,0:T(8,128)} %get-tuple-element.98) | copy-start | bytes 884740
  467.7 33.5 %copy-start.15 = (f32[192,768]{1,0:T(8,128)S(1)}, f32[192,768]{1,0:T(8,128)}, u32[]{:S(2)}) copy-start(f32[192,768]{1,0:T(8,128)} %refs_0_.5) | copy-start | bytes 1769476
  467.7 37.2 %copy-start.13 = (bf16[512,1536]{1,0:T(8,128)(2,1)S(1)}, bf16[512,1536]{1,0:T(8,128)(2,1)}, u32[]{:S(2)}) copy-start(bf16[512,1536]{1,0:T(8,128)(2,1)} %get-tuple-element.92) | copy-start | bytes 4718596
  478.6 18.0 %copy-start.4 = (f32[2,192,1024]{2,1,0:T(8,128)S(1)}, f32[2,192,1024]{2,1,0:T(8,128)}, u32[]{:S(2)}) copy-start(f32[2,192,1024]{2,1,0:T(8,128)} %refs_0_.4) | copy-start | bytes 4718596
  493.7 6.1 %copy-start.17 = (f32[384,192]{0,1:T(8,128)S(1)}, f32[384,192]{0,1:T(8,128)}, u32[]{:S(2)}) copy-start(f32[384,192]{0,1:T(8,128)} %param.22) | copy-start | bytes 884740
  493.7 11.2 %copy-start.12 = (bf16[1,512,1536]{2,1,0:T(8,128)(2,1)S(1)}, bf16[1,512,1536]{2,1,0:T(8,128)(2,1)}, u32[]{:S(2)}) copy-start(bf16[1,512,1536]{2,1,0:T(8,128)(2,1)} %get-tuple-element.91) | copy-start | bytes 4718596
  496.6 8.3 %copy-start.2 = (bf16[512,1536]{1,0:T(8,128)(2,1)S(1)}, bf16[512,1536]{1,0:T(8,128)(2,1)}, u32[]{:S(2)}) copy-start(bf16[512,1536]{1,0:T(8,128)(2,1)} %refs_0_.3) | copy-start | bytes 4718596
  496.6 8.3 %copy-start.5 = (f32[512,1536]{1,0:T(8,128)S(1)}, f32[512,1536]{1,0:T(8,128)}, u32[]{:S(2)}) copy-start(f32[512,1536]{1,0:T(8,128)} %get-tuple-element.121) | copy-start | bytes 9437188
  496.6 8.3 %copy-start.11 = (bf16[512,1536]{1,0:T(8,128)(2,1)S(1)}, bf16[512,1536]{1,0:T(8,128)(2,1)}, u32[]{:S(2)}) copy-start(bf16[512,1536]{1,0:T(8,128)(2,1)} %get-tuple-element.90) | copy-start | bytes 4718596
  504.9 2.9 copy-start.19
  505.0 2.9 copy-start.20
  505.0 2.9 copy-start.21

commit v5 on v4

--- a/solution.py
+++ b/solution.py
@@ -78,18 +78,28 @@
 
 
 class Remote:
-    def __init__(self, copy):
-        self.copy = copy
+    def __init__(self, copy, sends=None, receives=None):
+        self.copy, self.sends, self.receives = copy, sends, receives
         self.landed = self.left = False
+
+    @staticmethod
+    def only(condition, action):
+        if condition is None:
+            action()
+        else:
+            pl.when(condition)(action)
+
+    def start(self):
+        self.only(self.sends, self.copy.start)
 
     def wait_recv(self):
         if not self.landed:
-            self.copy.wait_recv()
+            self.only(self.receives, self.copy.wait_recv)
         self.landed = True
 
     def wait_send(self):
         if not self.left:
-            self.copy.wait_send()
+            self.only(self.sends, self.copy.wait_send)
         self.left = True
 
 
@@ -150,7 +160,7 @@
     def flush(self, source, target):
         self.store(source, target)
 
-    def remote(self, source, target, peer):
+    def remote(self, source, target, peer, sends=None, receives=None):
         n = len(self.remotes)
         copy = pltpu.make_async_remote_copy(
             src_ref=source,
@@ -160,8 +170,8 @@
             device_id=peer,
             device_id_type=MESH,
         )
-        copy.start()
-        self.remotes.append(Remote(copy))
+        self.remotes.append(Remote(copy, sends, receives))
+        self.remotes[-1].start()
         return self.remotes[-1]
 
     def finish(self):
@@ -275,43 +285,59 @@
 class Gather:
     def __init__(self, k, streams, n_z, blk):
         d = lax.axis_index("dp")
-        self.k, self.streams = k, streams
-        self.peers, self.other_x = z_peers(n_z), permuted("dp", 1)
-        self.order = [(s, i) for s in range(len(streams)) for i in z_order(n_z)]
+        self.k, self.streams, self.n_z = k, streams, n_z
+        self.z = d // 2
+        self.right = {"dp": lax.rem(d + 2, 2 * n_z)}
+        self.left = {"dp": lax.rem(d + 2 * n_z - 2, 2 * n_z)}
+        self.other_x = permuted("dp", 1)
+        self.order = [(s, hop) for s in range(len(streams)) for hop in range(1, n_z)]
         self.rows = {
             i: pl.ds(pl.multiple_of(lax.rem(d + 2 * (n_z - i), 2 * n_z) * blk, 16), blk)
             for i in range(n_z)
         }
         self.sent, self.along_x = {}, {}
-        self.next_send = self.next_arrival = 0
-
-    def send(self):
-        if self.next_send < len(self.order):
-            s, i = self.order[self.next_send]
-            source, target, at = self.streams[s]
-            self.sent[s, i] = self.k.remote(source, target.at[at + (self.rows[0],)], self.peers[i])
-            self.next_send += 1
+        self.next_arrival = 0
+
+    def send(self, s, hop):
+        if s >= len(self.streams) or (s, hop) in self.sent:
+            return
+        source, target, at = self.streams[s]
+        z, n_z, far = self.z, self.n_z, hop - 1
+        pair = []
+        for shift, peer, sends, receives in (
+            (far, self.right, (z >= far) & (z < n_z - 1), z >= hop),
+            ((n_z - far) % n_z, self.left, (z < n_z - far) & (z > 0), z < n_z - hop),
+        ):
+            block = target.at[at + (self.rows[shift],)]
+            pair.append(self.k.remote(block if far else source, block, peer, sends, receives))
+        self.sent[s, hop] = pair
 
     def own_along_x(self, s):
         source, target, at = self.streams[s]
-        self.along_x[s, 0] = self.k.remote(source, target.at[at + (self.rows[0],)], self.other_x)
+        block = target.at[at + (self.rows[0],)]
+        self.along_x.setdefault(s, []).append(self.k.remote(source, block, self.other_x))
 
     def pump(self):
-        if self.next_arrival < len(self.order):
-            s, i = self.order[self.next_arrival]
-            self.next_arrival += 1
-            self.sent[s, i].wait_recv()
-            self.send()
-            if (s, 0) not in self.along_x:
-                self.own_along_x(s)
-            _, target, at = self.streams[s]
-            block = target.at[at + (self.rows[i],)]
-            self.along_x[s, i] = self.k.remote(block, block, self.other_x)
+        if self.next_arrival == len(self.order):
+            return
+        s, hop = self.order[self.next_arrival]
+        self.next_arrival += 1
+        for copy in self.sent[s, hop]:
+            copy.wait_recv()
+        if hop + 1 < self.n_z:
+            self.send(s, hop + 1)
+        if hop == min(2, self.n_z - 1):
+            self.send(s + 1, 1)
+        _, target, at = self.streams[s]
+        for shift, copy in zip((hop, self.n_z - hop), self.sent[s, hop]):
+            block = target.at[at + (self.rows[shift],)]
+            self.along_x[s].append(
+                self.k.remote(block, block, self.other_x, copy.receives, copy.receives)
+            )
 
     def complete(self, s):
-        for (stream, _), copy in self.along_x.items():
-            if stream == s:
-                copy.wait_recv()
+        for copy in self.along_x[s]:
+            copy.wait_recv()
 
 
 def opening_body(nb, rows_each, kv, n_z, blk, k):
@@ -340,8 +366,8 @@
     gain_copy = k.remote(k.held.at[0], k.got.at[0], stages[0])
     far_copy = k.remote(k.tokens, far_x.at[0], over)
     near_copies = [k.remote(k.tokens, near_x.at[r], peer) for r, peer in peers]
-    for _ in range(WINDOW):
-        gather.send()
+    gather.send(0, 1)
+    gather.send(1, 1)
     for stage in range(len(stages)):
         gain_copy.wait_recv()
         k.held[stage + 1, :, :] = k.held[stage, :, :] + k.got[stage, :, :]
@@ -795,12 +821,14 @@
     for tag in (NEAR, FAR):
         late.append(k.local(k.hbm.of(tag).att, k.of(tag).att))
         late.append(k.local(k.hbm.of(tag).normed, k.of(tag).normed))
-    k.meet([over, other_x] + [peer for _, peer in peers] + list(z_peers(n_z).values()))
+    tensor_peers, dp_peers = all_peers(2 * n_z, 2 * nb)
+    k.meet(tensor_peers + dp_peers)
     far_first = [
         k.remote(k.own_a.at[rows_of(c)], k.far_a.at[0, rows_of(c)], over)
         for c in range(per_block)
     ]
     near_copies = [k.remote(k.own_a, k.near_a.at[r], peer) for r, peer in peers]
+    landing, near_landing = [], []
     scatter = Scatter(k, n_z, blk)
     for _ in range(WINDOW):
         scatter.send()
@@ -847,7 +875,9 @@
                 parts[local ^ b, rows, :] = part.astype(BF16)
             if tag == NEAR:
                 for r, peer in peers:
-                    k.remote(parts.at[r, rows_of(c)], k.near_got.at[r - 1, rows_of(c)], peer)
+                    near_landing.append(
+                        k.remote(parts.at[r, rows_of(c)], k.near_got.at[r - 1, rows_of(c)], peer)
+                    )
             else:
                 copies = [
                     k.remote(parts.at[r, rows_of(c)], k.far_got.at[r - 1, rows_of(c)], peer)
@@ -858,11 +888,9 @@
                     copy.wait_recv()
                     total = total + k.far_got[r, rows, :].astype(F32)
                 parts[0, rows, :] = total.astype(BF16)
-                k.remote(parts.at[0, rows_of(c)], k.landed.at[rows_of(c)], over)
+                landing.append(k.remote(parts.at[0, rows_of(c)], k.landed.at[rows_of(c)], over))
         if tag == NEAR:
             k.store(parts.at[0], k.near_own)
-        else:
-            k.remote(k.far_out, k.out_landed, over)
         scatter.pump()
     width = k.w_qkv.shape[0]
     arriving = []
@@ -904,6 +932,8 @@
 
         lax.fori_loop(0, width // G_COLS, chunk, 0)
         arriving.append(k.remote(k.other.at[which], k.arrived.at[which], other_x))
+        if which == 0:
+            k.remote(k.far_out, k.out_landed, over)
         scatter.pump()
     while scatter.pump():
         pass
@@ -916,9 +946,34 @@
                 k.remote(k.same.at[which, i], k.sums.at[which, i], scatter.peers[i])
             else:
                 k.store(k.same.at[which, 0], k.sums.at[which, 0])
-
-
-def attention_backward(attention_grad, lengths, fwd, grads, far_out, tables, spread, nb, n_z, collective_id):
+    for copy in landing + near_landing:
+        copy.wait_recv()
+    k.flush(k.near_got, k.hbm.near_got)
+    loads = [k.local(k.landed, k.near_a.at[0]), k.local(k.tokens, k.near_a.at[1])]
+    for copy in loads:
+        copy.wait()
+
+    def gain_rows(i, carry):
+        rows = pl.ds(pl.multiple_of(i * 32, 32), 32)
+        dn = k.near_parts[0, rows, :].astype(F32) + k.near_a[0, rows, :].astype(F32)
+        for r in range(nb - 1):
+            dn = dn + k.near_got[r, rows, :].astype(F32)
+        v = k.near_a[1, rows, :].astype(F32)
+        inv = lax.rsqrt(jnp.mean(v * v, axis=-1, keepdims=True) + NORM_EPSILON)
+        return carry + jnp.sum(dn * v * inv, axis=0, keepdims=True)
+
+    t = lax.axis_index("tensor")
+    k.first[t, 0:1, :] = lax.fori_loop(0, rows_each // 32, gain_rows, jnp.zeros((1, width), F32))
+    k.first[t, 1:2, :] = k.gain_part[...]
+    gain_copies = share(k, k.first, t, tensor_peers)
+    k.second[d, :, :] = sum_slots(k.first, gain_copies)
+    gain_copies = share(k, k.second, d, dp_peers)
+    k.gain_sums[...] = sum_slots(k.second, gain_copies)
+
+
+def attention_backward(
+    attention_grad, tokens, gain_part, lengths, fwd, grads, far_out, tables, spread, nb, n_z, collective_id
+):
     rows_each, width = attention_grad.shape
     seq_len = nb * rows_each
     w_qkv, w_out = fwd["w_qkv"], fwd["w_out"]
@@ -937,6 +992,8 @@
         spread=(spread, LOAD),
         grads=(grads, IN_HBM),
         far_out=(far_out, IN_HBM),
+        tokens=(tokens, IN_HBM),
+        gain_part=(gain_part, IN_VMEM),
     )
     for tag in (NEAR, FAR):
         for key in ("qkvp", "lse", "att", "normed"):
@@ -950,9 +1007,10 @@
         inputs,
         dict(
             near_own=own,
-            near_got=(sds((nb - 1, rows_each, width), BF16), IN_HBM),
+            near_got=(sds((nb - 1, rows_each, width), BF16), FLUSH),
             landed=own,
             out_landed=own,
+            gain_sums=(sds((2, width), F32), IN_VMEM),
             sums=(sums, IN_HBM),
             x_got=(sds((3, n_z, blk, units), BF16), IN_HBM),
             ffn_sums=(sds((3, n_z, blk, units), BF16), IN_HBM),
@@ -972,6 +1030,8 @@
             other=pltpu.VMEM(sums.shape, BF16),
             arrived=pltpu.VMEM(sums.shape, BF16),
             staged=pltpu.VMEM((2, blk, units), BF16),
+            first=pltpu.VMEM((2 * nb, 2, width), F32),
+            second=pltpu.VMEM((2 * n_z, 2, width), F32),
             narrow=pltpu.VMEM((SLOTS, blk, units), BF16),
         ),
         8 * seq_len * width * (kv * G_PAD + heads * PAD) + heads * seq_len * seq_len * 20 * 256,
@@ -1211,18 +1271,27 @@
     residual_grad = cotangent.astype(F32) + residual_part
     far_out = total(ff["far_own_out"], ff["far_got_out"]).astype(BF16)
     bwd = attention_backward(
-        residual_grad.astype(BF16), lengths, fwd, ff["grads"], far_out, tables, spread, nb, n_z, 3
+        residual_grad.astype(BF16),
+        tokens,
+        ffn_gain_grad,
+        lengths,
+        fwd,
+        ff["grads"],
+        far_out,
+        tables,
+        spread,
+        nb,
+        n_z,
+        3,
     )
     normed_grad = total(bwd["near_own"], bwd["near_got"], bwd["landed"])
     _, first_pull = jax.vjp(rms_norm, inputs, attention_gain)
-    input_part, attention_gain_grad = first_pull(normed_grad)
+    input_part, _ = first_pull(normed_grad)
     grad_tokens = residual_grad + input_part
-    gain_grads = jnp.concatenate([attention_gain_grad, ffn_gain_grad], axis=0)
-    gain_all = sum_all(gain_grads.reshape(-1, PAD), n_dp, n_t, 4).reshape(2, width)
     layer_out = (residual + total(ff["near_own_out"], ff["near_got_out"], bwd["out_landed"])).astype(
         BF16
     )
-    gain_sum = lax.dynamic_slice(gain_all, (0, gain_start), (2, gain_cols))
+    gain_sum = lax.dynamic_slice(bwd["gain_sums"], (0, gain_start), (2, gain_cols))
 
     def lift(gains):
         return gains[:, None, :]

time: 520 us -> 488 us (0.938)
  Pallas kernels: 462 us -> 430 us
    pallas_call x5 -> x4, Pallas kernels: 446 us -> 414 us  [frame_call(): pl.pallas_call(kernel, out_shape=out_shapes, in_specs=specs, out_specs=ou...]
where the time goes in v5:
time: 488 us; the launch traced here: 479 us
  Pallas kernels  430 us (88%)
  other arithmetic  41.2 us (8%)
  local copies, waits for them, and re-layouts  6.19 us (1%)
    pallas_call x4, Pallas kernels, frame_call(): pl.pallas_call(kernel, out_shape=out_shapes, in_specs=specs, out_specs=ou...  414 us
    pallas_call x2, Pallas kernels, moments(): pl.pallas_call(functools.partial(moments_kernel, names, kv), out_shape=sh...  15.9 us

profile of v5, /device:TPU:0, one launch (start us, length us, event | category | flops | bytes accessed | tf_op | source)
XLA Modules:
  0.0 478.8 jit_solution(12825877297832773101)
XLA Ops:
  0.7 1.4 fusion.30
  2.1 1.9 pad_add_fusion.refs_2_.refs_0_
  4.0 0.7 convert_convert_fusion
  4.9 1.6 convert_bitcast_fusion.1.refs_5_
  6.6 1.8 convert_element_type.65.refs_4_
  8.4 0.9 fusion.13.refs_9_.refs_6_
  9.3 1.2 convert_bitcast_fusion
  10.6 1.1 pad_maximum_fusion.refs_6_
  11.7 2.0 fusion.16
  13.7 1.3 maximum_maximum_fusion.1
  15.0 162.8 %attention_forward.1 = (bf16[1024,1536]{1,0:T(8,128)(2,1)}, bf16[1024,1536]{1,0:T(8,128)(2,1)}, bf16[1024,1024]{1,0:T(8,128)(2,1)}, bf16[1024,1024]{1,0:T(8,128)...) custom-call(bf16[512,1536]{1,0:T(8,128)(2,1)} %refs_9_.1, ...), custom_call_target="tpu_custom_call" | custom-call | flops 18253611008 | bytes 6221832 | tf_op jit(solution)/shard_map/attention_forward/pallas_call | solution.py:216
  177.8 2.2 multiply_reduce_fusion.2
  180.0 76.9 %feed_forward.1 = (bf16[3,1536,1024]{2,1,0:T(8,128)(2,1)}, bf16[512,1536]{1,0:T(8,128)(2,1)}, bf16[1,512,1536]{2,1,0:T(8,128)(2,1)}, bf16[512,1536]{1,0:T(8,128)...) custom-call(bf16[512,1536]{1,0:T(8,128)(2,1)} %get-tuple-element.68., ...), custom_call_target="tpu_custom_call" | custom-call | flops 57982058496 | bytes 14155776 | tf_op jit(solution)/shard_map/feed_forward/pallas_call | solution.py:216
  257.0 3.9 multiply_reduce_fusion
  261.6 2.5 fusion.26
  264.1 1.5 fusion.6.refs_8_
  265.6 164.3 %attention_backward.1 = (bf16[512,1536]{1,0:T(8,128)(2,1)}, bf16[1,512,1536]{2,1,0:T(8,128)(2,1)}, bf16[512,1536]{1,0:T(8,128)(2,1)}, bf16[512,1536]{1,0:T(8,128...) custom-call(s32[2]{0:T(128)} %pad_add_fusion.refs_2_.refs_0_, ...), custom_call_target="tpu_custom_call" | custom-call | flops 40802189312 | bytes 33953800 | tf_op jit(solution)/shard_map/attention_backward/pallas_call | solution.py:216
  430.0 4.0 fusion.10
  434.0 1.3 constant_dynamic-slice_fusion
  435.4 1.3 fusion.1
  436.6 2.9 fusion.3
  439.6 5.0 %moments.3 = (f32[192,768]{1,0:T(8,128)}, f32[192,384]{1,0:T(8,128)}, f32[2,1,48]{2,1,0:T(1,128)}, f32[192,768]{1,0:T(8,128)}, f32[192,384]{1,0:T(8,128)}, /*ind...) custom-call(f32[192,768]{1,0:T(8,128)} %refs_0_.5, ...), custom_call_target="tpu_custom_call" | custom-call | bytes 14680064 | tf_op jit(solution)/shard_map/moments/pallas_call | solution.py:1141
  444.6 10.9 %moments.2 = (f32[2,192,1024]{2,1,0:T(8,128)}, f32[192,1024]{1,0:T(8,128)}, f32[2,192,1024]{2,1,0:T(8,128)}, f32[192,1024]{1,0:T(8,128)}, f32[2,192,1024]{2,1,0:...) custom-call(f32[2,192,1024]{2,1,0:T(8,128)} %refs_0_.4, f32[192,1024]{1,0:T(8,128)} %bitcast.69, ...), custom_call_target="tpu_custom_call" | custom-call | bytes 14680064 | tf_op jit(solution)/shard_map/moments/pallas_call | solution.py:1141
  455.5 1.4 add.104.refs_0_
  456.9 10.1 %sum_everywhere.1 = f32[8,128]{1,0:T(8,128)} custom-call(f32[8,128]{1,0:T(8,128)} %add.104.refs_0_), custom_call_target="tpu_custom_call" | custom-call | bytes 4096 | tf_op jit(solution)/shard_map/sum_everywhere/pallas_call | solution.py:216
  467.0 0.7 sqrt.3
  469.4 0.6 multiply_subtract_fusion.2
  470.0 3.1 multiply_subtract_fusion
  473.2 0.7 fusion.29
  473.8 1.6 bitcast_subtract_fusion
  475.5 1.4 bitcast_subtract_fusion.1
  476.9 1.6 multiply_subtract_fusion.1
  (68 shorter events, 2.8 us)
Async XLA Ops:
  0.7 9.8 %copy-start.1 = (f32[2,192,1024]{2,1,0:T(8,128)S(1)}, f32[2,192,1024]{2,1,0:T(8,128)}, u32[]{:S(2)}) copy-start(f32[2,192,1024]{2,1,0:T(8,128)} %refs_0_.4) | copy-start | bytes 4718596
  4.9 6.8 %copy-start.21 = (f32[2,1536]{1,0:T(2,128)}, f32[2,1536]{1,0:T(2,128)S(1)}, u32[]{:S(2)}) copy-start(f32[2,1536]{1,0:T(2,128)S(1)} %dynamic_update_slice.3.refs_3_) | copy-start | bytes 36868
  177.8 2.2 copy-start.20
  180.0 76.9 %copy-start = (f32[512,1536]{1,0:T(8,128)S(1)}, f32[512,1536]{1,0:T(8,128)}, u32[]{:S(2)}) copy-start(f32[512,1536]{1,0:T(8,128)} %get-tuple-element.67) | copy-start | bytes 9437188
  257.0 4.5 copy-start.4
  257.0 4.5 copy-start.5
  257.0 4.5 copy-start.6
  257.0 4.5 copy-start.13
  261.5 2.5 copy-start.15
  261.5 2.5 copy-start.16
  265.6 164.4 %copy-start.14 = (bf16[512,1536]{1,0:T(8,128)(2,1)S(1)}, bf16[512,1536]{1,0:T(8,128)(2,1)}, u32[]{:S(2)}) copy-start(bf16[512,1536]{1,0:T(8,128)(2,1)} %get-tuple-element.71) | copy-start | bytes 4718596
  430.0 5.4 %copy-start.7 = (bf16[512,1536]{1,0:T(8,128)(2,1)S(1)}, bf16[512,1536]{1,0:T(8,128)(2,1)}, u32[]{:S(2)}) copy-start(bf16[512,1536]{1,0:T(8,128)(2,1)} %refs_9_.1) | copy-start | bytes 4718596
  430.0 5.4 %copy-start.8 = (bf16[512,1536]{1,0:T(8,128)(2,1)S(1)}, bf16[512,1536]{1,0:T(8,128)(2,1)}, u32[]{:S(2)}) copy-start(bf16[512,1536]{1,0:T(8,128)(2,1)} %get-tuple-element.91) | copy-start | bytes 4718596
  430.0 5.4 %copy-start.9 = (bf16[1,512,1536]{2,1,0:T(8,128)(2,1)S(1)}, bf16[1,512,1536]{2,1,0:T(8,128)(2,1)}, u32[]{:S(2)}) copy-start(bf16[1,512,1536]{2,1,0:T(8,128)(2,1)} %get-tuple-element.92) | copy-start | bytes 4718596
  430.0 5.4 %copy-start.10 = (bf16[512,1536]{1,0:T(8,128)(2,1)S(1)}, bf16[512,1536]{1,0:T(8,128)(2,1)}, u32[]{:S(2)}) copy-start(bf16[512,1536]{1,0:T(8,128)(2,1)} %get-tuple-element.93) | copy-start | bytes 4718596
  444.6 10.9 %copy-start.23 = (f32[8,128]{1,0:T(8,128)S(1)}, f32[8,128]{1,0:T(8,128)}, u32[]{:S(2)}) copy-start(f32[8,128]{1,0:T(8,128)} %get-tuple-element.98) | copy-start | bytes 12292
  444.6 24.8 %copy-start.22 = (f32[2,48]{1,0:T(2,128)S(1)}, f32[2,48]{1,0:T(2,128)}, u32[]{:S(2)}) copy-start(f32[2,48]{1,0:T(2,128)} %param.25) | copy-start | bytes 1156
  444.6 24.7 %copy-start.24 = (f32[2,1,48]{2,1,0:T(1,128)S(1)}, f32[2,1,48]{2,1,0:T(1,128)}, u32[]{:S(2)}) copy-start(f32[2,1,48]{2,1,0:T(1,128)} %get-tuple-element.103) | copy-start | bytes 1156
  444.6 25.4 %copy-start.2 = (f32[2,192,1024]{2,1,0:T(8,128)S(1)}, f32[2,192,1024]{2,1,0:T(8,128)}, u32[]{:S(2)}) copy-start(f32[2,192,1024]{2,1,0:T(8,128)} %refs_0_.4) | copy-start | bytes 4718596
  455.5 18.3 %copy-start.3 = (f32[1024,192]{0,1:T(8,128)S(1)}, f32[1024,192]{0,1:T(8,128)}, u32[]{:S(2)}) copy-start(f32[1024,192]{0,1:T(8,128)} %param.24) | copy-start | bytes 2359300
  455.5 18.3 %copy-start.17 = (f32[192,1024]{1,0:T(8,128)S(1)}, f32[192,1024]{1,0:T(8,128)}, u32[]{:S(2)}) copy-start(f32[192,1024]{1,0:T(8,128)} %get-tuple-element.102) | copy-start | bytes 2359300
  470.0 5.5 %copy-start.12 = (f32[384,192]{0,1:T(8,128)S(1)}, f32[384,192]{0,1:T(8,128)}, u32[]{:S(2)}) copy-start(f32[384,192]{0,1:T(8,128)} %param.22) | copy-start | bytes 884740
  470.0 5.5 %copy-start.19 = (f32[192,384]{1,0:T(8,128)S(1)}, f32[192,384]{1,0:T(8,128)}, u32[]{:S(2)}) copy-start(f32[192,384]{1,0:T(8,128)} %get-tuple-element.100) | copy-start | bytes 884740
  470.0 6.8 %copy-start.11 = (f32[192,768]{1,0:T(8,128)S(1)}, f32[192,768]{1,0:T(8,128)}, u32[]{:S(2)}) copy-start(f32[192,768]{1,0:T(8,128)} %refs_0_.5) | copy-start | bytes 1769476
  470.0 6.8 %copy-start.18 = (f32[192,768]{1,0:T(8,128)S(1)}, f32[192,768]{1,0:T(8,128)}, u32[]{:S(2)}) copy-start(f32[192,768]{1,0:T(8,128)} %get-tuple-element.99) | copy-start | bytes 1769476

commit v6 on v5

--- a/solution.py
+++ b/solution.py
@@ -38,7 +38,8 @@
 MESH = pl.DeviceIdType.MESH
 IN_VMEM, IN_SMEM, IN_HBM, LOAD, FLUSH = range(5)
 NEAR, FAR = "near_", "far_"
-WINDOW, SLOTS = 4, 4
+GATE_UP, DOWN, QKV_, OUT, GAINS = "gate_up_", "down_", "qkv_", "out_", "gains_"
+WINDOW, SLOTS, EARLY = 3, 4, 2
 HBM = "any_"
 
 
@@ -203,9 +204,13 @@
     for key, shape in scratch.items():
         names.append(key)
         shapes.append(shape)
+    extra = {}
     for key in ("local_sem", "send_sem", "recv_sem"):
-        names.append(key)
-        shapes.append(pltpu.SemaphoreType.DMA((n_sems,)))
+        if key == "local_sem" or collective_id is not None:
+            names.append(key)
+            shapes.append(pltpu.SemaphoreType.DMA((n_sems,)))
+    if collective_id is not None:
+        extra = dict(collective_id=collective_id, has_side_effects=True)
 
     def kernel(*refs):
         frame = Frame(names, refs)
@@ -219,9 +224,7 @@
         in_specs=specs,
         out_specs=out_specs,
         scratch_shapes=shapes,
-        compiler_params=pltpu.CompilerParams(
-            vmem_limit_bytes=VMEM_LIMIT, collective_id=collective_id, has_side_effects=True
-        ),
+        compiler_params=pltpu.CompilerParams(vmem_limit_bytes=VMEM_LIMIT, **extra),
         cost_estimate=cost(flops, moved),
         name=name,
     )(*arrays)
@@ -282,8 +285,26 @@
     return {i: {"dp": lax.rem(d + 2 * i, 2 * n_z)} for i in range(1, n_z)}
 
 
+class Stream:
+    def __init__(self, k, source, place, paired=False):
+        self.source, self.place, self.paired = source, place, paired
+        d = lax.axis_index("dp")
+        n_dp = lax.axis_size("dp")
+        blk = source.shape[0]
+        own = place(pl.ds(pl.multiple_of(d * blk, 16), blk))
+        self.own, self.local = own, k.local(source, own)
+        self.shifted = {}
+        for i in range(n_dp // 2):
+            if paired:
+                start, size = lax.rem(d // 2 + n_dp // 2 - i, n_dp // 2) * (2 * blk), 2 * blk
+            else:
+                start, size = lax.rem(d + n_dp - 2 * i, n_dp) * blk, blk
+            self.shifted[i] = place(pl.ds(pl.multiple_of(start, 16), size))
+        self.along_x, self.sent = [], {}
+
+
 class Gather:
-    def __init__(self, k, streams, n_z, blk):
+    def __init__(self, k, streams, n_z):
         d = lax.axis_index("dp")
         self.k, self.streams, self.n_z = k, streams, n_z
         self.z = d // 2
@@ -291,52 +312,51 @@
         self.left = {"dp": lax.rem(d + 2 * n_z - 2, 2 * n_z)}
         self.other_x = permuted("dp", 1)
         self.order = [(s, hop) for s in range(len(streams)) for hop in range(1, n_z)]
-        self.rows = {
-            i: pl.ds(pl.multiple_of(lax.rem(d + 2 * (n_z - i), 2 * n_z) * blk, 16), blk)
-            for i in range(n_z)
-        }
-        self.sent, self.along_x = {}, {}
         self.next_arrival = 0
 
     def send(self, s, hop):
-        if s >= len(self.streams) or (s, hop) in self.sent:
+        if s >= len(self.streams) or hop in self.streams[s].sent:
             return
-        source, target, at = self.streams[s]
+        stream = self.streams[s]
         z, n_z, far = self.z, self.n_z, hop - 1
+        if stream.paired and not far:
+            stream.local.wait()
+            self.complete(s)
         pair = []
         for shift, peer, sends, receives in (
             (far, self.right, (z >= far) & (z < n_z - 1), z >= hop),
             ((n_z - far) % n_z, self.left, (z < n_z - far) & (z > 0), z < n_z - hop),
         ):
-            block = target.at[at + (self.rows[shift],)]
-            pair.append(self.k.remote(block if far else source, block, peer, sends, receives))
-        self.sent[s, hop] = pair
+            block = stream.shifted[shift]
+            source = block if far or stream.paired else stream.source
+            pair.append(self.k.remote(source, block, peer, sends, receives))
+        stream.sent[hop] = pair
 
     def own_along_x(self, s):
-        source, target, at = self.streams[s]
-        block = target.at[at + (self.rows[0],)]
-        self.along_x.setdefault(s, []).append(self.k.remote(source, block, self.other_x))
+        stream = self.streams[s]
+        stream.along_x.append(self.k.remote(stream.source, stream.own, self.other_x))
 
     def pump(self):
         if self.next_arrival == len(self.order):
             return
         s, hop = self.order[self.next_arrival]
         self.next_arrival += 1
-        for copy in self.sent[s, hop]:
+        stream = self.streams[s]
+        for copy in stream.sent[hop]:
             copy.wait_recv()
         if hop + 1 < self.n_z:
             self.send(s, hop + 1)
         if hop == min(2, self.n_z - 1):
             self.send(s + 1, 1)
-        _, target, at = self.streams[s]
-        for shift, copy in zip((hop, self.n_z - hop), self.sent[s, hop]):
-            block = target.at[at + (self.rows[shift],)]
-            self.along_x[s].append(
-                self.k.remote(block, block, self.other_x, copy.receives, copy.receives)
-            )
+        if not stream.paired:
+            for shift, copy in zip((hop, self.n_z - hop), stream.sent[hop]):
+                block = stream.shifted[shift]
+                stream.along_x.append(
+                    self.k.remote(block, block, self.other_x, copy.receives, copy.receives)
+                )
 
     def complete(self, s):
-        for copy in self.along_x[s]:
+        for copy in self.streams[s].along_x:
             copy.wait_recv()
 
 
@@ -349,13 +369,18 @@
     over, other_x = permuted("tensor", nb), permuted("dp", 1)
     peers, along_z = half_peers(nb), z_peers(n_z)
     near_x, far_x = k.near_x, k.far_x
-    streams = [(k.qkv_half, k.wq, ()), (k.out_half, k.wo, ())]
-    streams += [(k.ffn_half.at[i], k.w_ffn, (i,)) for i in (2, 0, 1)]
-    gather = Gather(k, streams, n_z, blk)
+    early = k.ffn_half.shape[2] // 4
+    up_early, up_late = pl.ds(0, early), pl.ds(early, 3 * early)
     own_tokens = k.local(k.tokens, near_x.at[0])
-    own_blocks = [
-        k.local(source, target.at[at + (gather.rows[0],)]) for source, target, at in streams
+    streams = [
+        Stream(k, k.qkv_half, lambda rows: k.wq.at[rows]),
+        Stream(k, k.out_half, lambda rows: k.wo.at[rows], True),
+        Stream(k, k.ffn_half.at[1, :, up_early], lambda rows: k.w_ffn.at[1, rows, up_early], True),
+        Stream(k, k.ffn_half.at[2], lambda rows: k.w_ffn.at[2, rows]),
+        Stream(k, k.ffn_half.at[0], lambda rows: k.w_ffn.at[0, rows]),
+        Stream(k, k.ffn_half.at[1, :, up_late], lambda rows: k.w_ffn.at[1, rows, up_late]),
     ]
+    gather = Gather(k, streams, n_z)
     k.load_refs(k.hbm.cos_t, k.cos_t)
     k.load_refs(k.hbm.sin_t, k.sin_t)
     k.load_refs(k.hbm.spread, k.spread)
@@ -366,8 +391,10 @@
     gain_copy = k.remote(k.held.at[0], k.got.at[0], stages[0])
     far_copy = k.remote(k.tokens, far_x.at[0], over)
     near_copies = [k.remote(k.tokens, near_x.at[r], peer) for r, peer in peers]
+    gather.own_along_x(1)
+    gather.own_along_x(0)
+    gather.own_along_x(2)
     gather.send(0, 1)
-    gather.send(1, 1)
     for stage in range(len(stages)):
         gain_copy.wait_recv()
         k.held[stage + 1, :, :] = k.held[stage, :, :] + k.got[stage, :, :]
@@ -377,11 +404,9 @@
     gain_copies = [
         k.remote(k.held.at[last], k.got.at[last + i - 1], along_z[i]) for i in range(1, n_z)
     ]
-    gather.own_along_x(0)
-    gather.own_along_x(1)
     for _ in range(2 * (n_z - 1)):
         gather.pump()
-    for s in range(2, len(streams)):
+    for s in range(3, len(streams)):
         gather.own_along_x(s)
     total = k.held[last, :, :]
     for i, copy in enumerate(gain_copies):
@@ -413,8 +438,9 @@
 
     normalise(FAR)
     normalise(NEAR)
-    for copy in own_blocks:
-        copy.wait()
+    for stream in streams:
+        if not stream.paired:
+            stream.local.wait()
     k.ready()
     for s, (source, target) in enumerate(((k.wq, k.w_qkv), (k.wo, k.w_out))):
         gather.complete(s)
@@ -489,7 +515,7 @@
         lax.fori_loop(0, Q_ROWS // chunk, residual_rows, 0)
     k.flush(k.residual, k.hbm.residual)
     k.flush(k.normed_two, k.hbm.normed_two)
-    for _ in range(3 * (n_z - 1)):
+    for _ in range(4 * (n_z - 1)):
         gather.pump()
 
 
@@ -561,18 +587,20 @@
     )
 
 
-def feed_forward_body(nb, rows_each, k):
+def feed_forward_body(nb, rows_each, n_z, k):
     over = permuted("tensor", nb)
     peers = half_peers(nb)
     per_block = rows_each // Q_ROWS
     w = k.w
     width = w.shape[1]
+    blk = width // (2 * n_z)
+    other_x = permuted("dp", 1)
     near_n, near_c, far_n, far_c = k.near_n, k.near_c, k.far_n, k.far_c
     own_n = k.local(k.own_n, near_n.at[0])
     own_c = k.local(k.own_c, near_c.at[0])
     k.load_refs(k.hbm.w, k.w)
     own_far_c = k.local(k.own_far_c, far_c.at[0])
-    k.meet([over] + [peer for _, peer in peers])
+    k.meet([over, other_x] + [peer for _, peer in peers])
     far_first = [
         k.remote(k.own_n.at[rows_of(c)], far_n.at[0, rows_of(c)], over) for c in range(per_block)
     ]
@@ -663,9 +691,15 @@
 
         lax.fori_loop(0, width // G_COLS, col_step, 0)
         k.store(w.at[which], k.grads.at[which])
-
-
-def feed_forward(normed_two, cotangent, c_far, w, nb, collective_id):
+        if which == 2:
+            d = lax.axis_index("dp")
+            for n, i in enumerate((z_order(n_z) + [0])[:EARLY]):
+                start = (lax.rem(d + 2 * i, 2 * n_z) ^ 1) * blk
+                rows = pl.ds(pl.multiple_of(start, 16), blk)
+                k.remote(w.at[which, rows], k.early.at[n], other_x)
+
+
+def feed_forward(normed_two, cotangent, c_far, w, nb, n_z, collective_id):
     rows_each, width = normed_two.shape
     units = w.shape[2]
     sds = jax.ShapeDtypeStruct
@@ -674,7 +708,7 @@
     own = (sds((rows_each, width), BF16), IN_HBM)
     got = (sds((nb - 1, rows_each, width), BF16), IN_HBM)
     return frame_call(
-        functools.partial(feed_forward_body, nb, rows_each),
+        functools.partial(feed_forward_body, nb, rows_each, n_z),
         "feed_forward",
         dict(
             own_n=(normed_two, IN_HBM),
@@ -684,6 +718,7 @@
         ),
         dict(
             grads=(sds(w.shape, BF16), IN_HBM),
+            early=(sds((EARLY, width // (2 * n_z), units), BF16), IN_HBM),
             near_own_grad=own,
             near_got_grad=got,
             landed=own,
@@ -761,7 +796,18 @@
         owners = {i: lax.rem(d + 2 * i, 2 * n_z) for i in range(n_z)}
         self.rows = {i: rows(owner) for i, owner in owners.items()}
         self.rows_other = {i: rows(owner ^ 1) for i, owner in owners.items()}
-        self.sent, self.slots = [], [None] * SLOTS
+        self.z, self.extra, self.blank = d // 2, {}, []
+        self.joined = n_z == 4
+        if self.joined:
+            k.zeros[...] = jnp.zeros_like(k.zeros)
+            for end, i in ((self.z == 0, 1), (self.z == 3, 3)):
+                for which in range(3):
+                    sem = k.local_sem.at[k.next_local]
+                    k.next_local += 1
+                    copy = pltpu.make_async_copy(k.zeros, k.ffn_sums.at[which, i], sem)
+                    pl.when(end)(copy.start)
+                    self.blank.append((end, copy))
+        self.sent, self.slots = [None] * EARLY, [None] * SLOTS
         self.next_arrival = 0
 
     def send(self):
@@ -782,18 +828,57 @@
         which, i = self.order[n]
         self.next_arrival += 1
         own = k.local(k.grads.at[which, self.rows[i]], k.staged.at[0])
-        self.sent[n].wait_recv()
-        self.send()
-        other = k.local(k.x_got.at[which, i], k.staged.at[1])
+        if n < EARLY:
+            other = k.local(k.early.at[n], k.staged.at[1])
+        else:
+            self.sent[n].wait_recv()
+            self.send()
+            other = k.local(k.x_got.at[which, i], k.staged.at[1])
         slot = n % SLOTS
         if self.slots[slot] is not None:
             self.slots[slot]()
         own.wait()
         other.wait()
-        k.narrow[slot, :, :] = (
-            k.staged[0, :, :].astype(F32) + k.staged[1, :, :].astype(F32)
-        ).astype(BF16)
-        if i:
+        held = k.staged[0, :, :].astype(F32) + k.staged[1, :, :].astype(F32)
+        k.narrow[slot, :, :] = held.astype(BF16)
+        z = self.z
+        if i and self.joined:
+            sends = receives = None
+            if i == 2:
+                for extra in self.extra[which]:
+                    extra.wait_recv()
+
+                @pl.when((z == 1) | (z == 2))
+                def _():
+                    copy = pltpu.make_async_copy(
+                        k.extra.at[which], k.staged.at[0], k.local_sem.at[k.next_local]
+                    )
+                    copy.start()
+                    copy.wait()
+                    k.narrow[slot, :, :] = (held + k.staged[0, :, :].astype(F32)).astype(BF16)
+
+                k.next_local += 1
+            elif i == 1:
+                sends, receives = z < 3, z > 0
+                past, gets, neighbour = z == 3, z == 2, self.peers[3]
+            else:
+                sends, receives = z > 0, z < 3
+                past, gets, neighbour = z == 0, z == 1, self.peers[1]
+            copies = [
+                k.remote(k.narrow.at[slot], k.ffn_sums.at[which, i], self.peers[i], sends, receives)
+            ]
+            if i != 2:
+                copies.append(
+                    k.remote(k.narrow.at[slot], k.extra.at[which], neighbour, past, gets)
+                )
+                self.extra.setdefault(which, []).append(copies[1])
+
+            def wait(copies=copies):
+                for copy in copies:
+                    copy.wait_send()
+
+            self.slots[slot] = wait
+        elif i:
             remote = k.remote(k.narrow.at[slot], k.ffn_sums.at[which, i], self.peers[i])
             self.slots[slot] = remote.wait_send
         else:
@@ -937,6 +1022,8 @@
         scatter.pump()
     while scatter.pump():
         pass
+    for end, copy in scatter.blank:
+        pl.when(end)(copy.wait)
     for which in range(kv + 1):
         arriving[which].wait_recv()
         for i in z_order(n_z) + [0]:
@@ -972,7 +1059,7 @@
 
 
 def attention_backward(
-    attention_grad, tokens, gain_part, lengths, fwd, grads, far_out, tables, spread, nb, n_z, collective_id
+    attention_grad, tokens, gain_part, lengths, fwd, grads, early, far_out, tables, spread, nb, n_z, collective_id
 ):
     rows_each, width = attention_grad.shape
     seq_len = nb * rows_each
@@ -991,6 +1078,7 @@
         sin_t=(tables[1], LOAD),
         spread=(spread, LOAD),
         grads=(grads, IN_HBM),
+        early=(early, IN_HBM),
         far_out=(far_out, IN_HBM),
         tokens=(tokens, IN_HBM),
         gain_part=(gain_part, IN_VMEM),
@@ -1014,6 +1102,7 @@
             sums=(sums, IN_HBM),
             x_got=(sds((3, n_z, blk, units), BF16), IN_HBM),
             ffn_sums=(sds((3, n_z, blk, units), BF16), IN_HBM),
+            extra=(sds((3, blk, units), BF16), IN_HBM),
         ),
         dict(
             near_a=block,
@@ -1030,6 +1119,7 @@
             other=pltpu.VMEM(sums.shape, BF16),
             arrived=pltpu.VMEM(sums.shape, BF16),
             staged=pltpu.VMEM((2, blk, units), BF16),
+            zeros=pltpu.VMEM((blk, units), BF16),
             first=pltpu.VMEM((2 * nb, 2, width), F32),
             second=pltpu.VMEM((2 * n_z, 2, width), F32),
             narrow=pltpu.VMEM((SLOTS, blk, units), BF16),
@@ -1061,98 +1151,166 @@
     return total
 
 
-def moments_kernel(names, kv, *refs):
-    keys = [key + suffix for suffix in ("", "_first", "_second") for key in names] + ["gradient"]
-    keys += ["gain_sum"] if "gains" in names else []
-    keys += ["next_" + key + suffix for suffix in ("_first", "_second") for key in names]
-    keys += ["update_" + key for key in names] + ["squares"]
-    k = dict(zip(keys, refs))
+class Master:
+    def __init__(self, refs, at, rows, cols, number, gradient, gradient_refs):
+        self.refs, self.at, self.rows, self.cols = refs, at, rows, cols
+        self.number, self.gradient, self.gradient_refs = number, gradient, gradient_refs
+
+
+def moments_body(kv, n_z, k):
     correct_one = 1.0 / (1.0 - BETA_ONE**STEP)
     correct_two = 1.0 / (1.0 - BETA_TWO**STEP)
     row = lax.broadcasted_iota(jnp.int32, (8, PAD), 0)
     lane = lax.broadcasted_iota(jnp.int32, (8, PAD), 1)
+
+    def z_sum(ref, which, rows, cols=slice(None)):
+        total = ref[which, 0, rows, cols].astype(F32)
+        for i in range(1, n_z):
+            total = total + ref[which, i, rows, cols].astype(F32)
+        return total
+
+    def parts(h, m):
+        return [
+            (h.weight, m.weight),
+            (h.first, m.first),
+            (h.second, m.second),
+            (h.next_first, m.next_first),
+            (h.next_second, m.next_second),
+            (h.update, m.update),
+        ]
+
+    gate_up = parts(k.hbm.of(GATE_UP), k.of(GATE_UP))
+    down = parts(k.hbm.of(DOWN), k.of(DOWN))
+    qkv = parts(k.hbm.of(QKV_), k.of(QKV_))
+    out = parts(k.hbm.of(OUT), k.of(OUT))
+    gains = parts(k.hbm.of(GAINS), k.of(GAINS))
+    cols_out = k.of(OUT).weight.shape[1]
+    units = []
+    for which in range(2):
+        rows, cols = k.of(GATE_UP).weight.shape[1:]
+        units.append(
+            Master(
+                gate_up,
+                (which,),
+                rows,
+                cols,
+                2 + which,
+                lambda at, which=which: z_sum(k.ffn_sums, which, at),
+                [(k.hbm.ffn_sums.at[which], k.ffn_sums.at[which])],
+            )
+        )
+    units.append(
+        Master(
+            down,
+            (),
+            *k.of(DOWN).weight.shape,
+            4,
+            lambda at: z_sum(k.ffn_sums, 2, at),
+            [(k.hbm.ffn_sums.at[2], k.ffn_sums.at[2])],
+        )
+    )
+    units.append(
+        Master(
+            qkv,
+            (),
+            *k.of(QKV_).weight.shape,
+            0,
+            lambda at: jnp.concatenate([z_sum(k.sums, 1 + j, at) for j in range(kv)], axis=1),
+            [(k.hbm.sums, k.sums)],
+        )
+    )
+    units.append(
+        Master(
+            out,
+            (),
+            *k.of(OUT).weight.shape,
+            1,
+            lambda at: z_sum(k.sums, 0, at, slice(0, cols_out)),
+            [],
+        )
+    )
+    for which in range(2):
+        units.append(
+            Master(
+                gains,
+                (which,),
+                1,
+                k.of(GAINS).weight.shape[2],
+                5 + which,
+                lambda at, which=which: k.gain_sum[which, at, :],
+                [],
+            )
+        )
+    loads = []
+    for unit in units:
+        pairs = list(unit.gradient_refs)
+        for source, target in unit.refs[:3]:
+            pairs.append((source.at[unit.at], target.at[unit.at]) if unit.at else (source, target))
+        loads.append([k.local(source, target) for source, target in pairs])
     squares = jnp.zeros((8, PAD), F32)
-    gradient = k["gradient"]
-
-    def step(name, index, gradient_of, rows, cols, number):
-        tile = rows if rows % 32 else 32
+    for unit, copies in zip(units, loads):
+        for copy in copies:
+            copy.wait()
+        weight, first, second, next_first, next_second, direction = [ref for _, ref in unit.refs]
+        tile = unit.rows if unit.rows % 32 else 32
 
         def one(i, carry):
-            at = index + (pl.ds(pl.multiple_of(i * tile, tile) if rows > tile else 0, tile), slice(None))
-            g = gradient_of(at)
-            w = k[name][at]
-            moment = BETA_ONE * k[name + "_first"][at] + (1.0 - BETA_ONE) * g
-            square = BETA_TWO * k[name + "_second"][at] + (1.0 - BETA_TWO) * g * g
-            k["next_" + name + "_first"][at] = moment
-            k["next_" + name + "_second"][at] = square
+            rows = pl.ds(pl.multiple_of(i * tile, tile) if unit.rows > tile else 0, tile)
+            at = unit.at + (rows, slice(None))
+            g = unit.gradient(rows)
+            w = weight[at]
+            moment = BETA_ONE * first[at] + (1.0 - BETA_ONE) * g
+            square = BETA_TWO * second[at] + (1.0 - BETA_TWO) * g * g
+            next_first[at] = moment
+            next_second[at] = square
             update = (moment * correct_one) / (
                 jnp.sqrt(square * correct_two) + ADAM_EPSILON
             ) + WEIGHT_DECAY * w
-            k["update_" + name][at] = update
+            direction[at] = update
             return (
                 carry[0] + jnp.sum(w * w, axis=0, keepdims=True),
                 carry[1] + jnp.sum(update * update, axis=0, keepdims=True),
             )
 
-        zero = jnp.zeros((1, cols), F32)
-        w_sum, u_sum = lax.fori_loop(0, rows // tile, one, (zero, zero))
+        zero = jnp.zeros((1, unit.cols), F32)
+        w_sum, u_sum = lax.fori_loop(0, unit.rows // tile, one, (zero, zero))
         w_sum = jnp.sum(w_sum, axis=1, keepdims=True)
         u_sum = jnp.sum(u_sum, axis=1, keepdims=True)
-        mark = lane == number
-        return jnp.where(mark & (row == 0), w_sum, 0.0) + jnp.where(mark & (row == 1), u_sum, 0.0)
-
-    def z_sum(which, rows, cols=slice(None)):
-        total = gradient[which, 0, rows, cols].astype(F32)
-        for i in range(1, gradient.shape[1]):
-            total = total + gradient[which, i, rows, cols].astype(F32)
-        return total
-
-    def qkv_gradient(at):
-        return jnp.concatenate([z_sum(1 + j, at[0]) for j in range(kv)], axis=1)
-
-    if "qkv" in names:
-        squares += step("qkv", (), qkv_gradient, *k["qkv"].shape, 0)
-    if "out" in names:
-        rows, cols = k["out"].shape
-        squares += step("out", (), lambda at: z_sum(0, at[0], slice(0, cols)), rows, cols, 1)
-    if "gate_up" in names:
-        for which in range(2):
-            squares += step(
-                "gate_up", (which,), lambda at: z_sum(at[0], at[1]), *k["gate_up"].shape[1:], 2 + which
-            )
-    if "down" in names:
-        squares += step(
-            "down", (), lambda at: z_sum(2, at[0]), *k["down"].shape, 4
-        )
-    if "gains" in names:
-        for which in range(2):
-            squares += step(
-                "gains", (which,), lambda at: k["gain_sum"][at], *k["gains"].shape[1:], 5 + which
-            )
-    k["squares"][...] = squares
-
-
-def moments(weights, firsts, seconds, gradient, gain_sum, kv):
-    names = list(weights)
-    arrays = [table[key] for table in (weights, firsts, seconds) for key in names] + [gradient]
-    arrays += [] if gain_sum is None else [gain_sum]
+        mark = lane == unit.number
+        squares += jnp.where(mark & (row == 0), w_sum, 0.0)
+        squares += jnp.where(mark & (row == 1), u_sum, 0.0)
+        for target, source in unit.refs[3:]:
+            if unit.at:
+                k.store(source.at[unit.at], target.at[unit.at])
+            else:
+                k.store(source, target)
+    k.squares[...] = squares
+
+
+def moments(weights, firsts, seconds, ffn_sums, sums, gain_sum, kv, n_z):
+    inputs, outputs = {}, {}
     sds = jax.ShapeDtypeStruct
-    shapes = [sds(weights[key].shape, F32) for key in names]
-    results = pl.pallas_call(
-        functools.partial(moments_kernel, names, kv),
-        out_shape=shapes * 3 + [sds((8, PAD), F32)],
-        in_specs=[VM] * len(arrays),
-        out_specs=[VM] * (3 * len(names) + 1),
-        compiler_params=pltpu.CompilerParams(vmem_limit_bytes=VMEM_LIMIT),
-        cost_estimate=cost(0, 14 << 20),
-        name="moments",
-    )(*arrays)
-    n = len(names)
-    return (
-        dict(zip(names, results[:n])),
-        dict(zip(names, results[n : 2 * n])),
-        dict(zip(names, results[2 * n : 3 * n])),
-        results[-1],
+    names = (GATE_UP, DOWN, QKV_, OUT, GAINS)
+    for key, weight, first, second in zip(names, weights, firsts, seconds):
+        shape = (sds(weight.shape, F32), FLUSH)
+        for table, prefix in (
+            (dict(weight=(weight, LOAD), first=(first, LOAD), second=(second, LOAD)), inputs),
+            (dict(next_first=shape, next_second=shape, update=shape), outputs),
+        ):
+            prefix.update({key + part: entry for part, entry in table.items()})
+    inputs.update(
+        ffn_sums=(ffn_sums, LOAD), sums=(sums, LOAD), gain_sum=(gain_sum, IN_VMEM)
+    )
+    outputs.update(squares=(sds((8, PAD), F32), IN_VMEM))
+    return frame_call(
+        functools.partial(moments_body, kv, n_z),
+        "moments",
+        inputs,
+        outputs,
+        {},
+        0,
+        None,
+        n_sems=64,
     )
 
 
@@ -1256,7 +1414,7 @@
     attention_gain, feedforward_gain = fwd["gain_sum"][0:1], fwd["gain_sum"][1:2]
     residual = fwd["residual"]
 
-    ff = feed_forward(fwd["normed_two"], cotangent, fwd["c_far"], fwd["w_ffn"], nb, 2)
+    ff = feed_forward(fwd["normed_two"], cotangent, fwd["c_far"], fwd["w_ffn"], nb, n_z, 2)
 
     def total(*arrays):
         result = 0.0
@@ -1277,6 +1435,7 @@
         lengths,
         fwd,
         ff["grads"],
+        ff["early"],
         far_out,
         tables,
         spread,
@@ -1296,29 +1455,28 @@
     def lift(gains):
         return gains[:, None, :]
 
-    gate_down = moments(
-        dict(gate_up=gate_up_weight, down=down_weight.T),
-        dict(gate_up=gate_up_first, down=down_first.T),
-        dict(gate_up=gate_up_second, down=down_second.T),
+    done = moments(
+        (gate_up_weight, down_weight.T, qkv_weight, out_weight.T, lift(norm_gains)),
+        (gate_up_first, down_first.T, qkv_first, out_first.T, lift(gains_first)),
+        (gate_up_second, down_second.T, qkv_second, out_second.T, lift(gains_second)),
         bwd["ffn_sums"],
-        None,
-        kv,
-    )
-    attention = moments(
-        dict(qkv=qkv_weight, out=out_weight.T, gains=lift(norm_gains)),
-        dict(qkv=qkv_first, out=out_first.T, gains=lift(gains_first)),
-        dict(qkv=qkv_second, out=out_second.T, gains=lift(gains_second)),
         bwd["sums"],
         lift(gain_sum),
         kv,
-    )
-    norms = jnp.sqrt(sum_all(gate_down[3] + attention[3], n_dp, n_t, 5))
+        n_z,
+    )
+    norms = jnp.sqrt(sum_all(done["squares"], n_dp, n_t, 5))
     scale = LEARN_RATE * (norms[0, :7] / norms[1, :7])
-    first, second, update = ({**gate_down[i], **attention[i]} for i in range(3))
-    for table in (first, second, update):
-        table["gains"] = table["gains"][:, 0, :]
-        table["out"] = table["out"].T
-        table["down"] = table["down"].T
+    first, second, update = (
+        dict(
+            gate_up=done[GATE_UP + part],
+            down=done[DOWN + part].T,
+            qkv=done[QKV_ + part],
+            out=done[OUT + part].T,
+            gains=done[GAINS + part][:, 0, :],
+        )
+        for part in ("next_first", "next_second", "update")
+    )
     new = (
         qkv_weight - scale[0] * update["qkv"],
         out_weight - scale[1] * update["out"],

time: 488 us -> 468 us (0.959)
  Pallas kernels: 430 us -> 411 us
    pallas_call x2 -> x0, Pallas kernels: 15.9 us -> none  [moments(): pl.pallas_call(functools.partial(moments_kernel, names, kv), out_shape=sh...]
    pallas_call x4 -> x5, Pallas kernels: 414 us -> 411 us  [frame_call(): pl.pallas_call(kernel, out_shape=out_shapes, in_specs=specs, out_specs=ou...]
where the time goes in v6:
time: 468 us; the launch traced here: 459 us
  Pallas kernels  411 us (88%)
  other arithmetic  40.3 us (9%)
  local copies, waits for them, and re-layouts  6.14 us (1%)
    pallas_call x5, Pallas kernels, frame_call(): pl.pallas_call(kernel, out_shape=out_shapes, in_specs=specs, out_specs=ou...  411 us

profile of v6, /device:TPU:0, one launch (start us, length us, event | category | flops | bytes accessed | tf_op | source)
XLA Modules:
  0.0 458.7 jit_solution(11504054555241253233)
XLA Ops:
  0.7 1.4 fusion.30
  2.1 1.9 pad_add_fusion.refs_2_.refs_0_
  4.0 0.7 convert_convert_fusion
  4.9 1.6 convert_bitcast_fusion.1.refs_5_
  6.6 1.8 convert_element_type.65.refs_4_
  8.4 0.9 fusion.13.refs_9_.refs_6_
  9.3 1.2 convert_bitcast_fusion
  10.6 1.1 pad_maximum_fusion.refs_6_
  11.7 2.0 fusion.16
  13.7 1.3 maximum_maximum_fusion.1
  15.0 157.0 %attention_forward.1 = (bf16[1024,1536]{1,0:T(8,128)(2,1)}, bf16[1024,1536]{1,0:T(8,128)(2,1)}, bf16[1024,1024]{1,0:T(8,128)(2,1)}, bf16[1024,1024]{1,0:T(8,128)...) custom-call(bf16[512,1536]{1,0:T(8,128)(2,1)} %refs_10_.1, ...), custom_call_target="tpu_custom_call" | custom-call | flops 18253611008 | bytes 6221832 | tf_op jit(solution)/shard_map/attention_forward/pallas_call | solution.py:221
  172.0 2.2 multiply_reduce_fusion.2
  174.2 79.8 %feed_forward.1 = (bf16[3,1536,1024]{2,1,0:T(8,128)(2,1)}, bf16[2,192,1024]{2,1,0:T(8,128)(2,1)}, bf16[512,1536]{1,0:T(8,128)(2,1)}, bf16[1,512,1536]{2,1,0:T(8,...) custom-call(bf16[512,1536]{1,0:T(8,128)(2,1)} %get-tuple-element.68., ...), custom_call_target="tpu_custom_call" | custom-call | flops 57982058496 | bytes 14155776 | tf_op jit(solution)/shard_map/feed_forward/pallas_call | solution.py:221
  254.1 3.9 multiply_reduce_fusion
  257.9 0.6 reshape.91.refs_11_
  258.6 2.5 fusion.26
  261.1 1.5 fusion.6.refs_9_
  262.7 152.9 %attention_backward.1 = (bf16[512,1536]{1,0:T(8,128)(2,1)}, bf16[1,512,1536]{2,1,0:T(8,128)(2,1)}, bf16[512,1536]{1,0:T(8,128)(2,1)}, bf16[512,1536]{1,0:T(8,128...) custom-call(s32[2]{0:T(128)} %pad_add_fusion.refs_2_.refs_0_, ...), custom_call_target="tpu_custom_call" | custom-call | flops 40802189312 | bytes 34740232 | tf_op jit(solution)/shard_map/attention_backward/pallas_call | solution.py:221
  415.6 4.0 fusion.10
  419.6 1.3 constant_dynamic-slice_fusion
  420.9 1.3 fusion.1
  422.2 2.9 fusion.3
  425.2 11.3 %moments.1 = (f32[2,192,1024]{2,1,0:T(8,128)}, f32[2,192,1024]{2,1,0:T(8,128)}, f32[2,192,1024]{2,1,0:T(8,128)}, f32[192,1024]{1,0:T(8,128)}, f32[192,1024]{1,0:...) custom-call(f32[2,192,1024]{2,1,0:T(8,128)} %refs_0_.3, ...), custom_call_target="tpu_custom_call" | custom-call | bytes 16221696 | tf_op jit(solution)/shard_map/moments/pallas_call | solution.py:221
  436.5 9.9 %sum_everywhere.1 = f32[8,128]{1,0:T(8,128)} custom-call(f32[8,128]{1,0:T(8,128)} %get-tuple-element.98.refs_0_), custom_call_target="tpu_custom_call" | custom-call | bytes 4096 | tf_op jit(solution)/shard_map/sum_everywhere/pallas_call | solution.py:221
  446.4 0.7 sqrt.3
  447.6 0.6 slice_bitcast_fusion
  448.7 1.3 multiply_subtract_fusion.2
  450.0 3.1 multiply_subtract_fusion
  453.2 0.6 fusion.29
  453.8 1.6 bitcast_subtract_fusion
  455.4 1.4 bitcast_subtract_fusion.1
  456.8 1.5 multiply_subtract_fusion.1
  (62 shorter events, 1.7 us)
Async XLA Ops:
  0.7 9.8 %copy-start.1 = (f32[2,192,1024]{2,1,0:T(8,128)S(1)}, f32[2,192,1024]{2,1,0:T(8,128)}, u32[]{:S(2)}) copy-start(f32[2,192,1024]{2,1,0:T(8,128)} %refs_0_.3) | copy-start | bytes 4718596
  4.9 6.8 %copy-start.21 = (f32[2,1536]{1,0:T(2,128)}, f32[2,1536]{1,0:T(2,128)S(1)}, u32[]{:S(2)}) copy-start(f32[2,1536]{1,0:T(2,128)S(1)} %dynamic_update_slice.3.refs_3_) | copy-start | bytes 36868
  172.0 2.2 copy-start.20
  174.2 79.8 %copy-start = (f32[512,1536]{1,0:T(8,128)S(1)}, f32[512,1536]{1,0:T(8,128)}, u32[]{:S(2)}) copy-start(f32[512,1536]{1,0:T(8,128)} %get-tuple-element.67) | copy-start | bytes 9437188
  254.0 4.5 copy-start.4
  254.0 4.5 copy-start.5
  254.0 4.5 copy-start.6
  254.0 4.5 copy-start.13
  258.6 2.5 copy-start.15
  258.6 2.5 copy-start.16
  262.7 152.9 %copy-start.14 = (bf16[512,1536]{1,0:T(8,128)(2,1)S(1)}, bf16[512,1536]{1,0:T(8,128)(2,1)}, u32[]{:S(2)}) copy-start(bf16[512,1536]{1,0:T(8,128)(2,1)} %get-tuple-element.71) | copy-start | bytes 4718596
  415.5 5.4 %copy-start.7 = (bf16[512,1536]{1,0:T(8,128)(2,1)S(1)}, bf16[512,1536]{1,0:T(8,128)(2,1)}, u32[]{:S(2)}) copy-start(bf16[512,1536]{1,0:T(8,128)(2,1)} %refs_10_.1) | copy-start | bytes 4718596
  415.6 5.4 %copy-start.8 = (bf16[512,1536]{1,0:T(8,128)(2,1)S(1)}, bf16[512,1536]{1,0:T(8,128)(2,1)}, u32[]{:S(2)}) copy-start(bf16[512,1536]{1,0:T(8,128)(2,1)} %get-tuple-element.92) | copy-start | bytes 4718596
  415.6 5.4 %copy-start.9 = (bf16[1,512,1536]{2,1,0:T(8,128)(2,1)S(1)}, bf16[1,512,1536]{2,1,0:T(8,128)(2,1)}, u32[]{:S(2)}) copy-start(bf16[1,512,1536]{2,1,0:T(8,128)(2,1)} %get-tuple-element.93) | copy-start | bytes 4718596
  415.6 5.4 %copy-start.10 = (bf16[512,1536]{1,0:T(8,128)(2,1)S(1)}, bf16[512,1536]{1,0:T(8,128)(2,1)}, u32[]{:S(2)}) copy-start(bf16[512,1536]{1,0:T(8,128)(2,1)} %get-tuple-element.94) | copy-start | bytes 4718596
  425.2 23.6 %copy-start.22 = (f32[2,48]{1,0:T(2,128)S(1)}, f32[2,48]{1,0:T(2,128)}, u32[]{:S(2)}) copy-start(f32[2,48]{1,0:T(2,128)} %param.25) | copy-start | bytes 1156
  425.2 24.9 %copy-start.2 = (f32[2,192,1024]{2,1,0:T(8,128)S(1)}, f32[2,192,1024]{2,1,0:T(8,128)}, u32[]{:S(2)}) copy-start(f32[2,192,1024]{2,1,0:T(8,128)} %refs_0_.3) | copy-start | bytes 4718596
  436.4 17.4 %copy-start.3 = (f32[1024,192]{0,1:T(8,128)S(1)}, f32[1024,192]{0,1:T(8,128)}, u32[]{:S(2)}) copy-start(f32[1024,192]{0,1:T(8,128)} %param.24) | copy-start | bytes 2359300
  436.5 17.4 %copy-start.17 = (f32[192,1024]{1,0:T(8,128)S(1)}, f32[192,1024]{1,0:T(8,128)}, u32[]{:S(2)}) copy-start(f32[192,1024]{1,0:T(8,128)} %get-tuple-element.102) | copy-start | bytes 2359300
  450.0 5.4 %copy-start.12 = (f32[384,192]{0,1:T(8,128)S(1)}, f32[384,192]{0,1:T(8,128)}, u32[]{:S(2)}) copy-start(f32[384,192]{0,1:T(8,128)} %param.22) | copy-start | bytes 884740
  450.0 5.4 %copy-start.19 = (f32[192,384]{1,0:T(8,128)S(1)}, f32[192,384]{1,0:T(8,128)}, u32[]{:S(2)}) copy-start(f32[192,384]{1,0:T(8,128)} %get-tuple-element.100) | copy-start | bytes 884740
  450.0 6.7 %copy-start.11 = (f32[192,768]{1,0:T(8,128)S(1)}, f32[192,768]{1,0:T(8,128)}, u32[]{:S(2)}) copy-start(f32[192,768]{1,0:T(8,128)} %refs_6_.1) | copy-start | bytes 1769476
  450.0 6.7 %copy-start.18 = (f32[192,768]{1,0:T(8,128)S(1)}, f32[192,768]{1,0:T(8,128)}, u32[]{:S(2)}) copy-start(f32[192,768]{1,0:T(8,128)} %get-tuple-element.99) | copy-start | bytes 1769476
